TPU v7x, 32 devices: a whole 2x2x4 slice. The times are simulated.
32 devices in a mesh: batch: 4 (over y, x), seq: 8 (over z, core).
Axes of the slice: x: 2, y: 2, z: 4, core: 2. Of those that a mesh axis runs over, the one named last changes fastest.
Arguments:
- states: bfloat16 [16384, 768], P(('batch', 'seq')), may hold values from -6 to 6
- lengths: int32 [16], replicated, may hold values from 64 to 1024, as said below
- first_gain: bfloat16 [768], replicated, may hold values from 0.5 to 1.5
- query_weight: bfloat16 [768, 768], replicated, may hold values from -0.21875 to 0.21875
- key_weight: bfloat16 [768, 768], replicated, may hold values from -0.21875 to 0.21875
- value_weight: bfloat16 [768, 768], replicated, may hold values from -0.21875 to 0.21875
- output_weight: bfloat16 [768, 768], replicated, may hold values from -0.875 to 0.875
- second_gain: bfloat16 [768], replicated, may hold values from 0.5 to 1.5
- gate_weight: bfloat16 [768, 2048], replicated, may hold values from -0.21875 to 0.21875
- up_weight: bfloat16 [768, 2048], replicated, may hold values from -0.21875 to 0.21875
- down_weight: bfloat16 [2048, 768], replicated, may hold values from -0.125 to 0.125
- cotangent: bfloat16 [16384, 768], P(('batch', 'seq')), may hold values from -6 to 6
Outputs:
- layer_out: bfloat16 [16384, 768], P(('batch', 'seq'))
- input_grad: bfloat16 [16384, 768], P(('batch', 'seq'))
- grad_first: float32 [768], replicated
- grad_query: float32 [768, 768], P('seq', 'batch')
- grad_key: float32 [768, 768], P('seq', 'batch')
- grad_value: float32 [768, 768], P('seq', 'batch')
- grad_output: float32 [768, 768], P('seq', 'batch')
- grad_second: float32 [768], replicated
- grad_gate: float32 [768, 2048], P('seq', 'batch')
- grad_up: float32 [768, 2048], P('seq', 'batch')
- grad_down: float32 [2048, 768], P('seq', 'batch')
Inputs may be any that keep to these rules, and one draw needn't show every extreme that they name: `lengths`: in each aligned block of 2 sequences exactly one sequence, drawn from the seed, has length 1024; some sequence has length 64.
All inputs are finite; a program needn't handle non-finite values.
Results may differ from a plain program's by a relative error of at most 0.017.
Values may be sent and summed in bfloat16 or wider, within the bound.
No kernel may reach another device: no remote copies, remote signals or barrier semaphores. Data moves between devices by JAX's collectives and lax.ppermute only.
A program may use at most 128 MiB of HBM per device.

v0:
```python
import math

import jax
import jax.numpy as jnp
from jax import lax
from jax.sharding import PartitionSpec as P

HEADS = 12
HEAD_FEATURES = 64
MAXLEN = 1024
GROUP = 4


epsilon = 1e-06
masked_score = -1e30


def partner(block, axis, distance):
    count = lax.axis_size(axis)
    route = []
    for low in range(count):
        high = low | 1 << distance
        if high != low and high < count:
            route += [(low, high), (high, low)]
    return lax.ppermute(block, axis, route)


def for_sending(x):
    return jax.tree.map(lambda a: a.astype(jnp.bfloat16) if a.dtype == jnp.float32 else a, x)


def normalize_rows(values, gain_vector):
    factor = lax.rsqrt(jnp.mean(values * values, axis=-1, keepdims=True) + epsilon)
    return (values * factor * gain_vector, factor)


def normalize_back(values, factor, gain_vector, upstream):
    scaled = upstream * gain_vector
    row_inner = jnp.mean(scaled * values, axis=-1, keepdims=True)
    grad_rows = factor * scaled - values * (factor * factor * factor) * row_inner
    grad_gain = jnp.sum((upstream * values * factor).reshape(-1, values.shape[-1]), axis=0)
    return (grad_rows, grad_gain)


def rope_tables(positions):
    middle = HEAD_FEATURES // 2
    frequency = 10000.0 ** (-jnp.arange(middle, dtype=jnp.float32) * 2.0 / HEAD_FEATURES)
    angles = positions.astype(jnp.float32)[:, None] * frequency[None, :]
    angles = jnp.concatenate([angles, angles], axis=1)
    return (jnp.cos(angles), jnp.sin(angles))


def rotate(values, cosine_table, sine_table):
    middle = values.shape[-1] // 2
    turned = jnp.concatenate([-values[..., middle:], values[..., :middle]], axis=-1)
    return values * cosine_table + turned * sine_table


def rotate_back(values, cosine_table, sine_table):
    middle = values.shape[-1] // 2
    scaled = values * sine_table
    turned = jnp.concatenate([scaled[..., middle:], -scaled[..., :middle]], axis=-1)
    return values * cosine_table + turned


def butterfly(values, axis_number, sender):
    position = lax.axis_index("seq")
    initial = values.shape
    divided = values.reshape(initial[:axis_number] + (2, 2) + initial[axis_number + 1 :])
    for bit_index in (1, 0):
        digit_axis = axis_number + 1 - bit_index
        own_bit = position >> bit_index & 1
        staying = lax.dynamic_index_in_dim(divided, own_bit, digit_axis, keepdims=True)
        leaving = lax.dynamic_index_in_dim(divided, 1 - own_bit, digit_axis, keepdims=True)
        arrived = sender(leaving, bit_index)
        lower_first = jnp.concatenate([staying, arrived], axis=digit_axis)
        upper_first = jnp.concatenate([arrived, staying], axis=digit_axis)
        divided = jnp.where(own_bit == 0, lower_first, upper_first)
    return divided.reshape(initial)


def attend_forward(packed):
    query_rows, key_rows, value_rows, length_one = packed
    positions = jnp.arange(MAXLEN, dtype=jnp.int32)
    score_scale = 1.0 / math.sqrt(HEAD_FEATURES)
    block_rows = min(512, MAXLEN)
    outputs = []
    totals = []
    for row_start in range(0, MAXLEN, block_rows):
        query_block = query_rows[row_start : row_start + block_rows]
        score_matrix = (
            jnp.einsum("qhe,khe->hqk", query_block, key_rows, preferred_element_type=jnp.float32)
            * score_scale
        )
        causal = positions[row_start : row_start + block_rows, None] >= positions[None, :]
        score_matrix = jnp.where(causal[None], score_matrix, masked_score)
        row_max = jnp.max(score_matrix, axis=-1, keepdims=True)
        weights = jnp.exp(score_matrix - row_max)
        row_total = jnp.sum(weights, axis=-1, keepdims=True)
        probability_low = (weights / row_total).astype(jnp.bfloat16)
        rows_mixed = jnp.einsum(
            "hqk,khe->qhe", probability_low, value_rows, preferred_element_type=jnp.float32
        )
        live_rows = (positions[row_start : row_start + block_rows] < length_one).astype(
            jnp.float32
        )[:, None, None]
        outputs.append((rows_mixed * live_rows).astype(jnp.bfloat16))
        totals.append((row_max + jnp.log(row_total))[..., 0])
    return (jnp.concatenate(outputs, axis=0), jnp.concatenate(totals, axis=1))


def attend_back(packed):
    query_rows, key_rows, value_rows, row_log, grad_rows, length_one = packed
    positions = jnp.arange(MAXLEN, dtype=jnp.int32)
    score_scale = 1.0 / math.sqrt(HEAD_FEATURES)
    block_rows = min(512, MAXLEN)
    live_rows = (positions < length_one).astype(jnp.bfloat16)[:, None, None]
    grad_live = grad_rows * live_rows
    key_grad = jnp.zeros(key_rows.shape, jnp.float32)
    value_grad = jnp.zeros(value_rows.shape, jnp.float32)
    query_parts = []
    for row_start in range(0, MAXLEN, block_rows):
        query_block = query_rows[row_start : row_start + block_rows]
        grad_block = grad_live[row_start : row_start + block_rows]
        score_matrix = (
            jnp.einsum("qhe,khe->hqk", query_block, key_rows, preferred_element_type=jnp.float32)
            * score_scale
        )
        causal = positions[row_start : row_start + block_rows, None] >= positions[None, :]
        score_matrix = jnp.where(causal[None], score_matrix, masked_score)
        attention_probability = jnp.exp(
            score_matrix - row_log[:, row_start : row_start + block_rows, None]
        )
        grad_probability = jnp.einsum(
            "qhe,khe->hqk", grad_block, value_rows, preferred_element_type=jnp.float32
        )
        row_inner = jnp.sum(attention_probability * grad_probability, axis=-1, keepdims=True)
        grad_scores = (attention_probability * (grad_probability - row_inner)).astype(jnp.bfloat16)
        query_parts.append(
            jnp.einsum("hqk,khe->qhe", grad_scores, key_rows, preferred_element_type=jnp.float32)
            * score_scale
        )
        key_grad = (
            key_grad
            + jnp.einsum(
                "hqk,qhe->khe", grad_scores, query_block, preferred_element_type=jnp.float32
            )
            * score_scale
        )
        value_grad = value_grad + jnp.einsum(
            "hqk,qhe->khe",
            attention_probability.astype(jnp.bfloat16),
            grad_block,
            preferred_element_type=jnp.float32,
        )
    cosine_head, sine_head = rope_tables(positions)
    cosine_head = cosine_head[:, None, :]
    sine_head = sine_head[:, None, :]
    query_grad = rotate_back(jnp.concatenate(query_parts, axis=0), cosine_head, sine_head)
    key_grad = rotate_back(key_grad, cosine_head, sine_head)
    return jnp.stack([query_grad, key_grad, value_grad]).astype(jnp.bfloat16)


def body(
    states,
    lengths,
    first_gain,
    query_weight,
    key_weight,
    value_weight,
    output_weight,
    second_gain,
    gate_weight,
    up_weight,
    down_weight,
    cotangent,
):
    token_count, width = states.shape
    local_heads = HEADS // GROUP
    head_lanes = local_heads * HEAD_FEATURES
    piece_rows = MAXLEN // GROUP
    sequence_count = token_count // piece_rows
    place_index = lax.axis_index("seq")
    member = place_index % GROUP
    first_sequence = (
        lax.axis_index("batch") * (lax.axis_size("seq") // GROUP) + place_index // GROUP
    ) * sequence_count
    own_lengths = lax.dynamic_slice_in_dim(lengths, first_sequence, sequence_count)
    token_positions = member * piece_rows + jnp.arange(piece_rows, dtype=jnp.int32)
    live_tokens = (token_positions[None, :] < own_lengths[:, None]).astype(jnp.float32)[:, :, None]
    inputs_full = states.astype(jnp.float32).reshape(sequence_count, piece_rows, width)
    gain_first = first_gain.astype(jnp.float32)
    gain_second = second_gain.astype(jnp.float32)
    normed, factor_first = normalize_rows(inputs_full, gain_first)
    normed_low = normed.astype(jnp.bfloat16)
    stacked = jnp.stack([query_weight, key_weight, value_weight]).reshape(
        3, width, GROUP, head_lanes
    )
    projected = jnp.einsum(
        "std,kdge->ksgte", normed_low, stacked, preferred_element_type=jnp.float32
    )
    projected = projected.reshape(3, sequence_count, GROUP, piece_rows, local_heads, HEAD_FEATURES)
    cosine_token, sine_token = rope_tables(token_positions)
    turned = rotate(projected[:2], cosine_token[:, None, :], sine_token[:, None, :])
    outgoing = jnp.concatenate([turned, projected[2:]], axis=0).astype(jnp.bfloat16)
    outgoing = outgoing.reshape(3, sequence_count, GROUP, piece_rows, head_lanes)
    regrouped = butterfly(
        outgoing, 2, lambda leaving, bit_index: partner(leaving, "seq", bit_index)
    )
    regrouped = regrouped.reshape(3, sequence_count, MAXLEN, local_heads, HEAD_FEATURES)
    attended, row_log = lax.map(
        attend_forward, (regrouped[0], regrouped[1], regrouped[2], own_lengths)
    )
    attended = attended.reshape(sequence_count, GROUP, piece_rows, head_lanes)
    mixed_tokens = butterfly(
        attended,
        1,
        lambda leaving, bit_index: partner(for_sending(leaving), "seq", bit_index).astype(
            leaving.dtype
        ),
    )
    output_blocks = output_weight.reshape(GROUP, head_lanes, width)
    branch = jnp.einsum(
        "sgte,gef->stf", mixed_tokens, output_blocks, preferred_element_type=jnp.float32
    )
    hidden = inputs_full + branch
    second_normed, second_factor = normalize_rows(hidden, gain_second)
    second_low = second_normed.astype(jnp.bfloat16)
    gate_values = jnp.einsum(
        "std,df->stf", second_low, gate_weight, preferred_element_type=jnp.float32
    )
    up_values = jnp.einsum("std,df->stf", second_low, up_weight, preferred_element_type=jnp.float32)
    sigmoid_gate = jax.nn.sigmoid(gate_values)
    silu_gate = jax.nn.silu(gate_values)
    activated = (silu_gate * up_values).astype(jnp.bfloat16)
    down_values = jnp.einsum(
        "stf,fd->std", activated, down_weight, preferred_element_type=jnp.float32
    )
    layer_out = (
        ((hidden + down_values) * live_tokens).astype(jnp.bfloat16).reshape(token_count, width)
    )
    upstream = (
        cotangent.astype(jnp.float32).reshape(sequence_count, piece_rows, width) * live_tokens
    )
    upstream_low = upstream.astype(jnp.bfloat16)
    down_grad = jnp.einsum(
        "stf,std->fd", activated, upstream_low, preferred_element_type=jnp.float32
    )
    active_grad = jnp.einsum(
        "std,fd->stf", upstream_low, down_weight, preferred_element_type=jnp.float32
    )
    gate_delta = (
        active_grad * up_values * (sigmoid_gate * (1.0 + gate_values * (1.0 - sigmoid_gate)))
    ).astype(jnp.bfloat16)
    up_delta = (active_grad * silu_gate).astype(jnp.bfloat16)
    gate_grad = jnp.einsum(
        "std,stf->df", second_low, gate_delta, preferred_element_type=jnp.float32
    )
    up_grad = jnp.einsum("std,stf->df", second_low, up_delta, preferred_element_type=jnp.float32)
    second_delta = jnp.einsum(
        "stf,df->std", gate_delta, gate_weight, preferred_element_type=jnp.float32
    )
    second_delta = second_delta + jnp.einsum(
        "stf,df->std", up_delta, up_weight, preferred_element_type=jnp.float32
    )
    hidden_delta, second_grad = normalize_back(hidden, second_factor, gain_second, second_delta)
    hidden_grad = upstream + hidden_delta
    hidden_low = hidden_grad.astype(jnp.bfloat16)
    output_grad = jnp.einsum(
        "sgte,stf->gef", mixed_tokens, hidden_low, preferred_element_type=jnp.float32
    ).reshape(width, width)
    mixed_delta = jnp.einsum(
        "stf,gef->sgte", hidden_low, output_blocks, preferred_element_type=jnp.float32
    ).astype(jnp.bfloat16)
    mixed_heads = butterfly(
        mixed_delta, 1, lambda leaving, bit_index: partner(leaving, "seq", bit_index)
    )
    mixed_heads = mixed_heads.reshape(sequence_count, MAXLEN, local_heads, HEAD_FEATURES)
    heads_delta = lax.map(
        attend_back, (regrouped[0], regrouped[1], regrouped[2], row_log, mixed_heads, own_lengths)
    )
    heads_delta = heads_delta.reshape(sequence_count, 3, GROUP, piece_rows, head_lanes)
    token_delta = butterfly(
        heads_delta,
        2,
        lambda leaving, bit_index: partner(for_sending(leaving), "seq", bit_index).astype(
            leaving.dtype
        ),
    )
    weight_grads = jnp.einsum(
        "std,skgte->kdge", normed_low, token_delta, preferred_element_type=jnp.float32
    )
    weight_grads = weight_grads.reshape(3, width, width)
    normed_delta = jnp.einsum(
        "skgte,kdge->std", token_delta, stacked, preferred_element_type=jnp.float32
    )
    input_delta, first_grad = normalize_back(inputs_full, factor_first, gain_first, normed_delta)
    input_grad = (hidden_grad + input_delta).astype(jnp.bfloat16).reshape(token_count, width)
    gain_total = lax.psum((first_grad, second_grad), ("batch", "seq"))
    weight_terms = (
        weight_grads[0],
        weight_grads[1],
        weight_grads[2],
        output_grad,
        gate_grad,
        up_grad,
        down_grad,
    )
    shared = (
        lax.psum_scatter(weight_terms[0], "seq", scatter_dimension=0, tiled=True),
        lax.psum_scatter(weight_terms[1], "seq", scatter_dimension=0, tiled=True),
        lax.psum_scatter(weight_terms[2], "seq", scatter_dimension=0, tiled=True),
        lax.psum_scatter(weight_terms[3], "seq", scatter_dimension=0, tiled=True),
        lax.psum_scatter(weight_terms[4], "seq", scatter_dimension=0, tiled=True),
        lax.psum_scatter(weight_terms[5], "seq", scatter_dimension=0, tiled=True),
        lax.psum_scatter(weight_terms[6], "seq", scatter_dimension=0, tiled=True),
    )
    shared = (
        lax.psum_scatter(
            shared[0].astype(jnp.bfloat16), "batch", scatter_dimension=1, tiled=True
        ).astype(jnp.float32),
        lax.psum_scatter(
            shared[1].astype(jnp.bfloat16), "batch", scatter_dimension=1, tiled=True
        ).astype(jnp.float32),
        lax.psum_scatter(
            shared[2].astype(jnp.bfloat16), "batch", scatter_dimension=1, tiled=True
        ).astype(jnp.float32),
        lax.psum_scatter(
            shared[3].astype(jnp.bfloat16), "batch", scatter_dimension=1, tiled=True
        ).astype(jnp.float32),
        lax.psum_scatter(
            shared[4].astype(jnp.bfloat16), "batch", scatter_dimension=1, tiled=True
        ).astype(jnp.float32),
        lax.psum_scatter(
            shared[5].astype(jnp.bfloat16), "batch", scatter_dimension=1, tiled=True
        ).astype(jnp.float32),
        lax.psum_scatter(
            shared[6].astype(jnp.bfloat16), "batch", scatter_dimension=1, tiled=True
        ).astype(jnp.float32),
    )
    return (
        layer_out,
        input_grad,
        gain_total[0],
        shared[0],
        shared[1],
        shared[2],
        shared[3],
        gain_total[1],
        shared[4],
        shared[5],
        shared[6],
    )


def solution(mesh):
    in_specs = (
        P(("batch", "seq"), None),
        P(),
        P(),
        P(),
        P(),
        P(),
        P(),
        P(),
        P(),
        P(),
        P(),
        P(("batch", "seq"), None),
    )
    out_specs = (
        P(("batch", "seq"), None),
        P(("batch", "seq"), None),
        P(),
        P("seq", "batch"),
        P("seq", "batch"),
        P("seq", "batch"),
        P("seq", "batch"),
        P(),
        P("seq", "batch"),
        P("seq", "batch"),
        P("seq", "batch"),
    )
    return jax.shard_map(body, mesh=mesh, in_specs=in_specs, out_specs=out_specs, check_vma=False)
```

profile of v0, /device:TPU:0, one launch (start us, length us, event | category | flops | bytes accessed | tf_op | source)
XLA Modules:
  0.0 890.6 jit_solution(7985792812361037484)
XLA Ops:
  17.2 4.3 fusion.111
  24.6 4.0 slice_negate_fusion.2
  28.6 3.9 pad_maximum_fusion.2
  32.6 3.5 add_convert_fusion
  37.8 3.0 collective-permute-start
  40.8 26.3 %collective-permute-done = bf16[3,2,1,2,256,192]{4,5,1,3,2,0:T(8,128)(2,1)} collective-permute-done((bf16[3,2,1,2,256,192]{4,5,1,3,2,0:T(8,128)(2,1)}, bf16[3,2,1,2,256,192]{4,5,1,3,2,0:T(8,128)(2,1)}, u32[]{:S(2)}, u32[]{:S(2)}) %collective-permute-start) | collective-permute-done | bytes 1179680 | tf_op jit(solution)/shard_map/ppermute | solution.py:25
  67.1 2.9 maximum_select_fusion
  71.7 3.1 collective-permute-done.1
  74.8 2.9 maximum_select_fusion.1
  80.7 3.1 squeeze.67
  83.9 2.8 copy.65
  86.7 3.1 squeeze.68
  89.8 2.8 copy.66
  92.7 3.3 squeeze.69
  95.9 40.7 %while.24 = (s32[]{:T(128)}, bf16[2,1024,3,64]{1,3,2,0:T(8,128)(2,1)}, f32[2,3,1024]{2,1,0:T(4,128)}, bf16[2,1024,3,64]{1,3,2,0:T(8,128)(2,1)}, bf16[2,1024,3,64...) while((s32[]{:T(128)}, ...), condition=%wide.region_6.7_spmd, body=%wide.region_1.6_spmd.sunk | while | flops 845285376 | bytes 101875984 | solution.py:211
  96.3 2.7 fusion.203
  102.8 2.7 fusion.200
  109.2 3.1 fusion.205
  112.3 3.1 fusion.202
  123.2 2.7 fusion.200
  129.5 3.1 fusion.205
  132.7 3.1 fusion.202
  136.6 3.6 reshape_reshape.4
  143.9 9.3 %collective-permute-done.2 = bf16[2,1,2,256,192]{3,4,2,1,0:T(8,128)(2,1)S(1)} collective-permute-done((bf16[2,1,2,256,192]{3,4,2,1,0:T(8,128)(2,1)S(1)}, bf16[2,1,2,256,192]{3,4,2,1,0:T(8,128)(2,1)S(1)}, u32[]{:S(2)}, u32[]{:S(2)}) %collective-permute-start.2) | collective-permute-done | bytes 393248 | tf_op jit(solution)/shard_map/ppermute | solution.py:25
  160.1 4.7 multiply_convert_fusion.3
  172.7 9.8 %collective-permute-done.4 = bf16[2,1,2,256,192]{3,4,2,1,0:T(8,128)(2,1)S(1)} collective-permute-done((bf16[2,1,2,256,192]{3,4,2,1,0:T(8,128)(2,1)S(1)}, bf16[2,1,2,256,192]{3,4,2,1,0:T(8,128)(2,1)S(1)}, u32[]{:S(2)}, u32[]{:S(2)}) %collective-permute-start.4) | collective-permute-done | bytes 393248 | tf_op jit(solution)/shard_map/ppermute | solution.py:25
  186.8 82.1 %while.25 = (s32[]{:T(128)}, bf16[2,3,1024,3,64]{2,4,3,1,0:T(8,128)(2,1)}, bf16[2,1024,3,64]{1,3,2,0:T(8,128)(2,1)S(1)}, bf16[2,1024,3,64]{1,3,2,0:T(8,128)(2,1)...) while((s32[]{:T(128)}, ...), condition=%wide.region_12.13_spmd, body=%wide.region_9.12_spmd.sunk | while | flops 2068807680 | bytes 141681680 | solution.py:279
  191.6 5.3 multiply_reduce_fusion.9
  199.2 5.3 multiply_reduce_fusion.10
  204.5 7.6 multiply_convert_fusion.10
  212.1 3.1 convolution_multiply_fusion.4
  232.3 5.3 multiply_reduce_fusion.9
  240.0 5.3 multiply_reduce_fusion.10
  245.3 7.6 multiply_convert_fusion.10
  252.9 3.1 convolution_multiply_fusion.4
  268.8 6.6 reshape_reshape.10
  275.4 5.2 constant_dynamic-slice_fusion.3
  284.6 41.2 %collective-permute-done.6 = bf16[2,3,1,2,256,192]{4,3,2,5,1,0:T(2,128)(2,1)} collective-permute-done((bf16[2,3,1,2,256,192]{4,3,2,5,1,0:T(2,128)(2,1)}, bf16[2,3,1,2,256,192]{4,3,2,5,1,0:T(2,128)(2,1)}, u32[]{:S(2)}, u32[]{:S(2)}) %collective-permute-start.6) | collective-permute-done | bytes 1179680 | tf_op jit(solution)/shard_map/ppermute | solution.py:25
  325.8 7.2 broadcast_select_fusion
  333.0 4.9 constant_dynamic-slice_fusion.1
  342.8 11.1 %broadcast_select_fusion.1 = bf16[2,3,2,2,256,192]{4,3,2,5,1,0:T(2,128)(2,1)} fusion(pred[]{:T(512)S(6)} %eq.6, bf16[2,3,2,1,256,192]{4,3,2,5,1,0:T(2,128)(2,1)S(1)} %copy.71, bf16[2,3,2,1,256,192]{4,3,2,5,1,0:T(2,128)(2,1)S(1)} %get-tuple-element.256), kind=kLoop, calls=%fused_computation.131 | loop fusion | flops 10616832 | bytes 4718593 | tf_op jit(solution)/shard_map/jit(_where)/select_n | solution.py:78
  353.9 5.5 select_n.155
  361.5 3.0 fusion.141
  364.5 3.1 copy.75
  367.6 3.1 copy.76
  370.8 3.1 copy.77
  375.0 6.3 convolution_bitcast_fusion
  382.5 6.1 convolution_bitcast_fusion.2
  388.6 6.1 convolution_bitcast_fusion.1
  396.7 9.4 %reduce-scatter.25.cloned.1.call-done = f32[96,768]{1,0:T(8,128)} async-done(((f32[768,768]{1,0:T(8,128)}), f32[96,768]{1,0:T(8,128)}) %reduce-scatter.25.cloned.1.call-update) | async-done | bytes 294928 | tf_op jit(solution)/shard_map/reduce_scatter | solution.py:310
  408.0 36.1 %reduce-scatter.27.cloned.1.call-done = f32[96,768]{1,0:T(8,128)} async-done(((f32[768,768]{1,0:T(8,128)}), f32[96,768]{1,0:T(8,128)}) %reduce-scatter.27.cloned.1.call-update) | async-done | bytes 294928 | tf_op jit(solution)/shard_map/reduce_scatter | solution.py:311
  446.0 35.7 %reduce-scatter.29.cloned.1.call-done = f32[96,768]{1,0:T(8,128)} async-done(((f32[768,768]{1,0:T(8,128)}), f32[96,768]{1,0:T(8,128)}) %reduce-scatter.29.cloned.1.call-update) | async-done | bytes 294928 | tf_op jit(solution)/shard_map/reduce_scatter | solution.py:312
  483.6 69.3 %reduce-scatter.41.cloned.1.call-done = f32[256,768]{1,0:T(8,128)} async-done(((f32[2048,768]{1,0:T(8,128)}), f32[256,768]{1,0:T(8,128)}) %reduce-scatter.41.cloned.1.call-update) | async-done | bytes 786448 | tf_op jit(solution)/shard_map/reduce_scatter | solution.py:316
  555.0 68.2 %reduce-scatter.33.cloned.1.call-done = f32[96,2048]{1,0:T(8,128)} async-done(((f32[768,2048]{1,0:T(8,128)}), f32[96,2048]{1,0:T(8,128)}) %reduce-scatter.33.cloned.1.call-update) | async-done | bytes 786448 | tf_op jit(solution)/shard_map/reduce_scatter | solution.py:314
  625.5 5.7 multiply_convert_fusion.6
  631.2 62.5 %reduce-scatter.37.cloned.1.call-done = f32[96,2048]{1,0:T(8,128)} async-done(((f32[768,2048]{1,0:T(8,128)}), f32[96,2048]{1,0:T(8,128)}) %reduce-scatter.37.cloned.1.call-update) | async-done | bytes 786448 | tf_op jit(solution)/shard_map/reduce_scatter | solution.py:315
  695.7 5.4 fusion.117
  701.1 37.8 %all-reduce = (f32[768]{0:T(1024)}, f32[768]{0:T(1024)}) all-reduce(f32[768]{0:T(1024)S(1)} %get-tuple-element.188, f32[768]{0:T(1024)S(1)} %copy-done.35), channel_id=1, replica_groups=mesh['batch'=4,'seq'=8] {'batch','seq'}, use_global_device_ids=true, to_apply=%region_15.16 | all-reduce | flops 1536 | bytes 12288 | tf_op jit(solution)/shard_map/psum | solution.py:299
  739.0 3.6 add_convert_fusion.1
  747.8 25.6 %reduce-scatter.45.cloned.1.call-done = bf16[192,96]{1,0:T(8,128)(2,1)} async-done(((bf16[768,96]{1,0:T(8,128)(2,1)}), bf16[192,96]{1,0:T(8,128)(2,1)}) %reduce-scatter.45.cloned.1.call-update) | async-done | bytes 36880
  775.0 25.8 %reduce-scatter.47.cloned.1.call-done = bf16[192,96]{1,0:T(8,128)(2,1)} async-done(((bf16[768,96]{1,0:T(8,128)(2,1)}), bf16[192,96]{1,0:T(8,128)(2,1)}) %reduce-scatter.47.cloned.1.call-update) | async-done | bytes 36880
  802.4 25.5 %reduce-scatter.51.cloned.1.call-done = bf16[192,256]{1,0:T(8,128)(2,1)} async-done(((bf16[768,256]{1,0:T(8,128)(2,1)}), bf16[192,256]{1,0:T(8,128)(2,1)}) %reduce-scatter.51.cloned.1.call-update) | async-done | bytes 98320
  829.7 25.5 %reduce-scatter.35.cloned.1.call-done = bf16[96,512]{1,0:T(8,128)(2,1)} async-done(((bf16[96,2048]{1,0:T(8,128)(2,1)}), bf16[96,512]{1,0:T(8,128)(2,1)}) %reduce-scatter.35.cloned.1.call-update) | async-done | bytes 98320 | tf_op jit(solution)/shard_map/reduce_scatter | solution.py:331
  856.7 25.5 %reduce-scatter.39.cloned.1.call-done = bf16[96,512]{1,0:T(8,128)(2,1)} async-done(((bf16[96,2048]{1,0:T(8,128)(2,1)}), bf16[96,512]{1,0:T(8,128)(2,1)}) %reduce-scatter.39.cloned.1.call-update) | async-done | bytes 98320 | tf_op jit(solution)/shard_map/reduce_scatter | solution.py:334
  (302 shorter events, 141.0 us)
Async XLA Ops:
  7.2 152.9 %copy-start = (bf16[768,2048]{1,0:T(8,128)(2,1)S(1)}, bf16[768,2048]{1,0:T(8,128)(2,1)}, u32[]{:S(2)}) copy-start(bf16[768,2048]{1,0:T(8,128)(2,1)} %param.24) | copy-start | bytes 9437188
  7.2 387.6 %reduce-scatter.31.cloned.1.call-start = ((), (), s32[]{:S(2)}) async-start(), calls=%async_computation.17 | async-start | bytes 2654208 | tf_op jit(solution)/shard_map/reduce_scatter | solution.py:313
  9.4 7.8 copy-start.29
  10.1 7.2 copy-start.27
  32.6 3.5 copy-start.21
  37.8 29.3 %collective-permute-start = (bf16[3,2,1,2,256,192]{4,5,1,3,2,0:T(8,128)(2,1)}, bf16[3,2,1,2,256,192]{4,5,1,3,2,0:T(8,128)(2,1)}, u32[]{:S(2)}, u32[]{:S(2)}) collective-permute-start(bf16[3,2,1,2,256,192]{4,5,1,3,2,0:T(8,128)(2,1)} %get-tuple-element.266), channel_id=1, source_target_pairs={{0,2},{2,0},{1,3},{3,1},{4,6},{6,4},{5,7},{7,5},{8,10},{10,8},{9,1... | collective-permute-start | bytes 3538952 | tf_op jit(solution)/shard_map/ppermute | solution.py:25
  69.9 1.7 copy-start.40
  71.6 3.2 collective-permute-start.1
  96.3 2.7 copy-start.7
  99.0 2.7 copy-start.3
  102.8 2.7 copy-start.9
  105.5 3.7 copy-start.4
  105.5 3.7 copy-start.8
  116.7 2.7 copy-start.7
  119.3 2.7 copy-start.3
  123.2 2.7 copy-start.9
  125.9 3.7 copy-start.4
  125.9 3.7 copy-start.8
  136.6 7.2 copy-start.36
  141.9 11.5 %copy-start.24 = (bf16[512,768]{1,0:T(8,128)(2,1)S(1)}, bf16[512,768]{1,0:T(8,128)(2,1)}, u32[]{:S(2)}) copy-start(bf16[512,768]{1,0:T(8,128)(2,1)} %param.27) | copy-start | bytes 2359300
  141.9 11.5 %copy-start.38 = (bf16[2048,768]{1,0:T(8,128)(2,1)S(1)}, bf16[2048,768]{1,0:T(8,128)(2,1)}, u32[]{:S(2)}) copy-start(bf16[2048,768]{1,0:T(8,128)(2,1)} %param.26) | copy-start | bytes 9437188
  142.0 11.2 %collective-permute-start.2 = (bf16[2,1,2,256,192]{3,4,2,1,0:T(8,128)(2,1)S(1)}, bf16[2,1,2,256,192]{3,4,2,1,0:T(8,128)(2,1)S(1)}, u32[]{:S(2)}, u32[]{:S(2)}) collective-permute-start(bf16[2,1,2,256,192]{3,4,2,1,0:T(8,128)(2,1)S(1)} %copy.107), channel_id=1, source_target_pairs={{0,2},{2,0},{1,3},{3,1},{4,6},{6,4},{5,7},{7,5},{8,10},{10,8},{9,1... | collective-permute-start | bytes 1179656 | tf_op jit(solution)/shard_map/ppermute | solution.py:25
  143.9 25.4 %copy-start.33 = (f32[2,256]{1,0:T(2,128)}, f32[2,256]{1,0:T(2,128)S(1)}, u32[]{:S(2)}) copy-start(f32[2,256]{1,0:T(2,128)S(1)} %compare_convert_fusion.2) | copy-start | bytes 6148
  153.4 2.0 collective-permute-start.3
  153.5 2.0 copy-start.15
  153.5 2.0 copy-start.39
  155.5 2.7 copy-start.37
  156.5 12.9 %copy-start.18 = (f32[2,256,768]{2,1,0:T(8,128)}, f32[2,256,768]{2,1,0:T(8,128)S(1)}, u32[]{:S(2)}) copy-start(f32[2,256,768]{2,1,0:T(8,128)S(1)} %get-tuple-element.280) | copy-start | bytes 4718596
  158.2 1.8 copy-start.13
  164.7 1.9 copy-start.22
  164.7 2.0 copy-start.23
  169.8 1.1 copy-start.11
  171.0 11.5 %collective-permute-start.4 = (bf16[2,1,2,256,192]{3,4,2,1,0:T(8,128)(2,1)S(1)}, bf16[2,1,2,256,192]{3,4,2,1,0:T(8,128)(2,1)S(1)}, u32[]{:S(2)}, u32[]{:S(2)}) collective-permute-start(bf16[2,1,2,256,192]{3,4,2,1,0:T(8,128)(2,1)S(1)} %get-tuple-element.270), channel_id=1, source_target_pairs={{0,2},{2,0},{1,3},{3,1},{4,6},{6,4},{5,7},{7,5},{8,10},{10,8},{9,1... | collective-permute-start | bytes 1179656 | tf_op jit(solution)/shard_map/ppermute | solution.py:25
  182.6 1.8 collective-permute-start.5
  184.4 2.3 copy-start.5
  189.2 2.0 copy-start.26
  219.6 1.9 copy-start.2
  226.3 1.4 copy-start.6
  229.9 2.0 copy-start.26
  260.4 1.9 copy-start.2
  267.0 1.4 copy-start.6
  275.4 6.9 copy-start.12
  275.4 6.9 copy-start.20
  280.6 45.2 %collective-permute-start.6 = (bf16[2,3,1,2,256,192]{4,3,2,5,1,0:T(2,128)(2,1)}, bf16[2,3,1,2,256,192]{4,3,2,5,1,0:T(2,128)(2,1)}, u32[]{:S(2)}, u32[]{:S(2)}) collective-permute-start(bf16[2,3,1,2,256,192]{4,3,2,5,1,0:T(2,128)(2,1)} %get-tuple-element.259), channel_id=1, source_target_pairs={{0,2},{2,0},{1,3},{3,1},{4,6},{6,4},{5,7},{7,5},{8,10},{10,8},{9,1... | collective-permute-start | bytes 3538952 | tf_op jit(solution)/shard_map/ppermute | solution.py:25
  284.6 121.5 %reduce-scatter.25.cloned.1.call-start = ((), (), s32[]{:S(2)}) async-start(), calls=%async_computation.14 | async-start | bytes 2654208 | tf_op jit(solution)/shard_map/reduce_scatter | solution.py:310
  337.8 1.1 copy-start.16
  338.1 2.9 collective-permute-start.7
  367.6 76.5 %reduce-scatter.27.cloned.1.call-start = ((), (), s32[]{:S(2)}) async-start(), calls=%async_computation.15 | async-start | bytes 2654208 | tf_op jit(solution)/shard_map/reduce_scatter | solution.py:311
  370.8 110.9 %reduce-scatter.29.cloned.1.call-start = ((), (), s32[]{:S(2)}) async-start(), calls=%async_computation.16 | async-start | bytes 2654208 | tf_op jit(solution)/shard_map/reduce_scatter | solution.py:312
  373.9 178.9 %reduce-scatter.41.cloned.1.call-start = ((), (), s32[]{:S(2)}) async-start(), calls=%async_computation.22 | async-start | bytes 7077888 | tf_op jit(solution)/shard_map/reduce_scatter | solution.py:316
  381.3 1.1 copy-start.14
  381.3 241.9 %reduce-scatter.33.cloned.1.call-start = ((), (), s32[]{:S(2)}) async-start(), calls=%async_computation.18 | async-start | bytes 7077888 | tf_op jit(solution)/shard_map/reduce_scatter | solution.py:314
  388.6 305.2 %reduce-scatter.37.cloned.1.call-start = ((), (), s32[]{:S(2)}) async-start(), calls=%async_computation.20 | async-start | bytes 7077888 | tf_op jit(solution)/shard_map/reduce_scatter | solution.py:315
  394.7 347.8 %reduce-scatter.49.cloned.1.call-start = ((), (), s32[]{:S(2)}) async-start(), calls=%async_computation.26 | async-start | bytes 245760
  396.6 349.7 %reduce-scatter.43.cloned.1.call-start = ((), (), s32[]{:S(2)}) async-start(), calls=%async_computation.23 | async-start | bytes 245760
  408.0 365.5 %reduce-scatter.45.cloned.1.call-start = ((), (), s32[]{:S(2)}) async-start(), calls=%async_computation.24 | async-start | bytes 245760
  445.9 179.6 %copy-start.30 = (f32[2,256]{1,0:T(2,128)S(1)}, f32[2,256]{1,0:T(2,128)}, u32[]{:S(2)}) copy-start(f32[2,256]{1,0:T(2,128)} %copy-done.29) | copy-start | bytes 6148
  445.9 354.9 %reduce-scatter.47.cloned.1.call-start = ((), (), s32[]{:S(2)}) async-start(), calls=%async_computation.25 | async-start | bytes 245760
  483.5 344.4 %reduce-scatter.51.cloned.1.call-start = ((), (), s32[]{:S(2)}) async-start(), calls=%async_computation.27 | async-start | bytes 491520
  555.0 300.2 %reduce-scatter.35.cloned.1.call-start = ((), (), s32[]{:S(2)}) async-start(), calls=%async_computation.19 | async-start | bytes 491520 | tf_op jit(solution)/shard_map/reduce_scatter | solution.py:331
  625.2 257.1 %reduce-scatter.39.cloned.1.call-start = ((), (), s32[]{:S(2)}) async-start(), calls=%async_computation.21 | async-start | bytes 491520 | tf_op jit(solution)/shard_map/reduce_scatter | solution.py:334
  625.5 70.2 %copy-start.17 = (bf16[512,768]{1,0:T(8,128)(2,1)S(1)}, bf16[512,768]{1,0:T(8,128)(2,1)}, u32[]{:S(2)}) copy-start(bf16[512,768]{1,0:T(8,128)(2,1)} %param.16) | copy-start | bytes 2359300
  695.7 5.4 copy-start.35
  739.0 144.9 %copy-start.1 = (bf16[768,2048]{1,0:T(8,128)(2,1)S(1)}, bf16[768,2048]{1,0:T(8,128)(2,1)}, u32[]{:S(2)}) copy-start(bf16[768,2048]{1,0:T(8,128)(2,1)} %param.24) | copy-start | bytes 9437188
  (8 other events, 8.4 us)
Sparse Core Ops, SparseCore 0:
  284.7 50.0 reduce-scatter.30
  367.7 38.4 reduce-scatter.24
  408.5 35.5 reduce-scatter.26
  446.2 35.3 reduce-scatter.28
  483.8 68.9 reduce-scatter.40
  555.0 68.1 reduce-scatter.32
  625.5 68.1 reduce-scatter.36
  696.5 22.3 reduce-scatter.48
  722.3 23.9 reduce-scatter.42
  749.5 23.9 reduce-scatter.44
  776.8 23.9 reduce-scatter.46
  803.5 24.4 reduce-scatter.50
  830.7 24.4 reduce-scatter.34
  857.8 24.4 reduce-scatter.38
where the time goes:
time: 902 us; the launch traced here: 891 us
  waiting for transfers between devices  505 us (56%)
  matrix products  126 us (14%)
  other arithmetic  99 us (11%)
  local copies, waits for them, and re-layouts  98.2 us (11%)
  blocking collectives  37.8 us (4%)
  between operations  14.8 us (2%)
  starting transfers between devices  9.32 us (1%)
    ppermute x8, waiting for transfers between devices, partner(): return lax.ppermute(block, axis, route)  93.1 us
    unnamed x19, waiting for transfers between devices  79.5 us
    reduce_scatter x1, waiting for transfers between devices, body(): lax.psum_scatter(weight_terms[6], 'seq', scatter_dimension=0, tiled=True)  69.3 us
    reduce_scatter x1, waiting for transfers between devices, body(): lax.psum_scatter(weight_terms[4], 'seq', scatter_dimension=0, tiled=True)  68.2 us
    reduce_scatter x1, waiting for transfers between devices, body(): lax.psum_scatter(weight_terms[5], 'seq', scatter_dimension=0, tiled=True)  62.5 us
    psum x1, blocking collectives, body(): gain_total = lax.psum((first_grad, second_grad), ('batch', 'seq'))  37.8 us
    reduce_scatter x1, waiting for transfers between devices, body(): lax.psum_scatter(weight_terms[1], 'seq', scatter_dimension=0, tiled=True)  36.1 us
    reduce_scatter x1, waiting for transfers between devices, body(): lax.psum_scatter(weight_terms[2], 'seq', scatter_dimension=0, tiled=True)  35.7 us
  transfers between devices with their start and end apart: 22, of which 19 were waited for; matrix products, arithmetic and copies ran while one was open for 12% of the time, Pallas kernels for 0%

commit v1 on v0

v1 whole, which is shorter than its diff:
```python
import functools
import math

import jax
import jax.numpy as jnp
import numpy as np
from jax import lax
from jax.experimental import pallas as pl
from jax.experimental.pallas import tpu as pltpu
from jax.sharding import PartitionSpec as P

HEADS = 12
HEAD_FEATURES = 64
MAXLEN = 1024
GROUP = 4
PIECE = MAXLEN // GROUP
PAIR = 2 * HEAD_FEATURES

epsilon = 1e-06
masked_score = -1e30
f32 = jnp.float32
bf16 = jnp.bfloat16
MIB = 1024 * 1024


def mm(a, b):
    return lax.dot_general(a, b, (((1,), (0,)), ((), ())), preferred_element_type=f32)


def mm_nt(a, b):
    return lax.dot_general(a, b, (((1,), (1,)), ((), ())), preferred_element_type=f32)


def mm_tn(a, b):
    return lax.dot_general(a, b, (((0,), (0,)), ((), ())), preferred_element_type=f32)


def call(body, grid, in_specs, out_specs, out_shape, scratch=(), aliases=None, vmem=56, flops=0, nbytes=0):
    return pl.pallas_call(
        body,
        grid_spec=pltpu.PrefetchScalarGridSpec(
            num_scalar_prefetch=1,
            grid=grid,
            in_specs=in_specs,
            out_specs=out_specs,
            scratch_shapes=list(scratch),
        ),
        out_shape=out_shape,
        input_output_aliases=aliases or {},
        compiler_params=pltpu.CompilerParams(
            dimension_semantics=("arbitrary",) * len(grid), vmem_limit_bytes=vmem * MIB
        ),
        cost_estimate=pl.CostEstimate(flops=flops, bytes_accessed=nbytes, transcendentals=0),
    )


def whole(shape):
    return pl.BlockSpec(shape, lambda *a: (0,) * len(shape))


def sds(shape, dtype):
    return jax.ShapeDtypeStruct(shape, dtype)


def rope_tables():
    middle = HEAD_FEATURES // 2
    frequency = 10000.0 ** (-np.arange(middle, dtype=np.float64) * 2.0 / HEAD_FEATURES)
    angles = np.arange(MAXLEN, dtype=np.float64)[:, None] * frequency[None, :]
    cosine, sine = np.cos(angles), np.sin(angles)
    none = np.zeros_like(sine)
    table = np.stack(
        [
            np.concatenate([cosine, cosine] * 2, axis=1),
            np.concatenate([-sine, none] * 2, axis=1),
            np.concatenate([none, sine] * 2, axis=1),
        ]
    )
    return table.astype(np.float32)


def rotate(u, table, sign):
    up = pltpu.roll(u, PAIR - HEAD_FEATURES // 2, 1)
    down = pltpu.roll(u, HEAD_FEATURES // 2, 1)
    if sign > 0:
        return u * table[0] + (up * table[1] + down * table[2])
    return u * table[0] - (up * table[1] + down * table[2])


def project_body(s, own, part, gain, wq, wk, wv, table, *rest):
    qkv, normed = rest[-2:]
    x = jnp.where(pl.program_id(0) == s[0], own[...], part[...]).astype(f32)
    r = lax.rsqrt(jnp.mean(x * x, axis=-1, keepdims=True) + epsilon)
    low = (x * r * gain[...].astype(f32)).astype(bf16)
    normed[...] = low
    width = wq.shape[1]
    for m, w in enumerate((wq, wk, wv)):
        u = mm(low, w[...])
        if m == 0:
            u = u * (1.0 / math.sqrt(HEAD_FEATURES))
        for p in range(width // PAIR):
            v = u[:, p * PAIR : (p + 1) * PAIR]
            if m < 2:
                v = rotate(v, table, 1)
            at = m * width + p * PAIR
            qkv[:, at : at + PAIR] = v.astype(bf16)


def project(scalars, own, part, half, gain, weights, table, filled):
    width = weights[0].shape[0]
    cols = width // 2
    place = lambda t, s: (s[half] * 2 + t, 0)
    weight_spec = pl.BlockSpec((width, cols), lambda t, s: (0, s[0]))
    in_specs = [
        whole((PIECE, width)),
        whole((PIECE, width)),
        whole((1, width)),
        weight_spec,
        weight_spec,
        weight_spec,
        pl.BlockSpec((3, PIECE, PAIR), lambda t, s: (0, s[half] * 2 + t, 0)),
    ]
    args = [scalars, own, part, gain, *weights, table]
    aliases = None
    if filled is not None:
        in_specs += [pl.BlockSpec(memory_space=pl.ANY)] * 2
        aliases = {len(args): 0, len(args) + 1: 1}
        args += list(filled)
    return call(
        project_body,
        (2,),
        in_specs,
        [pl.BlockSpec((PIECE, 3 * cols), place), pl.BlockSpec((PIECE, width), place)],
        [sds((MAXLEN, 3 * cols), bf16), sds((MAXLEN, width), bf16)],
        aliases=aliases,
        flops=2 * 512 * width * 3 * cols,
        nbytes=4 * MIB,
    )(*args)


def head_mask(h):
    lane = lax.broadcasted_iota(jnp.int32, (1, PAIR), 1)
    return lane < HEAD_FEATURES if h == 0 else lane >= HEAD_FEATURES


def attend_body(s, q, k, v, out, lse):
    row = lax.broadcasted_iota(jnp.int32, (PIECE, PIECE), 0)
    col = lax.broadcasted_iota(jnp.int32, (PIECE, PIECE), 1)
    lane = lax.broadcasted_iota(jnp.int32, (PIECE, PAIR), 1)
    for b in range(GROUP):
        at = b * PIECE
        joined, logs = None, None
        for h in range(2):
            qh = jnp.where(head_mask(h), q[at : at + PIECE, :], jnp.zeros((), bf16))
            near = mm_nt(qh, k[at : at + PIECE, :])
            near = jnp.where(row >= col, near, masked_score)
            top = jnp.max(near, axis=-1, keepdims=True)
            if b > 0:
                far = mm_nt(qh, k[:at, :])
                top = jnp.maximum(top, jnp.max(far, axis=-1, keepdims=True))
            near = jnp.exp(near - top)
            total = jnp.sum(near, axis=-1, keepdims=True)
            mixed = mm(near.astype(bf16), v[at : at + PIECE, :])
            if b > 0:
                far = jnp.exp(far - top)
                total = total + jnp.sum(far, axis=-1, keepdims=True)
                mixed = mixed + mm(far.astype(bf16), v[:at, :])
            mixed = mixed * (1.0 / total)
            logged = top + jnp.log(total)
            if h == 0:
                joined, logs = mixed, jnp.broadcast_to(logged, (PIECE, PAIR))
            else:
                joined = jnp.where(head_mask(0), joined, mixed)
                logs = jnp.where(lane == 0, logs, logged)
        slot = at + lax.broadcasted_iota(jnp.int32, (PIECE, 1), 0)
        out[at : at + PIECE, :] = jnp.where(slot < s[2], joined, 0.0).astype(bf16)
        lse[0, :, at : at + PIECE] = jnp.transpose(logs)[:8]


def attend(scalars, qkv):
    pairs = qkv.shape[1] // 3 // PAIR
    spec = lambda m: pl.BlockSpec((MAXLEN, PAIR), lambda p, s, m=m: (0, m * pairs + p))
    return call(
        attend_body,
        (pairs,),
        [spec(0), spec(1), spec(2)],
        [pl.BlockSpec((MAXLEN, PAIR), lambda p, s: (0, p)), pl.BlockSpec((1, 8, MAXLEN), lambda p, s: (p, 0, 0))],
        [sds((MAXLEN, pairs * PAIR), bf16), sds((pairs, 8, MAXLEN), f32)],
        flops=8 * 1000 * MIB,
        nbytes=4 * MIB,
    )(scalars, qkv, qkv, qkv)


def attend_back_body(s, q, k, v, o, lse, own, part, wo, table, out, da, dq, dk, dv):
    core = s[0]
    for half in range(2):
        for source, place in ((own, core), (part, 1 - core)):
            at = pl.multiple_of(half * 2 * PIECE + place * PIECE, PIECE)
            slot = at + lax.broadcasted_iota(jnp.int32, (PIECE, 1), 0)
            d = mm_nt(source[half], wo[...])
            da[pl.ds(at, PIECE), :] = jnp.where(slot < s[2], d, 0.0).astype(bf16)
    product = da[...].astype(f32) * o[...].astype(f32)
    ones = jnp.where(
        lax.broadcasted_iota(jnp.int32, (8, PAIR), 0)
        == lax.broadcasted_iota(jnp.int32, (8, PAIR), 1) // HEAD_FEATURES,
        1.0,
        0.0,
    ).astype(f32)
    inner = lax.dot_general(
        ones, product, (((1,), (1,)), ((), ())), preferred_element_type=f32, precision=lax.Precision.HIGHEST
    )
    dq[...] = jnp.zeros_like(dq)
    key = lax.broadcasted_iota(jnp.int32, (PIECE, PIECE), 0)
    query = lax.broadcasted_iota(jnp.int32, (PIECE, PIECE), 1)
    zero = jnp.zeros((), bf16)
    for b in range(GROUP):
        at = b * PIECE
        kb, vb = k[at : at + PIECE, :], v[at : at + PIECE, :]
        key_grad, value_grad = None, None
        for h in range(2):
            mask = head_mask(h)
            kh = jnp.where(mask, kb, zero)
            vh = jnp.where(mask, vb, zero)
            for a in range(b, GROUP):
                to = a * PIECE
                qa = jnp.where(mask, q[to : to + PIECE, :], zero)
                ga = jnp.where(mask, da[to : to + PIECE, :], zero)
                score = mm_nt(kb, qa) - lse[0, h : h + 1, to : to + PIECE]
                if a == b:
                    score = jnp.where(query >= key, score, masked_score)
                prob = jnp.exp(score)
                delta = mm_nt(vb, ga) - inner[h : h + 1, to : to + PIECE]
                ds = (prob * delta).astype(bf16)
                vg = mm(prob.astype(bf16), ga)
                kg = mm(ds, qa)
                value_grad = vg if value_grad is None else value_grad + vg
                key_grad = kg if key_grad is None else key_grad + kg
                dq[to : to + PIECE, :] += mm_tn(ds, kh)
        dk[at : at + PIECE, :] = key_grad
        dv[at : at + PIECE, :] = value_grad
    out[0] = rotate(dq[...] * (1.0 / math.sqrt(HEAD_FEATURES)), table, -1).astype(bf16)
    out[1] = rotate(dk[...], table, -1).astype(bf16)
    out[2] = dv[...].astype(bf16)


def attend_back(scalars, qkv, attn, lse, own, part, wo, table):
    pairs = attn.shape[1] // PAIR
    width = wo.shape[1]
    spec = lambda m: pl.BlockSpec((MAXLEN, PAIR), lambda p, s, m=m: (0, m * pairs + p))
    return call(
        attend_back_body,
        (pairs,),
        [
            spec(0),
            spec(1),
            spec(2),
            spec(0),
            pl.BlockSpec((1, 8, MAXLEN), lambda p, s: (p, 0, 0)),
            whole((2, PIECE, width)),
            whole((2, PIECE, width)),
            pl.BlockSpec((PAIR, width), lambda p, s: (s[0] * pairs + p, 0)),
            whole((3, MAXLEN, PAIR)),
        ],
        pl.BlockSpec((3, MAXLEN, PAIR), lambda p, s: (0, 0, p)),
        sds((3, MAXLEN, pairs * PAIR), bf16),
        scratch=[pltpu.VMEM((MAXLEN, PAIR), bf16)] + [pltpu.VMEM((MAXLEN, PAIR), f32)] * 3,
        flops=16 * 1000 * MIB,
        nbytes=8 * MIB,
    )(scalars, qkv, qkv, qkv, attn, lse, own, part, wo, table)


def split_rows(total, core, count, rows):
    keep = [total[pl.ds(pl.multiple_of((2 * z + core) * rows, 8), rows), :] for z in range(count)]
    send = [total[pl.ds(pl.multiple_of((2 * z + 1 - core) * rows, 8), rows), :] for z in range(count)]
    return keep, send


def feed_body(n_seq, s, x, dy, mine, theirs, wo_mine, wo_theirs, gain, wg, wu, wd, *rest):
    (out, dh, dhb, second, gate_keep, gate_send, up_keep, up_send, down_keep, down_send) = rest[:10]
    hidden, low, low_t, dyb, dyb_t, down, back, acts, dgs, dus, total = rest[10:]
    f = pl.program_id(0)
    core = s[0]
    tokens, width = x.shape
    scale = gain[...].astype(f32)

    def live(t):
        slot = t * 2 * PIECE + core * PIECE + lax.broadcasted_iota(jnp.int32, (PIECE, 1), 0)
        return slot < s[2]

    @pl.when(f == 0)
    def _():
        for t in range(2):
            rows = slice(t * PIECE, (t + 1) * PIECE)
            h = x[rows, :].astype(f32) + mm(mine[t, 0], wo_mine[0]) + mm(theirs[t], wo_theirs[0])
            hidden[rows, :] = h
            r = lax.rsqrt(jnp.mean(h * h, axis=-1, keepdims=True) + epsilon)
            low[rows, :] = (h * r * scale).astype(bf16)
            dyb[rows, :] = jnp.where(live(t), dy[rows, :], jnp.zeros((), bf16))
        low_t[...] = jnp.transpose(low[...])
        dyb_t[...] = jnp.transpose(dyb[...])
        down[...] = jnp.zeros_like(down)
        back[...] = jnp.zeros_like(back)

    for t in range(2):
        rows = slice(t * PIECE, (t + 1) * PIECE)
        gate = mm(low[rows, :], wg[...])
        up = mm(low[rows, :], wu[...])
        dact = mm_nt(dyb[rows, :], wd[...])
        sig = jax.nn.sigmoid(gate)
        silu = gate * sig
        act = (silu * up).astype(bf16)
        dg = (dact * up * (sig * (1.0 + gate * (1.0 - sig)))).astype(bf16)
        du = (dact * silu).astype(bf16)
        acts[rows, :] = act
        dgs[rows, :] = dg
        dus[rows, :] = du
        down[rows, :] += mm(act, wd[...])
        back[rows, :] += mm_nt(dg, wg[...]) + mm_nt(du, wu[...])

    rows = width // n_seq
    count = n_seq // 2
    for grads, keep, send in ((dgs, gate_keep, gate_send), (dus, up_keep, up_send)):
        g = mm(low_t[...], grads[...])
        if rows % 16 == 0:
            total[...] = g
            kept, sent = split_rows(total, core, count, rows)
            for z in range(count):
                keep[z, 0] = kept[z].astype(bf16)
                send[z, 0] = sent[z].astype(bf16)
        else:
            keep[0] = g.astype(bf16)
            send[0] = jnp.zeros_like(send[0])
    g = mm(dyb_t[...], acts[...])
    lanes = down_keep.shape[-1]
    if rows % 16 == 0:
        total[...] = g
        batches = down_keep.shape[1]
        step = width // batches
        for b in range(batches):
            part = slice(b * step, (b + 1) * step)
            down_keep[0, b] = total[part, pl.ds(pl.multiple_of(core * lanes, 128), lanes)].astype(bf16)
            down_send[0, b] = total[part, pl.ds(pl.multiple_of((1 - core) * lanes, 128), lanes)].astype(bf16)
    else:
        down_keep[0] = g.astype(bf16)
        down_send[0] = jnp.zeros_like(down_send[0])

    @pl.when(f == pl.num_programs(0) - 1)
    def _():
        sums = jnp.zeros((1, width), f32)
        for t in range(2):
            rows = slice(t * PIECE, (t + 1) * PIECE)
            h = hidden[rows, :]
            r = lax.rsqrt(jnp.mean(h * h, axis=-1, keepdims=True) + epsilon)
            out[t] = jnp.where(live(t), h + down[rows, :], 0.0).astype(bf16)
            upstream = jnp.where(live(t), dy[rows, :].astype(f32), 0.0)
            dn = back[rows, :]
            sums = sums + jnp.sum(dn * h * r, axis=0, keepdims=True)
            scaled = dn * scale
            inner = jnp.mean(scaled * h, axis=-1, keepdims=True)
            d = upstream + r * scaled - h * (r * r * r) * inner
            dh[t] = d
            dhb[t] = d.astype(bf16)
        second[...] = sums


def feed(scalars, x, dy, attn, theirs, wo, gain, wg, wu, wd, n_seq):
    tokens, width = x.shape
    hidden_units = wg.shape[1]
    heads = attn.shape[1]
    blocks = 4
    cols = hidden_units // blocks
    count, rows = n_seq // 2, width // n_seq
    fast = rows % 16 == 0
    if fast:
        side = pl.BlockSpec((count, 1, rows, cols), lambda f, s: (0, f, 0, 0))
        side_shape = sds((count, blocks, rows, cols), bf16)
        lanes = hidden_units // n_seq
        foot = pl.BlockSpec((1, 4, width // 4, lanes), lambda f, s: (f, 0, 0, 0))
        foot_shape = sds((count, 4, width // 4, lanes), bf16)
        assert cols == 2 * lanes
    else:
        side = pl.BlockSpec((1, width, cols), lambda f, s: (f, 0, 0))
        side_shape = sds((blocks, width, cols), bf16)
        foot = side
        foot_shape = side_shape
    pieces = attn.reshape(2, 2, PIECE, heads)
    wo_parts = wo.reshape(2, heads, width)
    return call(
        functools.partial(feed_body, n_seq),
        (blocks,),
        [
            whole((tokens, width)),
            whole((tokens, width)),
            pl.BlockSpec((2, 1, PIECE, heads), lambda f, s: (0, s[0], 0, 0)),
            whole((2, PIECE, heads)),
            pl.BlockSpec((1, heads, width), lambda f, s: (s[0], 0, 0)),
            pl.BlockSpec((1, heads, width), lambda f, s: (1 - s[0], 0, 0)),
            whole((1, width)),
            pl.BlockSpec((width, cols), lambda f, s: (0, f)),
            pl.BlockSpec((width, cols), lambda f, s: (0, f)),
            pl.BlockSpec((cols, width), lambda f, s: (f, 0)),
        ],
        [whole((2, PIECE, width))] * 3 + [whole((1, width))] + [side] * 4 + [foot] * 2,
        [
            sds((2, PIECE, width), bf16),
            sds((2, PIECE, width), f32),
            sds((2, PIECE, width), bf16),
            sds((1, width), f32),
        ]
        + [side_shape] * 4
        + [foot_shape] * 2,
        scratch=[
            pltpu.VMEM((tokens, width), f32),
            pltpu.VMEM((tokens, width), bf16),
            pltpu.VMEM((width, tokens), bf16),
            pltpu.VMEM((tokens, width), bf16),
            pltpu.VMEM((width, tokens), bf16),
            pltpu.VMEM((tokens, width), f32),
            pltpu.VMEM((tokens, width), f32),
            pltpu.VMEM((tokens, cols), bf16),
            pltpu.VMEM((tokens, cols), bf16),
            pltpu.VMEM((tokens, cols), bf16),
            pltpu.VMEM((width, cols), f32),
        ],
        flops=16 * 1000 * MIB,
        nbytes=24 * MIB,
    )(scalars, x, dy, pieces, theirs, wo_parts, wo_parts, gain, wg, wu, wd)


def emit_rows(total, keep, send, core, n_seq, width):
    rows = width // n_seq
    count = total.shape[0] // rows // 2
    if rows % 16 == 0:
        kept, sent = split_rows(total, core, count, rows)
        for z in range(count):
            keep(z, kept[z].astype(bf16))
            send(z, sent[z].astype(bf16))


def output_grad_body(n_seq, s, attn, own, part, keep, send, total):
    core = s[0]
    width = own.shape[2]
    acc = None
    for half in range(2):
        for source, place in ((own, core), (part, 1 - core)):
            at = pl.multiple_of(half * 2 * PIECE + place * PIECE, PIECE)
            g = mm_tn(attn[pl.ds(at, PIECE), :], source[half])
            acc = g if acc is None else acc + g
    rows = width // n_seq
    if rows % 16 == 0:
        total[...] = acc
        count = total.shape[0] // rows // 2
        kept, sent = split_rows(total, core, count, rows)
        for z in range(count):
            for y in range(2):
                part_of = slice(y * width // 2, (y + 1) * width // 2)
                keep[z, y] = kept[z][:, part_of].astype(bf16)
                send[z, y] = sent[z][:, part_of].astype(bf16)
    else:
        keep[...] = acc.astype(bf16)
        send[...] = jnp.zeros_like(send)


def output_grad(scalars, attn, own, part, n_seq):
    heads = attn.shape[1]
    width = own.shape[2]
    rows = width // n_seq
    shape = (heads // rows // 2, 2, rows, width // 2) if rows % 16 == 0 else (heads, width)
    return call(
        functools.partial(output_grad_body, n_seq),
        (1,),
        [whole(attn.shape), whole(own.shape), whole(part.shape)],
        [whole(shape)] * 2,
        [sds(shape, bf16)] * 2,
        scratch=[pltpu.VMEM((heads, width), f32)],
        flops=2 * 1024 * heads * width,
        nbytes=4 * MIB,
    )(scalars, attn, own, part)


def input_grads_body(n_seq, s, normed, d, keep, send, total):
    core = s[0]
    width = normed.shape[1]
    total[...] = mm_tn(normed[...], d[0])
    rows = width // n_seq
    if rows % 16 == 0:
        count = n_seq // 2
        kept, sent = split_rows(total, core, count, rows)
        for z in range(count):
            keep[0, z] = kept[z].astype(bf16)
            send[0, z] = sent[z].astype(bf16)
    else:
        keep[0] = total[...].astype(bf16)
        send[0] = jnp.zeros_like(send[0])


def input_grads(scalars, normed, d, n_seq):
    width = normed.shape[1]
    heads = d.shape[2]
    rows = width // n_seq
    shape = (3, n_seq // 2, rows, heads) if rows % 16 == 0 else (3, width, heads)
    spec = pl.BlockSpec((1,) + shape[1:], lambda m, s: (m,) + (0,) * (len(shape) - 1))
    return call(
        functools.partial(input_grads_body, n_seq),
        (3,),
        [whole(normed.shape), pl.BlockSpec((1,) + d.shape[1:], lambda m, s: (m, 0, 0))],
        [spec] * 2,
        [sds(shape, bf16)] * 2,
        scratch=[pltpu.VMEM((width, heads), f32)],
        flops=2 * 1024 * 3 * heads * width,
        nbytes=6 * MIB,
    )(scalars, normed, d)


def norm_grad_body(s, d, wq, wk, wv, keep, send):
    core = s[0]
    for half in range(2):
        for place, target in ((core, keep), (1 - core, send)):
            at = pl.multiple_of(half * 2 * PIECE + place * PIECE, PIECE)
            acc = None
            for m, w in enumerate((wq, wk, wv)):
                g = mm_nt(d[m, pl.ds(at, PIECE), :], w[...])
                acc = g if acc is None else acc + g
            target[half] = acc.astype(target.dtype)


def norm_grad(scalars, d, weights):
    width = weights[0].shape[0]
    heads = d.shape[2]
    weight_spec = pl.BlockSpec((width, heads), lambda m, s: (0, s[0]))
    shape = (2, PIECE, width)
    return call(
        norm_grad_body,
        (1,),
        [whole(d.shape), weight_spec, weight_spec, weight_spec],
        [whole(shape)] * 2,
        [sds(shape, f32), sds(shape, bf16)],
        flops=2 * 1024 * 3 * heads * width,
        nbytes=8 * MIB,
    )(scalars, d, *weights)


def finish_body(s, x, keep, recv, dh, gain, out, first):
    scale = gain[...].astype(f32)
    sums = jnp.zeros((1, x.shape[1]), f32)
    for t in range(2):
        rows = slice(t * PIECE, (t + 1) * PIECE)
        h = x[rows, :].astype(f32)
        dn = keep[t] + recv[t].astype(f32)
        r = lax.rsqrt(jnp.mean(h * h, axis=-1, keepdims=True) + epsilon)
        sums = sums + jnp.sum(dn * h * r, axis=0, keepdims=True)
        scaled = dn * scale
        inner = jnp.mean(scaled * h, axis=-1, keepdims=True)
        out[t] = (dh[t] + r * scaled - h * (r * r * r) * inner).astype(bf16)
    first[...] = sums


def finish(scalars, x, keep, recv, dh, gain):
    width = x.shape[1]
    shape = (2, PIECE, width)
    return call(
        finish_body,
        (1,),
        [whole(x.shape), whole(shape), whole(shape), whole(shape), whole((1, width))],
        [whole(shape), whole((1, width))],
        [sds(shape, bf16), sds((1, width), f32)],
        flops=20 * 512 * width,
        nbytes=6 * MIB,
    )(scalars, x, keep, recv, dh, gain)


def exchange(block, axis, bit):
    count = lax.axis_size(axis)
    return lax.ppermute(block, axis, [(a, a ^ (1 << bit)) for a in range(count)])


def pick(block, index, dim):
    return lax.dynamic_index_in_dim(block, index, dim, keepdims=False)


class Bits:
    def __init__(self):
        self.seq_bits = int(math.log2(lax.axis_size("seq")))
        self.batch_bits = int(math.log2(lax.axis_size("batch")))
        self.chip_seq = [("seq", b) for b in reversed(range(1, self.seq_bits))]
        self.chip_batch = [("batch", b) for b in reversed(range(self.batch_bits))]

    def own(self, name):
        axis, bit = name
        return lax.axis_index(axis) >> bit & 1


def reduce_stage(array, names, name, bits, last=False):
    dim = names.index(name)
    own = bits.own(name)
    sent = pick(array, 1 - own, dim)
    kept = pick(array, own, dim)
    arrived = exchange(sent, *name)
    out = kept.astype(f32) + arrived.astype(f32)
    if not last:
        out = out.astype(bf16)
    return out, names[:dim] + names[dim + 1 :]


def reduce_all(array, names, order, bits):
    for at, name in enumerate(order):
        array, names = reduce_stage(array, names, name, bits, last=at == len(order) - 1)
    return array


def body(
    states,
    lengths,
    first_gain,
    query_weight,
    key_weight,
    value_weight,
    output_weight,
    second_gain,
    gate_weight,
    up_weight,
    down_weight,
    cotangent,
):
    tokens, width = states.shape
    n_seq, n_batch = lax.axis_size("seq"), lax.axis_size("batch")
    bits = Bits()
    place = lax.axis_index("seq")
    core = place & 1
    chip = place >> 1 & 1
    sequence = (lax.axis_index("batch") * (n_seq // GROUP) + place // GROUP) * 2 + chip
    length = pick(lengths, sequence, 0)
    scalars = jnp.stack([core, chip, length, 1 - chip]).astype(jnp.int32)
    table = jnp.asarray(rope_tables())
    gain_first = first_gain.reshape(1, width)
    gain_second = second_gain.reshape(1, width)
    weights = (query_weight, key_weight, value_weight)

    held = states.reshape(2, PIECE, width)
    mine = pick(held, chip, 0)
    arrived = exchange(pick(held, 1 - chip, 0), "seq", 1)
    mine_pair = exchange(mine, "seq", 0)
    arrived_pair = exchange(arrived, "seq", 0)
    held_back = cotangent.reshape(2, PIECE, width)
    back_mine = pick(held_back, chip, 0)
    back_arrived = exchange(pick(held_back, 1 - chip, 0), "seq", 1)

    def in_order(a, b):
        return jnp.concatenate([jnp.where(chip == 0, a, b), jnp.where(chip == 0, b, a)], axis=0)

    filled = project(scalars, mine, mine_pair, 1, gain_first, weights, table, None)
    qkv, normed = project(scalars, arrived, arrived_pair, 3, gain_first, weights, table, filled)
    attn, lse = attend(scalars, qkv)
    heads = attn.shape[1]
    x_own = in_order(mine, arrived)
    dy_own = in_order(back_mine, back_arrived)
    theirs = exchange(pick(attn.reshape(2, 2, PIECE, heads), 1 - core, 1), "seq", 0)
    (layer, dh, dhb, second, gate_keep, gate_send, up_keep, up_send, down_keep, down_send) = feed(
        scalars, x_own, dy_own, attn, theirs, output_weight, gain_second, gate_weight, up_weight, down_weight, n_seq
    )
    dhb_pair = exchange(dhb, "seq", 0)

    rows = width // n_seq
    fast = rows % 16 == 0
    count = n_seq // 2
    if not fast:

        def by_rows(array):
            array = array.reshape(n_batch, count, 2, rows, -1)
            return tuple(jnp.swapaxes(pick(array, a, 2), 0, 1) for a in (core, 1 - core))

        def by_lanes(array):
            array = jnp.swapaxes(array, 0, 1).reshape(n_batch, width // n_batch, count, 2, -1)
            return tuple(jnp.moveaxis(pick(array, a, 3), 2, 0) for a in (core, 1 - core))

        gate_keep, gate_send = by_rows(gate_keep)
        up_keep, up_send = by_rows(up_keep)
        down_keep, down_send = by_lanes(down_keep)

    chip_shape = (2,) * (bits.seq_bits - 1)
    batch_shape = (2,) * bits.batch_bits
    names = bits.chip_seq + bits.chip_batch
    *_, high, low = [None] + bits.chip_batch
    along = list(reversed(bits.chip_seq))

    def summed(keep, send):
        arrived = exchange(send, "seq", 0)
        out = (keep.astype(f32) + arrived.astype(f32)).astype(bf16)
        return out.reshape(chip_shape + batch_shape + out.shape[-2:])

    gate_grad = reduce_all(summed(gate_keep, gate_send), names, [low, high] + along, bits)
    up_grad = reduce_all(summed(up_keep, up_send), names, [high, low] + along, bits)
    down_grad = reduce_all(summed(down_keep, down_send), names, along[:1] + [low, high] + along[1:], bits)

    out_keep, out_send = output_grad(scalars, attn, dhb, dhb_pair, n_seq)
    if not fast:

        def out_rows(array):
            array = array.reshape(count // 2, 2, rows, 2, width // 2)
            return tuple(jnp.swapaxes(pick(array, a, 1), 1, 2) for a in (core, 1 - core))

        out_keep, out_send = out_rows(out_keep)
    out_arrived = exchange(out_send, "seq", 0)
    first_half = jnp.where(core == 0, out_keep, out_arrived)
    second_half = jnp.where(core == 0, out_arrived, out_keep)
    out_whole = jnp.concatenate([first_half, second_half], axis=0)
    narrow = bits.chip_seq + [high]

    def finish_columns(array, names, order):
        for name in order:
            array, names = reduce_stage(array, names, name, bits)
        halves = array.reshape(array.shape[0], 2, -1)
        sent = jnp.where(bits.own(low) == 0, halves[:, 1], halves[:, 0])
        kept = jnp.where(bits.own(low) == 0, halves[:, 0], halves[:, 1])
        return kept.astype(f32) + exchange(sent, *low).astype(f32)

    out_whole = out_whole.reshape(chip_shape + (2,) + out_whole.shape[-2:])
    output_grad_shard = finish_columns(out_whole, narrow, along + [high])

    d = attend_back(scalars, qkv, attn, lse, dhb, dhb_pair, output_weight, table)
    keep3, send3 = input_grads(scalars, normed, d, n_seq)
    if not fast:
        parted = keep3.reshape(3, count, 2, rows, heads)
        keep3, send3 = pick(parted, core, 2), pick(parted, 1 - core, 2)
    arrived3 = exchange(send3, "seq", 0)
    left = jnp.where(core == 0, keep3, arrived3)
    right = jnp.where(core == 0, arrived3, keep3)
    joined = jnp.stack([left, right], axis=2)
    joined = joined.reshape((3,) + chip_shape + (2,) + joined.shape[-2:])
    shards = [
        finish_columns(joined[0], narrow, [high] + along),
        finish_columns(joined[1], narrow, along[:1] + [high] + along[1:]),
        finish_columns(joined[2], narrow, along[:1] + [high] + along[1:]),
    ]

    norm_keep, norm_send = norm_grad(scalars, d, weights)
    norm_arrived = exchange(norm_send, "seq", 0)
    grad, first = finish(scalars, x_own, norm_keep, norm_arrived, dh, gain_first)

    def give_back(array):
        kept = pick(array, chip, 0)
        arrived = exchange(pick(array, 1 - chip, 0), "seq", 1)
        return in_order(kept, arrived)

    layer_out = give_back(layer)
    input_grad = give_back(grad)

    gains = jnp.concatenate([first, second], axis=0)
    for name in [("seq", 0)] + bits.chip_batch + bits.chip_seq:
        gains = gains + exchange(gains, *name)

    return (
        layer_out,
        input_grad,
        gains[0],
        shards[0],
        shards[1],
        shards[2],
        output_grad_shard,
        gains[1],
        gate_grad,
        up_grad,
        jnp.transpose(down_grad),
    )


def solution(mesh):
    split = P(("batch", "seq"), None)
    in_specs = (split,) + (P(),) * 10 + (split,)
    shard = P("seq", "batch")
    out_specs = (split, split, P(), shard, shard, shard, shard, P(), shard, shard, shard)
    return jax.shard_map(body, mesh=mesh, in_specs=in_specs, out_specs=out_specs, check_vma=False)
```

time: 902 us -> 259 us (0.29); the launches traced: 891 us -> 259 us
  waiting for transfers between devices: 505 us -> 73.7 us
  matrix products: 126 us -> 0 us
  Pallas kernels: 0 us -> 96.7 us
  local copies, waits for them, and re-layouts: 98.2 us -> 16.6 us
  other arithmetic: 99 us -> 22.5 us
  starting transfers between devices: 9.32 us -> 47.9 us
  blocking collectives: 37.8 us -> 0 us
  between operations: 14.8 us -> 1.35 us
    reduce_scatter x9 -> x0, waiting for transfers between devices: 332 us -> none  [the longest x1 69.3 us: body(): lax.psum_scatter(weight_terms[6], 'seq', scatter_dimension=0, tiled=True)]
    dot_general x43 -> x0, matrix products: 126 us -> none  [the longest x4 21.2 us: attend_back(): jnp.einsum('qhe,khe->hqk', grad_block, value_rows, preferred_element_type...]
    pallas_call x0 -> x9, Pallas kernels: none -> 96.7 us  [the longest x1 26.3 us: attend_back(): call(attend_back_body, (pairs,), [spec(0), spec(1), spec(2), spec(0), pl....]
    unnamed x19 -> x0, waiting for transfers between devices: 79.5 us -> none
    ppermute x8 -> x47, starting transfers between devices: 8.53 us -> 47.9 us  [exchange(): return lax.ppermute(block, axis, [(a, a ^ 1 << bit) for a in range(count)])]
    psum x1 -> x0, blocking collectives: 37.8 us -> none  [body(): gain_total = lax.psum((first_grad, second_grad), ('batch', 'seq'))]
    convert_element_type x27 -> x24, other arithmetic: 37.3 us -> 8.2 us  [the longest x21 6.66 us: reduce_stage(): out = out.astype(bf16)]
    select_n x8 -> x10, other arithmetic: 24.3 us -> 2.3 us  [the longest x4 1.36 us: in_order(): jnp.where(chip == 0, a, b)]
  transfers between devices with their start and end apart: 22 -> 47, of which waited for: 19 -> 26; matrix products, arithmetic and copies ran while one was open for 12% -> 13% of each run, Pallas kernels for 0% -> 28%
where the time goes in v1:
time: 259 us
  Pallas kernels  96.7 us (37%)
  waiting for transfers between devices  73.7 us (28%)
  starting transfers between devices  47.9 us (18%)
  other arithmetic  22.5 us (9%)
  local copies, waits for them, and re-layouts  16.6 us (6%)
    ppermute x47, waiting for transfers between devices, exchange(): return lax.ppermute(block, axis, [(a, a ^ 1 << bit) for a in range(count)])  73.7 us
    ppermute x47, starting transfers between devices, exchange(): return lax.ppermute(block, axis, [(a, a ^ 1 << bit) for a in range(count)])  47.9 us
    pallas_call x1, Pallas kernels, attend_back(): call(attend_back_body, (pairs,), [spec(0), spec(1), spec(2), spec(0), pl....  26.3 us
    pallas_call x1, Pallas kernels, feed(): call(functools.partial(feed_body, n_seq), (blocks,), [whole((tokens, widt...  25.4 us
    pallas_call x1, Pallas kernels, attend(): call(attend_body, (pairs,), [spec(0), spec(1), spec(2)], [pl.BlockSpec((M...  12.3 us
    pallas_call x2, Pallas kernels, project(): call(project_body, (2,), in_specs, [pl.BlockSpec((PIECE, 3 * cols), place...  10.4 us
    pallas_call x1, Pallas kernels, norm_grad(): call(norm_grad_body, (1,), [whole(d.shape), weight_spec, weight_spec, wei...  6.91 us
    convert_element_type x21, other arithmetic, reduce_stage(): out = out.astype(bf16)  6.66 us
  transfers between devices with their start and end apart: 47, of which 26 were waited for; matrix products, arithmetic and copies ran while one was open for 13% of the time, Pallas kernels for 28%

profile of v1, /device:TPU:0, one launch (start us, length us, event | category | flops | bytes accessed | tf_op | source)
XLA Modules:
  0.0 258.7 jit_solution(3691266980908906558)
XLA Ops:
  0.7 1.1 dynamic-slice_bitcast_fusion.7
  1.8 3.1 %collective-permute-start = (bf16[256,768]{1,0:T(8,128)(2,1)S(1)}, bf16[256,768]{1,0:T(8,128)(2,1)S(1)}, u32[]{:S(2)}, u32[]{:S(2)}) collective-permute-start(bf16[256,768]{1,0:T(8,128)(2,1)S(1)} %dynamic-slice_bitcast_fusion.7), channel_id=1, source_target_pairs={{0,2},{1,3},{2,0},{3,1},{4,6},{5,7},{6,4},{7,5},{8,10},{9,11},{10,... | collective-permute-start | bytes 1179656 | tf_op jit(solution)/shard_map/ppermute | solution.py:573
  4.9 9.1 %collective-permute-done.own = bf16[256,768]{1,0:T(8,128)(2,1)S(1)} collective-permute-done((bf16[256,768]{1,0:T(8,128)(2,1)S(1)}, bf16[256,768]{1,0:T(8,128)(2,1)S(1)}, u32[]{:S(2)}, u32[]{:S(2)}) %collective-permute-start) | collective-permute-done | bytes 393248 | tf_op jit(solution)/shard_map/ppermute | solution.py:573
  14.0 1.2 broadcast_select_fusion.1
  15.3 1.8 collective-permute-start.1
  17.9 1.2 pad_add_fusion.s
  21.2 5.2 %shard_map.212 = (bf16[1024,1152]{1,0:T(8,128)(2,1)}, bf16[1024,768]{1,0:T(8,128)(2,1)}) custom-call(s32[4]{0:T(128)} %pad_add_fusion.s, bf16[256,768]{1,0:T(8,128)(2,1)} %copy-done.1, bf16[256,768]{1,0:T(8,128)(2,1)} %copy-done.13, bf16[1,768]{1,0:T(2,128)(2,1)} %reshape.146.gain, bf16[768,768]{1,0:T(8,128)(2,1)} %wq.5, bf16[768,768]{1,0:T(8,128)(2,1)} %wk.5, ...), custom_call_target="tpu_custom_call" | custom-call | flops 905969664 | bytes 4194304 | tf_op jit(solution)/shard_map/pallas_call | solution.py:128
  27.2 5.2 %shard_map.213 = (bf16[1024,1152]{1,0:T(8,128)(2,1)}, bf16[1024,768]{1,0:T(8,128)(2,1)}) custom-call(s32[4]{0:T(128)} %pad_add_fusion.s, bf16[256,768]{1,0:T(8,128)(2,1)} %copy-done, bf16[256,768]{1,0:T(8,128)(2,1)} %copy-done.12, bf16[1,768]{1,0:T(2,128)(2,1)} %reshape.146.gain, bf16[768,768]{1,0:T(8,128)(2,1)} %wq.5, ...), custom_call_target="tpu_custom_call", output_to_operand_aliasing={{0}: (8, {}), {1}: (9, {})} | custom-call | flops 905969664 | bytes 4194304 | tf_op jit(solution)/shard_map/pallas_call | solution.py:128
  32.3 12.3 %shard_map.214 = (bf16[1024,384]{1,0:T(8,128)(2,1)}, f32[3,8,1024]{2,1,0:T(8,128)}) custom-call(s32[4]{0:T(128)} %pad_add_fusion.s, bf16[1024,1152]{1,0:T(8,128)(2,1)} %get-tuple-element.37.q.k.v, bf16[1024,1152]{1,0:T(8,128)(2,1)} %get-tuple-element.37.q.k.v, bf16[1024,1152]{1,0:T(8,128)(2,1)} %get-tuple-element.37.q.k.v), custom_call_target="tpu_custom_call" | custom-call | flops 8388608000 | bytes 4194304 | tf_op jit(solution)/shard_map/pallas_call | solution.py:182
  44.7 1.0 dynamic-slice_bitcast_fusion.5
  48.8 25.4 %shard_map.215 = (bf16[2,256,768]{2,1,0:T(8,128)(2,1)}, f32[2,256,768]{2,1,0:T(8,128)}, bf16[2,256,768]{2,1,0:T(8,128)(2,1)}, f32[1,768]{1,0:T(1,128)}, bf16[4,4...) custom-call(s32[4]{0:T(128)} %pad_add_fusion.s, ...), custom_call_target="tpu_custom_call" | custom-call | flops 16777216000 | bytes 25165824 | tf_op jit(solution)/shard_map/pallas_call | solution.py:387
  74.4 1.8 dynamic-slice_bitcast_fusion.4
  78.1 3.9 %shard_map.220 = (bf16[2,2,96,384]{3,2,1,0:T(8,128)(2,1)}, bf16[2,2,96,384]{3,2,1,0:T(8,128)(2,1)}) custom-call(s32[4]{0:T(128)} %pad_add_fusion.s, bf16[1024,384]{1,0:T(8,128)(2,1)} %get-tuple-element.38.o.attn, bf16[2,256,768]{2,1,0:T(8,128)(2,1)} %get-tuple-element.41.own, bf16[2,256,768]{2,1,0:T(8,128)(2,1)} %copy-done.6), custom_call_target="tpu_custom_call" | custom-call | flops 603979776 | bytes 4194304 | tf_op jit(solution)/shard_map/pallas_call | solution.py:468
  82.5 5.3 %collective-permute-done.5 = bf16[256,768]{1,0:T(8,128)(2,1)S(1)} collective-permute-done((bf16[256,768]{1,0:T(8,128)(2,1)}, bf16[256,768]{1,0:T(8,128)(2,1)S(1)}, u32[]{:S(2)}, u32[]{:S(2)}) %collective-permute-start.5) | collective-permute-done | bytes 393248 | tf_op jit(solution)/shard_map/ppermute | solution.py:573
  89.4 26.3 %shard_map.216.d = bf16[3,1024,384]{2,1,0:T(8,128)(2,1)} custom-call(s32[4]{0:T(128)} %pad_add_fusion.s, bf16[1024,1152]{1,0:T(8,128)(2,1)} %get-tuple-element.37.q.k.v, bf16[1024,1152]{1,0:T(8,128)(2,1)} %get-tuple-element.37.q.k.v, bf16[1024,1152]{1,0:T(8,128)(2,1)} %get-tuple-element.37.q.k.v, bf16[1024,384]{1,0:T(8,128)(2,1)} %get-tuple-element.38.o.attn, ...), custom_call_target="tpu_custom_call" | custom-call | flops 16777216000 | bytes 8388608 | tf_op jit(solution)/shard_map/pallas_call | solution.py:249
  115.6 6.6 %shard_map.219 = (bf16[3,4,96,384]{3,2,1,0:T(8,128)(2,1)}, bf16[3,4,96,384]{3,2,1,0:T(8,128)(2,1)}) custom-call(s32[4]{0:T(128)} %pad_add_fusion.s, bf16[1024,768]{1,0:T(8,128)(2,1)} %get-tuple-element.48.normed, bf16[3,1024,384]{2,1,0:T(8,128)(2,1)} %shard_map.216.d), custom_call_target="tpu_custom_call" | custom-call | flops 1811939328 | bytes 6291456 | tf_op jit(solution)/shard_map/pallas_call | solution.py:502
  122.4 2.8 %collective-permute-start.29 = (bf16[2,96,384]{2,1,0:T(8,128)(2,1)S(1)}, bf16[2,96,384]{2,1,0:T(8,128)(2,1)S(1)}, u32[]{:S(2)}, u32[]{:S(2)}) collective-permute-start(bf16[2,96,384]{2,1,0:T(8,128)(2,1)S(1)} %dynamic-slice_bitcast_fusion.15), channel_id=1, source_target_pairs={{0,4},{1,5},{2,6},{3,7},{4,0},{5,1},{6,2},{7,3},{8,12},{9,13},{10,... | collective-permute-start | bytes 442376 | tf_op jit(solution)/shard_map/ppermute | solution.py:573
  125.2 6.9 %shard_map.217 = (f32[2,256,768]{2,1,0:T(8,128)}, bf16[2,256,768]{2,1,0:T(8,128)(2,1)}) custom-call(s32[4]{0:T(128)} %pad_add_fusion.s, bf16[3,1024,384]{2,1,0:T(8,128)(2,1)} %shard_map.216.d, bf16[768,768]{1,0:T(8,128)(2,1)} %wq.5, bf16[768,768]{1,0:T(8,128)(2,1)} %wk.5, bf16[768,768]{1,0:T(8,128)(2,1)} %wv.5), custom_call_target="tpu_custom_call" | custom-call | flops 1811939328 | bytes 8388608 | tf_op jit(solution)/shard_map/pallas_call | solution.py:531
  133.5 1.6 collective-permute-start.30
  136.7 1.0 collective-permute-start.43
  140.2 4.8 %shard_map.218 = (bf16[2,256,768]{2,1,0:T(8,128)(2,1)}, f32[1,768]{1,0:T(1,128)}) custom-call(s32[4]{0:T(128)} %pad_add_fusion.s, bf16[512,768]{1,0:T(8,128)(2,1)} %pad_maximum_fusion.x, f32[2,256,768]{2,1,0:T(8,128)} %get-tuple-element.42.keep, bf16[2,256,768]{2,1,0:T(8,128)(2,1)} %copy-done.7, f32[2,256,768]{2,1,0:T(8,128)} %get-tuple-element.44.dh, ...), custom_call_target="tpu_custom_call" | custom-call | flops 7864320 | bytes 6291456 | tf_op jit(solution)/shard_map/pallas_call | solution.py:560
  147.0 1.2 collective-permute-start.10
  148.3 10.7 %collective-permute-done.10 = f32[2,768]{1,0:T(2,128)S(1)} collective-permute-done((f32[2,768]{1,0:T(2,128)S(1)}, f32[2,768]{1,0:T(2,128)S(1)}, u32[]{:S(2)}, u32[]{:S(2)}) %collective-permute-start.10) | collective-permute-done | bytes 6176 | tf_op jit(solution)/shard_map/ppermute | solution.py:573
  159.1 1.6 collective-permute-start.11
  161.4 1.0 copy.131
  162.8 1.5 collective-permute-start.33
  164.3 3.1 %collective-permute-start.12 = (f32[2,768]{1,0:T(2,128)S(1)}, f32[2,768]{1,0:T(2,128)S(1)}, u32[]{:S(2)}, u32[]{:S(2)}) collective-permute-start(f32[2,768]{1,0:T(2,128)S(1)} %add.223), channel_id=1, source_target_pairs={{0,4},{1,5},{2,6},{3,7},{4,0},{5,1},{6,2},{7,3},{8,12},{9,13},{10,... | collective-permute-start | bytes 18440 | tf_op jit(solution)/shard_map/ppermute | solution.py:573
  167.4 1.5 fusion.20
  169.0 1.0 reshape.154
  170.0 1.1 collective-permute-start.13
  171.3 2.4 collective-permute-done.13
  173.7 1.1 collective-permute-start.8
  175.8 1.3 select_bitcast_fusion
  177.4 4.6 %collective-permute-done.31 = bf16[96,192]{1,0:T(8,128)(2,1)S(1)} collective-permute-done((bf16[96,192]{1,0:T(8,128)(2,1)S(1)}, bf16[96,192]{1,0:T(8,128)(2,1)S(1)}, u32[]{:S(2)}, u32[]{:S(2)}) %collective-permute-start.31) | collective-permute-done | bytes 36896 | tf_op jit(solution)/shard_map/ppermute | solution.py:573
  182.0 1.0 collective-permute-start.23
  183.9 5.7 %collective-permute-done.23 = bf16[2,2,96,384]{3,2,0,1:T(8,128)(2,1)S(1)} collective-permute-done((bf16[2,2,96,384]{3,2,0,1:T(8,128)(2,1)S(1)}, bf16[2,2,96,384]{3,2,0,1:T(8,128)(2,1)S(1)}, u32[]{:S(2)}, u32[]{:S(2)}) %collective-permute-start.23) | collective-permute-done | bytes 294944 | tf_op jit(solution)/shard_map/ppermute | solution.py:573
  189.5 1.0 collective-permute-start.19
  190.7 5.6 %collective-permute-done.19 = bf16[2,2,96,384]{3,2,0,1:T(8,128)(2,1)S(1)} collective-permute-done((bf16[2,2,96,384]{3,2,0,1:T(8,128)(2,1)S(1)}, bf16[2,2,96,384]{3,2,0,1:T(8,128)(2,1)S(1)}, u32[]{:S(2)}, u32[]{:S(2)}) %collective-permute-start.19) | collective-permute-done | bytes 294944 | tf_op jit(solution)/shard_map/ppermute | solution.py:573
  196.9 1.6 collective-permute-start.24
  198.6 6.0 %collective-permute-done.15 = bf16[2,2,96,384]{3,2,0,1:T(8,128)(2,1)S(1)} collective-permute-done((bf16[2,2,96,384]{3,2,0,1:T(8,128)(2,1)S(1)}, bf16[2,2,96,384]{3,2,0,1:T(8,128)(2,1)S(1)}, u32[]{:S(2)}, u32[]{:S(2)}) %collective-permute-start.15) | collective-permute-done | bytes 294944 | tf_op jit(solution)/shard_map/ppermute | solution.py:573
  206.1 1.0 collective-permute-start.16
  207.2 2.5 collective-permute-done.20
  209.7 2.8 %collective-permute-start.25 = (bf16[96,384]{1,0:T(8,128)(2,1)S(1)}, bf16[96,384]{1,0:T(8,128)(2,1)S(1)}, u32[]{:S(2)}, u32[]{:S(2)}) collective-permute-start(bf16[96,384]{1,0:T(8,128)(2,1)S(1)} %dynamic-slice_bitcast_fusion.23), channel_id=1, source_target_pairs={{0,4},{1,5},{2,6},{3,7},{4,0},{5,1},{6,2},{7,3},{8,12},{9,13},{10,... | collective-permute-start | bytes 221192 | tf_op jit(solution)/shard_map/ppermute | solution.py:573
  212.7 1.4 collective-permute-start.21
  214.2 1.7 collective-permute-done.25
  215.9 2.0 collective-permute-start.17
  219.9 2.0 collective-permute-done.17
  221.9 1.2 collective-permute-start.22
  225.1 1.6 collective-permute-done.22
  227.3 1.0 collective-permute-done.18
  228.9 1.3 fusion
  231.2 1.3 fusion.1
  232.6 1.2 collective-permute-start.39
  233.8 1.3 fusion.2
  236.0 2.1 collective-permute-done.44
  239.0 3.3 %collective-permute-done.39 = bf16[2,2,96,512]{3,2,0,1:T(8,128)(2,1)S(1)} collective-permute-done((bf16[2,2,96,512]{3,2,0,1:T(8,128)(2,1)S(1)}, bf16[2,2,96,512]{3,2,0,1:T(8,128)(2,1)S(1)}, u32[]{:S(2)}, u32[]{:S(2)}) %collective-permute-start.39) | collective-permute-done | bytes 393248 | tf_op jit(solution)/shard_map/ppermute | solution.py:573
  242.5 1.1 collective-permute-start.40
  243.7 1.1 collective-permute-start.35
  245.2 1.7 collective-permute-start.46
  246.9 1.3 collective-permute-done.40
  248.3 1.5 collective-permute-start.41
  249.8 1.5 collective-permute-done.35
  252.8 2.2 collective-permute-done.41
  255.6 2.4 collective-permute-done.36
  (181 shorter events, 36.2 us)
Async XLA Ops:
  0.6 14.6 %copy-start.8 = (bf16[512,768]{1,0:T(8,128)(2,1)S(1)}, bf16[512,768]{1,0:T(8,128)(2,1)}, u32[]{:S(2)}) copy-start(bf16[512,768]{1,0:T(8,128)(2,1)} %param.24) | copy-start | bytes 2359300
  0.7 16.5 %copy-start.20 = (s32[16]{0:T(128)S(1)}, s32[16]{0:T(128)}, u32[]{:S(2)}) copy-start(s32[16]{0:T(128)} %param.14) | copy-start | bytes 196
  0.7 18.5 %copy-start.17 = (bf16[768]{0:T(1024)(128)(2,1)S(1)}, bf16[768]{0:T(1024)(128)(2,1)}, u32[]{:S(2)}) copy-start(bf16[768]{0:T(1024)(128)(2,1)} %param.15) | copy-start | bytes 4612
  0.7 19.1 %copy-start.18 = (bf16[768]{0:T(1024)(128)(2,1)S(1)}, bf16[768]{0:T(1024)(128)(2,1)}, u32[]{:S(2)}) copy-start(bf16[768]{0:T(1024)(128)(2,1)} %param.20) | copy-start | bytes 4612
  1.8 12.2 %collective-permute-start = (bf16[256,768]{1,0:T(8,128)(2,1)S(1)}, bf16[256,768]{1,0:T(8,128)(2,1)S(1)}, u32[]{:S(2)}, u32[]{:S(2)}) collective-permute-start(bf16[256,768]{1,0:T(8,128)(2,1)S(1)} %dynamic-slice_bitcast_fusion.7), channel_id=1, source_target_pairs={{0,2},{1,3},{2,0},{3,1},{4,6},{5,7},{6,4},{7,5},{8,10},{9,11},{10,... | collective-permute-start | bytes 1179656 | tf_op jit(solution)/shard_map/ppermute | solution.py:573
  14.0 6.4 %copy-start = (bf16[256,768]{1,0:T(8,128)(2,1)}, bf16[256,768]{1,0:T(8,128)(2,1)S(1)}, u32[]{:S(2)}) copy-start(bf16[256,768]{1,0:T(8,128)(2,1)S(1)} %collective-permute-done.own) | copy-start | bytes 1179652
  15.2 5.2 %copy-start.1 = (bf16[256,768]{1,0:T(8,128)(2,1)}, bf16[256,768]{1,0:T(8,128)(2,1)S(1)}, u32[]{:S(2)}) copy-start(bf16[256,768]{1,0:T(8,128)(2,1)S(1)} %get-tuple-element.62.own) | copy-start | bytes 1179652
  15.2 5.2 %collective-permute-start.3 = (bf16[256,768]{1,0:T(8,128)(2,1)S(1)}, bf16[256,768]{1,0:T(8,128)(2,1)S(1)}, u32[]{:S(2)}, u32[]{:S(2)}) collective-permute-start(bf16[256,768]{1,0:T(8,128)(2,1)S(1)} %get-tuple-element.62.own), channel_id=1, source_target_pairs={{0,1},{1,0},{2,3},{3,2},{4,5},{5,4},{6,7},{7,6},{8,9},{9,8},{10,11... | collective-permute-start | bytes 1179656 | tf_op jit(solution)/shard_map/ppermute | solution.py:573
  15.3 31.7 %collective-permute-start.1 = (bf16[256,768]{1,0:T(8,128)(2,1)S(1)}, bf16[256,768]{1,0:T(8,128)(2,1)S(1)}, u32[]{:S(2)}, u32[]{:S(2)}) collective-permute-start(bf16[256,768]{1,0:T(8,128)(2,1)S(1)} %dynamic-slice_bitcast_fusion.6), channel_id=1, source_target_pairs={{0,2},{1,3},{2,0},{3,1},{4,6},{5,7},{6,4},{7,5},{8,10},{9,11},{10,... | collective-permute-start | bytes 1179656 | tf_op jit(solution)/shard_map/ppermute | solution.py:573
  17.7 8.7 %collective-permute-start.2 = (bf16[256,768]{1,0:T(8,128)(2,1)S(1)}, bf16[256,768]{1,0:T(8,128)(2,1)S(1)}, u32[]{:S(2)}, u32[]{:S(2)}) collective-permute-start(bf16[256,768]{1,0:T(8,128)(2,1)S(1)} %collective-permute-done.own), channel_id=1, source_target_pairs={{0,1},{1,0},{2,3},{3,2},{4,5},{5,4},{6,7},{7,6},{8,9},{9,8},{10,11... | collective-permute-start | bytes 1179656 | tf_op jit(solution)/shard_map/ppermute | solution.py:573
  45.7 2.3 collective-permute-start.4
  74.2 3.0 %collective-permute-start.6 = (bf16[2,256,768]{2,1,0:T(8,128)(2,1)}, bf16[2,256,768]{2,1,0:T(8,128)(2,1)S(1)}, u32[]{:S(2)}, u32[]{:S(2)}) collective-permute-start(bf16[2,256,768]{2,1,0:T(8,128)(2,1)} %get-tuple-element.41.own), channel_id=1, source_target_pairs={{0,1},{1,0},{2,3},{3,2},{4,5},{5,4},{6,7},{7,6},{8,9},{9,8},{10,11... | collective-permute-start | bytes 2359304 | tf_op jit(solution)/shard_map/ppermute | solution.py:573
  74.4 13.4 %copy-start.11 = (bf16[2,256,768]{2,1,0:T(8,128)(2,1)S(1)}, bf16[2,256,768]{2,1,0:T(8,128)(2,1)}, u32[]{:S(2)}) copy-start(bf16[2,256,768]{2,1,0:T(8,128)(2,1)} %get-tuple-element.39) | copy-start | bytes 2359300
  76.3 11.5 %collective-permute-start.5 = (bf16[256,768]{1,0:T(8,128)(2,1)}, bf16[256,768]{1,0:T(8,128)(2,1)S(1)}, u32[]{:S(2)}, u32[]{:S(2)}) collective-permute-start(bf16[256,768]{1,0:T(8,128)(2,1)} %dynamic-slice_bitcast_fusion.4), channel_id=1, source_target_pairs={{0,2},{1,3},{2,0},{3,1},{4,6},{5,7},{6,4},{7,5},{8,10},{9,11},{10,... | collective-permute-start | bytes 1179656 | tf_op jit(solution)/shard_map/ppermute | solution.py:573
  76.6 56.9 %collective-permute-start.42 = (bf16[4,4,192,256]{3,2,1,0:T(8,128)(2,1)}, bf16[4,4,192,256]{3,2,1,0:T(8,128)(2,1)S(1)}, u32[]{:S(2)}, u32[]{:S(2)}) collective-permute-start(bf16[4,4,192,256]{3,2,1,0:T(8,128)(2,1)} %get-tuple-element.58), channel_id=1, source_target_pairs={{0,1},{1,0},{2,3},{3,2},{4,5},{5,4},{6,7},{7,6},{8,9},{9,8},{10,11... | collective-permute-start | bytes 4718600 | tf_op jit(solution)/shard_map/ppermute | solution.py:573
  76.6 60.1 %collective-permute-start.37 = (bf16[4,4,96,512]{3,2,1,0:T(8,128)(2,1)}, bf16[4,4,96,512]{3,2,1,0:T(8,128)(2,1)S(1)}, u32[]{:S(2)}, u32[]{:S(2)}) collective-permute-start(bf16[4,4,96,512]{3,2,1,0:T(8,128)(2,1)} %get-tuple-element.56), channel_id=1, source_target_pairs={{0,1},{1,0},{2,3},{3,2},{4,5},{5,4},{6,7},{7,6},{8,9},{9,8},{10,11... | collective-permute-start | bytes 4718600 | tf_op jit(solution)/shard_map/ppermute | solution.py:573
  77.1 68.6 %collective-permute-start.32 = (bf16[4,4,96,512]{3,2,1,0:T(8,128)(2,1)}, bf16[4,4,96,512]{3,2,1,0:T(8,128)(2,1)S(1)}, u32[]{:S(2)}, u32[]{:S(2)}) collective-permute-start(bf16[4,4,96,512]{3,2,1,0:T(8,128)(2,1)} %get-tuple-element.54), channel_id=1, source_target_pairs={{0,1},{1,0},{2,3},{3,2},{4,5},{5,4},{6,7},{7,6},{8,9},{9,8},{10,11... | collective-permute-start | bytes 4718600 | tf_op jit(solution)/shard_map/ppermute | solution.py:573
  77.1 0.9 copy-start.6
  82.0 6.8 %copy-start.14 = (bf16[2,2,96,384]{3,2,1,0:T(8,128)(2,1)S(1)}, bf16[2,2,96,384]{3,2,1,0:T(8,128)(2,1)}, u32[]{:S(2)}) copy-start(bf16[2,2,96,384]{3,2,1,0:T(8,128)(2,1)} %get-tuple-element.51) | copy-start | bytes 884740
  82.0 6.8 %collective-permute-start.27 = (bf16[2,2,96,384]{3,2,1,0:T(8,128)(2,1)}, bf16[2,2,96,384]{3,2,1,0:T(8,128)(2,1)S(1)}, u32[]{:S(2)}, u32[]{:S(2)}) collective-permute-start(bf16[2,2,96,384]{3,2,1,0:T(8,128)(2,1)} %get-tuple-element.52), channel_id=1, source_target_pairs={{0,1},{1,0},{2,3},{3,2},{4,5},{5,4},{6,7},{7,6},{8,9},{9,8},{10,11... | collective-permute-start | bytes 884744 | tf_op jit(solution)/shard_map/ppermute | solution.py:573
  89.0 33.2 %collective-permute-start.28 = (bf16[2,2,96,384]{3,2,1,0:T(8,128)(2,1)S(1)}, bf16[2,2,96,384]{3,2,1,0:T(8,128)(2,1)S(1)}, u32[]{:S(2)}, u32[]{:S(2)}) collective-permute-start(bf16[2,2,96,384]{3,2,1,0:T(8,128)(2,1)S(1)} %dynamic-slice_bitcast_fusion.9), channel_id=1, source_target_pairs={{0,2},{1,3},{2,0},{3,1},{4,6},{5,7},{6,4},{7,5},{8,10},{9,11},{10,... | collective-permute-start | bytes 884744 | tf_op jit(solution)/shard_map/ppermute | solution.py:573
  122.2 53.1 %collective-permute-start.14 = (bf16[3,4,96,384]{3,2,1,0:T(8,128)(2,1)}, bf16[3,4,96,384]{3,2,1,0:T(8,128)(2,1)}, u32[]{:S(2)}, u32[]{:S(2)}) collective-permute-start(bf16[3,4,96,384]{3,2,1,0:T(8,128)(2,1)} %get-tuple-element.50), channel_id=1, source_target_pairs={{0,1},{1,0},{2,3},{3,2},{4,5},{5,4},{6,7},{7,6},{8,9},{9,8},{10,11... | collective-permute-start | bytes 2654216 | tf_op jit(solution)/shard_map/ppermute | solution.py:573
  122.4 10.5 %collective-permute-start.29 = (bf16[2,96,384]{2,1,0:T(8,128)(2,1)S(1)}, bf16[2,96,384]{2,1,0:T(8,128)(2,1)S(1)}, u32[]{:S(2)}, u32[]{:S(2)}) collective-permute-start(bf16[2,96,384]{2,1,0:T(8,128)(2,1)S(1)} %dynamic-slice_bitcast_fusion.15), channel_id=1, source_target_pairs={{0,4},{1,5},{2,6},{3,7},{4,0},{5,1},{6,2},{7,3},{8,12},{9,13},{10,... | collective-permute-start | bytes 442376 | tf_op jit(solution)/shard_map/ppermute | solution.py:573
  125.2 10.0 %copy-start.4 = (bf16[4,4,192,256]{3,2,1,0:T(8,128)(2,1)S(1)}, bf16[4,4,192,256]{3,2,1,0:T(8,128)(2,1)}, u32[]{:S(2)}) copy-start(bf16[4,4,192,256]{3,2,1,0:T(8,128)(2,1)} %get-tuple-element.57) | copy-start | bytes 4718596
  132.8 6.5 %collective-permute-start.7 = (bf16[2,256,768]{2,1,0:T(8,128)(2,1)}, bf16[2,256,768]{2,1,0:T(8,128)(2,1)S(1)}, u32[]{:S(2)}, u32[]{:S(2)}) collective-permute-start(bf16[2,256,768]{2,1,0:T(8,128)(2,1)} %get-tuple-element.43), channel_id=1, source_target_pairs={{0,1},{1,0},{2,3},{3,2},{4,5},{5,4},{6,7},{7,6},{8,9},{9,8},{10,11... | collective-permute-start | bytes 2359304 | tf_op jit(solution)/shard_map/ppermute | solution.py:573
  133.5 30.8 %collective-permute-start.30 = (bf16[96,384]{1,0:T(8,128)(2,1)}, bf16[96,384]{1,0:T(8,128)(2,1)}, u32[]{:S(2)}, u32[]{:S(2)}) collective-permute-start(bf16[96,384]{1,0:T(8,128)(2,1)} %dynamic-slice_bitcast_fusion.22), channel_id=1, source_target_pairs={{0,16},{8,24},{16,0},{24,8},{1,17},{9,25},{17,1},{25,9},{2,18},{10... | collective-permute-start | bytes 221192 | tf_op jit(solution)/shard_map/ppermute | solution.py:573
  135.7 2.0 copy-start.3
  136.7 92.2 %collective-permute-start.43 = (bf16[2,2,2,192,256]{4,3,0,1,2:T(8,128)(2,1)}, bf16[2,2,2,192,256]{4,3,0,1,2:T(8,128)(2,1)}, u32[]{:S(2)}, u32[]{:S(2)}) collective-permute-start(bf16[2,2,2,192,256]{4,3,0,1,2:T(8,128)(2,1)} %bitcast.192), channel_id=1, source_target_pairs={{0,2},{1,3},{2,0},{3,1},{4,6},{5,7},{6,4},{7,5},{8,10},{9,11},{10,... | collective-permute-start | bytes 2359304 | tf_op jit(solution)/shard_map/ppermute | solution.py:573
  139.3 91.9 %collective-permute-start.38 = (bf16[2,2,2,96,512]{4,3,0,1,2:T(8,128)(2,1)}, bf16[2,2,2,96,512]{4,3,0,1,2:T(8,128)(2,1)}, u32[]{:S(2)}, u32[]{:S(2)}) collective-permute-start(bf16[2,2,2,96,512]{4,3,0,1,2:T(8,128)(2,1)} %bitcast.193), channel_id=1, source_target_pairs={{0,16},{8,24},{16,0},{24,8},{1,17},{9,25},{17,1},{25,9},{2,18},{10... | collective-permute-start | bytes 2359304 | tf_op jit(solution)/shard_map/ppermute | solution.py:573
  140.2 4.9 %copy-start.15 = (f32[1,768]{1,0:T(1,128)S(1)}, f32[1,768]{1,0:T(1,128)}, u32[]{:S(2)}) copy-start(f32[1,768]{1,0:T(1,128)} %get-tuple-element.47) | copy-start | bytes 9220
  140.2 5.6 %copy-start.2 = (bf16[4,4,96,512]{3,2,1,0:T(8,128)(2,1)S(1)}, bf16[4,4,96,512]{3,2,1,0:T(8,128)(2,1)}, u32[]{:S(2)}) copy-start(bf16[4,4,96,512]{3,2,1,0:T(8,128)(2,1)} %get-tuple-element.53) | copy-start | bytes 4718596
  145.8 1.2 collective-permute-start.9
  145.9 1.1 copy-start.16
  147.0 12.1 %collective-permute-start.10 = (f32[2,768]{1,0:T(2,128)S(1)}, f32[2,768]{1,0:T(2,128)S(1)}, u32[]{:S(2)}, u32[]{:S(2)}) collective-permute-start(f32[2,768]{1,0:T(2,128)S(1)} %fusion.28), channel_id=1, source_target_pairs={{0,16},{8,24},{16,0},{24,8},{1,17},{9,25},{17,1},{25,9},{2,18},{10... | collective-permute-start | bytes 18440 | tf_op jit(solution)/shard_map/ppermute | solution.py:573
  148.2 12.5 %copy-start.9 = (bf16[2,256,768]{2,1,0:T(8,128)(2,1)S(1)}, bf16[2,256,768]{2,1,0:T(8,128)(2,1)}, u32[]{:S(2)}) copy-start(bf16[2,256,768]{2,1,0:T(8,128)(2,1)} %get-tuple-element.45) | copy-start | bytes 2359300
  159.1 3.7 %collective-permute-start.11 = (f32[2,768]{1,0:T(2,128)S(1)}, f32[2,768]{1,0:T(2,128)S(1)}, u32[]{:S(2)}, u32[]{:S(2)}) collective-permute-start(f32[2,768]{1,0:T(2,128)S(1)} %fusion.29), channel_id=1, source_target_pairs={{0,8},{8,0},{16,24},{24,16},{1,9},{9,1},{17,25},{25,17},{2,10},{10... | collective-permute-start | bytes 18440 | tf_op jit(solution)/shard_map/ppermute | solution.py:573
  160.7 15.2 %copy-start.5 = (bf16[3,4,96,384]{3,2,1,0:T(8,128)(2,1)S(1)}, bf16[3,4,96,384]{3,2,1,0:T(8,128)(2,1)}, u32[]{:S(2)}) copy-start(bf16[3,4,96,384]{3,2,1,0:T(8,128)(2,1)} %get-tuple-element.49) | copy-start | bytes 2654212
  162.8 71.0 %collective-permute-start.33 = (bf16[2,2,2,96,512]{4,3,0,1,2:T(8,128)(2,1)}, bf16[2,2,2,96,512]{4,3,0,1,2:T(8,128)(2,1)}, u32[]{:S(2)}, u32[]{:S(2)}) collective-permute-start(bf16[2,2,2,96,512]{4,3,0,1,2:T(8,128)(2,1)} %bitcast.194), channel_id=1, source_target_pairs={{0,8},{8,0},{16,24},{24,16},{1,9},{9,1},{17,25},{25,17},{2,10},{10... | collective-permute-start | bytes 2359304 | tf_op jit(solution)/shard_map/ppermute | solution.py:573
  164.3 5.7 %collective-permute-start.12 = (f32[2,768]{1,0:T(2,128)S(1)}, f32[2,768]{1,0:T(2,128)S(1)}, u32[]{:S(2)}, u32[]{:S(2)}) collective-permute-start(f32[2,768]{1,0:T(2,128)S(1)} %add.223), channel_id=1, source_target_pairs={{0,4},{1,5},{2,6},{3,7},{4,0},{5,1},{6,2},{7,3},{8,12},{9,13},{10,... | collective-permute-start | bytes 18440 | tf_op jit(solution)/shard_map/ppermute | solution.py:573
  170.0 3.7 %collective-permute-start.13 = (f32[2,768]{1,0:T(2,128)S(1)}, f32[2,768]{1,0:T(2,128)S(1)}, u32[]{:S(2)}, u32[]{:S(2)}) collective-permute-start(f32[2,768]{1,0:T(2,128)S(1)} %add.224), channel_id=1, source_target_pairs={{0,2},{1,3},{2,0},{3,1},{4,6},{5,7},{6,4},{7,5},{8,10},{9,11},{10,... | collective-permute-start | bytes 18440 | tf_op jit(solution)/shard_map/ppermute | solution.py:573
  173.7 23.2 %collective-permute-start.8 = (bf16[256,768]{1,0:T(8,128)(2,1)}, bf16[256,768]{1,0:T(8,128)(2,1)S(1)}, u32[]{:S(2)}, u32[]{:S(2)}) collective-permute-start(bf16[256,768]{1,0:T(8,128)(2,1)} %dynamic-slice_bitcast_fusion.3), channel_id=1, source_target_pairs={{0,2},{1,3},{2,0},{3,1},{4,6},{5,7},{6,4},{7,5},{8,10},{9,11},{10,... | collective-permute-start | bytes 1179656 | tf_op jit(solution)/shard_map/ppermute | solution.py:573
  175.4 6.7 %collective-permute-start.31 = (bf16[96,192]{1,0:T(8,128)(2,1)S(1)}, bf16[96,192]{1,0:T(8,128)(2,1)S(1)}, u32[]{:S(2)}, u32[]{:S(2)}) collective-permute-start(bf16[96,192]{1,0:T(8,128)(2,1)S(1)} %bitcast.218), channel_id=1, source_target_pairs={{0,8},{8,0},{16,24},{24,16},{1,9},{9,1},{17,25},{25,17},{2,10},{10... | collective-permute-start | bytes 110600 | tf_op jit(solution)/shard_map/ppermute | solution.py:573
  182.0 7.5 %collective-permute-start.23 = (bf16[2,2,96,384]{3,2,0,1:T(8,128)(2,1)S(1)}, bf16[2,2,96,384]{3,2,0,1:T(8,128)(2,1)S(1)}, u32[]{:S(2)}, u32[]{:S(2)}) collective-permute-start(bf16[2,2,96,384]{3,2,0,1:T(8,128)(2,1)S(1)} %dynamic-slice_bitcast_fusion.10), channel_id=1, source_target_pairs={{0,2},{1,3},{2,0},{3,1},{4,6},{5,7},{6,4},{7,5},{8,10},{9,11},{10,... | collective-permute-start | bytes 884744 | tf_op jit(solution)/shard_map/ppermute | solution.py:573
  183.8 14.7 %copy-start.10 = (bf16[2,256,768]{2,1,0:T(8,128)(2,1)S(1)}, bf16[2,256,768]{2,1,0:T(8,128)(2,1)}, u32[]{:S(2)}) copy-start(bf16[2,256,768]{2,1,0:T(8,128)(2,1)} %get-tuple-element.45) | copy-start | bytes 2359300
  189.5 6.7 %collective-permute-start.19 = (bf16[2,2,96,384]{3,2,0,1:T(8,128)(2,1)S(1)}, bf16[2,2,96,384]{3,2,0,1:T(8,128)(2,1)S(1)}, u32[]{:S(2)}, u32[]{:S(2)}) collective-permute-start(bf16[2,2,96,384]{3,2,0,1:T(8,128)(2,1)S(1)} %dynamic-slice_bitcast_fusion.11), channel_id=1, source_target_pairs={{0,2},{1,3},{2,0},{3,1},{4,6},{5,7},{6,4},{7,5},{8,10},{9,11},{10,... | collective-permute-start | bytes 884744 | tf_op jit(solution)/shard_map/ppermute | solution.py:573
  196.3 8.3 %collective-permute-start.15 = (bf16[2,2,96,384]{3,2,0,1:T(8,128)(2,1)S(1)}, bf16[2,2,96,384]{3,2,0,1:T(8,128)(2,1)S(1)}, u32[]{:S(2)}, u32[]{:S(2)}) collective-permute-start(bf16[2,2,96,384]{3,2,0,1:T(8,128)(2,1)S(1)} %bitcast.216), channel_id=1, source_target_pairs={{0,16},{8,24},{16,0},{24,8},{1,17},{9,25},{17,1},{25,9},{2,18},{10... | collective-permute-start | bytes 884744 | tf_op jit(solution)/shard_map/ppermute | solution.py:573
  196.9 9.3 %collective-permute-start.24 = (bf16[2,96,384]{2,1,0:T(8,128)(2,1)S(1)}, bf16[2,96,384]{2,1,0:T(8,128)(2,1)S(1)}, u32[]{:S(2)}, u32[]{:S(2)}) collective-permute-start(bf16[2,96,384]{2,1,0:T(8,128)(2,1)S(1)} %dynamic-slice_bitcast_fusion.16), channel_id=1, source_target_pairs={{0,16},{8,24},{16,0},{24,8},{1,17},{9,25},{17,1},{25,9},{2,18},{10... | collective-permute-start | bytes 442376 | tf_op jit(solution)/shard_map/ppermute | solution.py:573
  204.6 5.1 %collective-permute-start.20 = (bf16[2,96,384]{2,1,0:T(8,128)(2,1)S(1)}, bf16[2,96,384]{2,1,0:T(8,128)(2,1)S(1)}, u32[]{:S(2)}, u32[]{:S(2)}) collective-permute-start(bf16[2,96,384]{2,1,0:T(8,128)(2,1)S(1)} %dynamic-slice_bitcast_fusion.17), channel_id=1, source_target_pairs={{0,16},{8,24},{16,0},{24,8},{1,17},{9,25},{17,1},{25,9},{2,18},{10... | collective-permute-start | bytes 442376 | tf_op jit(solution)/shard_map/ppermute | solution.py:573
  206.1 6.5 %collective-permute-start.16 = (bf16[2,96,384]{2,1,0:T(8,128)(2,1)S(1)}, bf16[2,96,384]{2,1,0:T(8,128)(2,1)S(1)}, u32[]{:S(2)}, u32[]{:S(2)}) collective-permute-start(bf16[2,96,384]{2,1,0:T(8,128)(2,1)S(1)} %dynamic-slice_bitcast_fusion.18), channel_id=1, source_target_pairs={{0,2},{1,3},{2,0},{3,1},{4,6},{5,7},{6,4},{7,5},{8,10},{9,11},{10,... | collective-permute-start | bytes 442376 | tf_op jit(solution)/shard_map/ppermute | solution.py:573
  209.7 6.2 %collective-permute-start.25 = (bf16[96,384]{1,0:T(8,128)(2,1)S(1)}, bf16[96,384]{1,0:T(8,128)(2,1)S(1)}, u32[]{:S(2)}, u32[]{:S(2)}) collective-permute-start(bf16[96,384]{1,0:T(8,128)(2,1)S(1)} %dynamic-slice_bitcast_fusion.23), channel_id=1, source_target_pairs={{0,4},{1,5},{2,6},{3,7},{4,0},{5,1},{6,2},{7,3},{8,12},{9,13},{10,... | collective-permute-start | bytes 221192 | tf_op jit(solution)/shard_map/ppermute | solution.py:573
  212.7 6.0 %collective-permute-start.21 = (bf16[96,384]{1,0:T(8,128)(2,1)S(1)}, bf16[96,384]{1,0:T(8,128)(2,1)S(1)}, u32[]{:S(2)}, u32[]{:S(2)}) collective-permute-start(bf16[96,384]{1,0:T(8,128)(2,1)S(1)} %dynamic-slice_bitcast_fusion.24), channel_id=1, source_target_pairs={{0,4},{1,5},{2,6},{3,7},{4,0},{5,1},{6,2},{7,3},{8,12},{9,13},{10,... | collective-permute-start | bytes 221192 | tf_op jit(solution)/shard_map/ppermute | solution.py:573
  215.9 6.0 %collective-permute-start.17 = (bf16[96,384]{1,0:T(8,128)(2,1)S(1)}, bf16[96,384]{1,0:T(8,128)(2,1)S(1)}, u32[]{:S(2)}, u32[]{:S(2)}) collective-permute-start(bf16[96,384]{1,0:T(8,128)(2,1)S(1)} %dynamic-slice_bitcast_fusion.25), channel_id=1, source_target_pairs={{0,4},{1,5},{2,6},{3,7},{4,0},{5,1},{6,2},{7,3},{8,12},{9,13},{10,... | collective-permute-start | bytes 221192 | tf_op jit(solution)/shard_map/ppermute | solution.py:573
  218.7 4.8 %collective-permute-start.26 = (bf16[96,192]{1,0:T(8,128)(2,1)S(1)}, bf16[96,192]{1,0:T(8,128)(2,1)S(1)}, u32[]{:S(2)}, u32[]{:S(2)}) collective-permute-start(bf16[96,192]{1,0:T(8,128)(2,1)S(1)} %bitcast.217), channel_id=1, source_target_pairs={{0,8},{8,0},{16,24},{24,16},{1,9},{9,1},{17,25},{25,17},{2,10},{10... | collective-permute-start | bytes 110600 | tf_op jit(solution)/shard_map/ppermute | solution.py:573
  221.9 4.7 %collective-permute-start.22 = (bf16[96,192]{1,0:T(8,128)(2,1)S(1)}, bf16[96,192]{1,0:T(8,128)(2,1)S(1)}, u32[]{:S(2)}, u32[]{:S(2)}) collective-permute-start(bf16[96,192]{1,0:T(8,128)(2,1)S(1)} %bitcast.219), channel_id=1, source_target_pairs={{0,8},{8,0},{16,24},{24,16},{1,9},{9,1},{17,25},{25,17},{2,10},{10... | collective-permute-start | bytes 110600 | tf_op jit(solution)/shard_map/ppermute | solution.py:573
  223.5 4.7 %collective-permute-start.18 = (bf16[96,192]{1,0:T(8,128)(2,1)S(1)}, bf16[96,192]{1,0:T(8,128)(2,1)S(1)}, u32[]{:S(2)}, u32[]{:S(2)}) collective-permute-start(bf16[96,192]{1,0:T(8,128)(2,1)S(1)} %bitcast.220), channel_id=1, source_target_pairs={{0,8},{8,0},{16,24},{24,16},{1,9},{9,1},{17,25},{25,17},{2,10},{10... | collective-permute-start | bytes 110600 | tf_op jit(solution)/shard_map/ppermute | solution.py:573
  230.3 7.8 %collective-permute-start.44 = (bf16[2,2,192,256]{3,2,0,1:T(8,128)(2,1)S(1)}, bf16[2,2,192,256]{3,2,0,1:T(8,128)(2,1)S(1)}, u32[]{:S(2)}, u32[]{:S(2)}) collective-permute-start(bf16[2,2,192,256]{3,2,0,1:T(8,128)(2,1)S(1)} %dynamic-slice_bitcast_fusion), channel_id=1, source_target_pairs={{0,8},{8,0},{16,24},{24,16},{1,9},{9,1},{17,25},{25,17},{2,10},{10... | collective-permute-start | bytes 1179656 | tf_op jit(solution)/shard_map/ppermute | solution.py:573
  232.6 9.7 %collective-permute-start.39 = (bf16[2,2,96,512]{3,2,0,1:T(8,128)(2,1)S(1)}, bf16[2,2,96,512]{3,2,0,1:T(8,128)(2,1)S(1)}, u32[]{:S(2)}, u32[]{:S(2)}) collective-permute-start(bf16[2,2,96,512]{3,2,0,1:T(8,128)(2,1)S(1)} %dynamic-slice_bitcast_fusion.1), channel_id=1, source_target_pairs={{0,8},{8,0},{16,24},{24,16},{1,9},{9,1},{17,25},{25,17},{2,10},{10... | collective-permute-start | bytes 1179656 | tf_op jit(solution)/shard_map/ppermute | solution.py:573
  235.2 8.3 %collective-permute-start.34 = (bf16[2,2,96,512]{3,2,0,1:T(8,128)(2,1)S(1)}, bf16[2,2,96,512]{3,2,0,1:T(8,128)(2,1)S(1)}, u32[]{:S(2)}, u32[]{:S(2)}) collective-permute-start(bf16[2,2,96,512]{3,2,0,1:T(8,128)(2,1)S(1)} %dynamic-slice_bitcast_fusion.2), channel_id=1, source_target_pairs={{0,16},{8,24},{16,0},{24,8},{1,17},{9,25},{17,1},{25,9},{2,18},{10... | collective-permute-start | bytes 1179656 | tf_op jit(solution)/shard_map/ppermute | solution.py:573
  238.2 6.9 %collective-permute-start.45 = (bf16[2,192,256]{2,1,0:T(8,128)(2,1)S(1)}, bf16[2,192,256]{2,1,0:T(8,128)(2,1)S(1)}, u32[]{:S(2)}, u32[]{:S(2)}) collective-permute-start(bf16[2,192,256]{2,1,0:T(8,128)(2,1)S(1)} %dynamic-slice_bitcast_fusion.12), channel_id=1, source_target_pairs={{0,16},{8,24},{16,0},{24,8},{1,17},{9,25},{17,1},{25,9},{2,18},{10... | collective-permute-start | bytes 589832 | tf_op jit(solution)/shard_map/ppermute | solution.py:573
  242.5 5.7 %collective-permute-start.40 = (bf16[2,96,512]{2,1,0:T(8,128)(2,1)S(1)}, bf16[2,96,512]{2,1,0:T(8,128)(2,1)S(1)}, u32[]{:S(2)}, u32[]{:S(2)}) collective-permute-start(bf16[2,96,512]{2,1,0:T(8,128)(2,1)S(1)} %dynamic-slice_bitcast_fusion.13), channel_id=1, source_target_pairs={{0,2},{1,3},{2,0},{3,1},{4,6},{5,7},{6,4},{7,5},{8,10},{9,11},{10,... | collective-permute-start | bytes 589832 | tf_op jit(solution)/shard_map/ppermute | solution.py:573
  243.7 7.7 %collective-permute-start.35 = (bf16[2,96,512]{2,1,0:T(8,128)(2,1)S(1)}, bf16[2,96,512]{2,1,0:T(8,128)(2,1)S(1)}, u32[]{:S(2)}, u32[]{:S(2)}) collective-permute-start(bf16[2,96,512]{2,1,0:T(8,128)(2,1)S(1)} %dynamic-slice_bitcast_fusion.14), channel_id=1, source_target_pairs={{0,2},{1,3},{2,0},{3,1},{4,6},{5,7},{6,4},{7,5},{8,10},{9,11},{10,... | collective-permute-start | bytes 589832 | tf_op jit(solution)/shard_map/ppermute | solution.py:573
  245.2 6.8 %collective-permute-start.46 = (bf16[192,256]{1,0:T(8,128)(2,1)S(1)}, bf16[192,256]{1,0:T(8,128)(2,1)S(1)}, u32[]{:S(2)}, u32[]{:S(2)}) collective-permute-start(bf16[192,256]{1,0:T(8,128)(2,1)S(1)} %dynamic-slice_bitcast_fusion.19), channel_id=1, source_target_pairs={{0,4},{1,5},{2,6},{3,7},{4,0},{5,1},{6,2},{7,3},{8,12},{9,13},{10,... | collective-permute-start | bytes 294920 | tf_op jit(solution)/shard_map/ppermute | solution.py:573
  248.3 6.6 %collective-permute-start.41 = (bf16[96,512]{1,0:T(8,128)(2,1)S(1)}, bf16[96,512]{1,0:T(8,128)(2,1)S(1)}, u32[]{:S(2)}, u32[]{:S(2)}) collective-permute-start(bf16[96,512]{1,0:T(8,128)(2,1)S(1)} %dynamic-slice_bitcast_fusion.20), channel_id=1, source_target_pairs={{0,4},{1,5},{2,6},{3,7},{4,0},{5,1},{6,2},{7,3},{8,12},{9,13},{10,... | collective-permute-start | bytes 294920 | tf_op jit(solution)/shard_map/ppermute | solution.py:573
  251.4 6.6 %collective-permute-start.36 = (bf16[96,512]{1,0:T(8,128)(2,1)S(1)}, bf16[96,512]{1,0:T(8,128)(2,1)S(1)}, u32[]{:S(2)}, u32[]{:S(2)}) collective-permute-start(bf16[96,512]{1,0:T(8,128)(2,1)S(1)} %dynamic-slice_bitcast_fusion.21), channel_id=1, source_target_pairs={{0,4},{1,5},{2,6},{3,7},{4,0},{5,1},{6,2},{7,3},{8,12},{9,13},{10,... | collective-permute-start | bytes 294920 | tf_op jit(solution)/shard_map/ppermute | solution.py:573
  (4 other events, 3.2 us)

commit v2 on v1

v2 whole, which is shorter than its diff:
```python
import functools
import math

import jax
import jax.numpy as jnp
import numpy as np
from jax import lax
from jax.experimental import pallas as pl
from jax.experimental.pallas import tpu as pltpu
from jax.sharding import PartitionSpec as P

HEADS = 12
HEAD_FEATURES = 64
MAXLEN = 1024
GROUP = 4
PIECE = MAXLEN // GROUP
PAIR = 2 * HEAD_FEATURES
LOG2E = math.log2(math.e)

epsilon = 1e-06
masked_score = -1e30
f32 = jnp.float32
bf16 = jnp.bfloat16
MIB = 1024 * 1024

CORE, CHIP, LENGTH, OTHER_CHIP, OWN_B, OWN_Z = range(6)


def mm(a, b):
    return lax.dot_general(a, b, (((1,), (0,)), ((), ())), preferred_element_type=f32)


def mm_nt(a, b):
    return lax.dot_general(a, b, (((1,), (1,)), ((), ())), preferred_element_type=f32)


def mm_tn(a, b):
    return lax.dot_general(a, b, (((0,), (0,)), ((), ())), preferred_element_type=f32)


def call(body, grid, in_specs, out_specs, out_shape, scratch=(), aliases=None, vmem=56):
    return pl.pallas_call(
        body,
        grid_spec=pltpu.PrefetchScalarGridSpec(
            num_scalar_prefetch=1,
            grid=grid,
            in_specs=in_specs,
            out_specs=out_specs,
            scratch_shapes=list(scratch),
        ),
        out_shape=out_shape,
        input_output_aliases=aliases or {},
        compiler_params=pltpu.CompilerParams(
            dimension_semantics=("arbitrary",) * len(grid), vmem_limit_bytes=vmem * MIB
        ),
        cost_estimate=pl.CostEstimate(flops=1000, bytes_accessed=1000, transcendentals=0),
    )


def whole(shape):
    return pl.BlockSpec(shape, lambda *a: (0,) * len(shape))


def sds(shape, dtype):
    return jax.ShapeDtypeStruct(shape, dtype)


def rope_tables():
    middle = HEAD_FEATURES // 2
    frequency = 10000.0 ** (-np.arange(middle, dtype=np.float64) * 2.0 / HEAD_FEATURES)
    angles = np.arange(MAXLEN, dtype=np.float64)[:, None] * frequency[None, :]
    cosine, sine = np.cos(angles), np.sin(angles)
    none = np.zeros_like(sine)
    table = np.stack(
        [
            np.concatenate([cosine, cosine] * 2, axis=1),
            np.concatenate([-sine, none] * 2, axis=1),
            np.concatenate([none, sine] * 2, axis=1),
        ]
    )
    return table.astype(np.float32)


def rotate(u, table, sign):
    up = pltpu.roll(u, PAIR - HEAD_FEATURES // 2, 1)
    down = pltpu.roll(u, HEAD_FEATURES // 2, 1)
    if sign > 0:
        return u * table[0] + (up * table[1] + down * table[2])
    return u * table[0] - (up * table[1] + down * table[2])


def slots(start):
    return start + lax.broadcasted_iota(jnp.int32, (PIECE, 1), 0)


def piece_rows(half, place):
    return pl.ds(pl.multiple_of(half * 2 * PIECE + place * PIECE, PIECE), PIECE)


def project_body(s, own, part, gain, wq, wk, wv, table, *rest):
    qkv, normed, copy = rest[-3:]
    low_x = jnp.where(pl.program_id(0) == s[CORE], own[0], part[0])
    copy[...] = low_x
    x = low_x.astype(f32)
    r = lax.rsqrt(jnp.mean(x * x, axis=-1, keepdims=True) + epsilon)
    low = (x * r * gain[...].astype(f32)).astype(bf16)
    normed[...] = low
    width = wq.shape[1]
    for m, w in enumerate((wq, wk, wv)):
        u = mm(low, w[...])
        if m == 0:
            u = u * (1.0 / math.sqrt(HEAD_FEATURES))
        for p in range(width // PAIR):
            v = u[:, p * PAIR : (p + 1) * PAIR]
            if m < 2:
                v = rotate(v, table, 1)
            at = m * width + p * PAIR
            qkv[:, at : at + PAIR] = v.astype(bf16)


def project(scalars, own, part, half, gain, weights, table, filled):
    width = weights[0].shape[0]
    cols = width // 2
    place = lambda t, s: (s[half] * 2 + t, 0)
    source = lambda a: pl.BlockSpec((1, PIECE, width), lambda t, s: (s[CHIP] if a.shape[0] > 1 else 0, 0, 0))
    weight_spec = pl.BlockSpec((width, cols), lambda t, s: (0, s[CORE]))
    in_specs = [
        source(own),
        source(part),
        whole((1, width)),
        weight_spec,
        weight_spec,
        weight_spec,
        pl.BlockSpec((3, PIECE, PAIR), lambda t, s: (0, s[half] * 2 + t, 0)),
    ]
    args = [scalars, own, part, gain, *weights, table]
    aliases = None
    if filled is not None:
        in_specs += [pl.BlockSpec(memory_space=pl.ANY)] * 3
        aliases = {len(args) + a: a for a in range(3)}
        args += list(filled)
    return call(
        project_body,
        (2,),
        in_specs,
        [pl.BlockSpec((PIECE, 3 * cols), place), pl.BlockSpec((PIECE, width), place), pl.BlockSpec((PIECE, width), place)],
        [sds((MAXLEN, 3 * cols), bf16), sds((MAXLEN, width), bf16), sds((MAXLEN, width), bf16)],
        aliases=aliases,
    )(*args)


def head_mask(h):
    lane = lax.broadcasted_iota(jnp.int32, (1, PAIR), 1)
    return lane < HEAD_FEATURES if h == 0 else lane >= HEAD_FEATURES


def attend_body(s, q, k, v, out, lse):
    row = lax.broadcasted_iota(jnp.int32, (PIECE, PIECE), 0)
    col = lax.broadcasted_iota(jnp.int32, (PIECE, PIECE), 1)
    lane = lax.broadcasted_iota(jnp.int32, (PIECE, PAIR), 1)
    ones = jnp.ones((MAXLEN, PAIR), bf16)

    def score(b, h):
        at = b * PIECE
        qh = jnp.where(head_mask(h), q[at : at + PIECE, :], jnp.zeros((), bf16))
        near = mm_nt(qh, k[at : at + PIECE, :])
        return near, mm_nt(qh, k[:at, :]) if b else None

    def mix(b, near, far):
        at = b * PIECE
        near = jnp.where(row >= col, near, masked_score)
        top = jnp.max(near, axis=-1, keepdims=True)
        if b:
            top = jnp.maximum(top, jnp.max(far, axis=-1, keepdims=True))
        shift = top * LOG2E
        near = jnp.exp2(near * LOG2E - shift).astype(bf16)
        mixed = mm(near, jnp.concatenate([v[at : at + PIECE, :], ones[:PIECE]], axis=1))
        if b:
            far = jnp.exp2(far * LOG2E - shift).astype(bf16)
            mixed = mixed + mm(far, jnp.concatenate([v[:at, :], ones[:at]], axis=1))
        total = mixed[:, PAIR:]
        return mixed[:, :PAIR] * (1.0 / total), top + jnp.log(total)

    units = [(b, h) for b in range(GROUP) for h in range(2)]
    ahead = score(*units[0])
    done = []
    for at, (b, h) in enumerate(units):
        now = ahead
        if at + 1 < len(units):
            ahead = score(*units[at + 1])
        done.append(mix(b, *now))
        if h == 1:
            rows = slice(b * PIECE, (b + 1) * PIECE)
            (left, left_log), (right, right_log) = done
            done = []
            joined = jnp.where(head_mask(0), left, right)
            out[rows, :] = jnp.where(slots(b * PIECE) < s[LENGTH], joined, 0.0).astype(bf16)
            lse[0, rows, :] = jnp.where(lane == 0, left_log, right_log)


def attend(scalars, qkv):
    pairs = qkv.shape[1] // 3 // PAIR
    spec = lambda m: pl.BlockSpec((MAXLEN, PAIR), lambda p, s, m=m: (0, m * pairs + p))
    return call(
        attend_body,
        (pairs,),
        [spec(0), spec(1), spec(2)],
        [pl.BlockSpec((MAXLEN, PAIR), lambda p, s: (0, p)), pl.BlockSpec((1, MAXLEN, PAIR), lambda p, s: (p, 0, 0))],
        [sds((MAXLEN, pairs * PAIR), bf16), sds((pairs, MAXLEN, PAIR), f32)],
    )(scalars, qkv, qkv, qkv)


def attend_back_body(
    n_seq, s, q, k, v, o, lse, hidden, dyb, dn_mine, dn_theirs, gain, wo, wq, wk, wv, normed, table, *rest
):
    (qkv_keep, qkv_send, out_keep, out_send, norm_keep, norm_send, dh_own, second) = rest[:8]
    dhb, dh, da, da_t, q_t, dk_t, dv_t, dq, grads, out_grad, dn = rest[8:]
    core = s[CORE]
    p = pl.program_id(0)
    width = normed.shape[1]
    zero = jnp.zeros((), bf16)

    @pl.when(p == 0)
    def _():
        scale = gain[...].astype(f32)
        sums = jnp.zeros((1, width), f32)
        for t in range(GROUP):
            rows = slice(t * PIECE, (t + 1) * PIECE)
            h = hidden[rows, :]
            r = lax.rsqrt(jnp.mean(h * h, axis=-1, keepdims=True) + epsilon)
            g = dn_mine[rows, :].astype(f32) + dn_theirs[rows, :].astype(f32)
            sums = sums + jnp.sum(g * h * r, axis=0, keepdims=True)
            scaled = g * scale
            inner = jnp.mean(scaled * h, axis=-1, keepdims=True)
            d = dyb[rows, :].astype(f32) + r * scaled - h * (r * r * r) * inner
            dh[rows, :] = d
            dhb[rows, :] = d.astype(bf16)
        second[...] = sums * 0.5
        for half in range(2):
            dh_own[half] = dh[piece_rows(half, core), :]

    for t in range(GROUP):
        rows = slice(t * PIECE, (t + 1) * PIECE)
        d = mm_nt(dhb[rows, :], wo[...])
        da[rows, :] = jnp.where(slots(t * PIECE) < s[LENGTH], d, 0.0).astype(bf16)
    out_grad[pl.ds(pl.multiple_of(p * PAIR, PAIR), PAIR), :] = mm_tn(o[...], dhb[...])
    da_t[...] = jnp.transpose(da[...])
    q_t[...] = jnp.transpose(q[...])

    row = lax.broadcasted_iota(jnp.int32, (PIECE, PIECE), 0)
    col = lax.broadcasted_iota(jnp.int32, (PIECE, PIECE), 1)

    def score(a, h):
        at = a * PIECE
        mask = head_mask(h)
        qh = jnp.where(mask, q[at : at + PIECE, :], zero)
        gh = jnp.where(mask, da[at : at + PIECE, :], zero)
        near = mm_nt(qh, k[at : at + PIECE, :]), mm_nt(gh, v[at : at + PIECE, :])
        far = (mm_nt(qh, k[:at, :]), mm_nt(gh, v[:at, :])) if a else None
        return near, far

    def back(a, h, near, far):
        at = a * PIECE
        rows = slice(at, at + PIECE)
        feats = slice(h * HEAD_FEATURES, (h + 1) * HEAD_FEATURES)
        mask = head_mask(h)
        shift = lse[0, rows, h : h + 1] * LOG2E
        product = da[rows, :].astype(f32) * o[rows, :].astype(f32)
        inner = jnp.sum(jnp.where(mask, product, 0.0), axis=-1, keepdims=True)
        near_prob = jnp.exp2(jnp.where(row >= col, near[0] * LOG2E - shift, masked_score))
        near_ds = (near_prob * (near[1] - inner)).astype(bf16)
        query_grad = mm(near_ds, jnp.where(mask, k[rows, :], zero))
        parts = [(rows, near_prob.astype(bf16), near_ds)]
        if a:
            far_prob = jnp.exp2(far[0] * LOG2E - shift)
            far_ds = (far_prob * (far[1] - inner)).astype(bf16)
            query_grad = query_grad + mm(far_ds, jnp.where(mask, k[:at, :], zero))
            parts.append((slice(0, at), far_prob.astype(bf16), far_ds))
        for cols, prob, ds in parts:
            value_grad = mm(da_t[feats, rows], prob)
            key_grad = mm(q_t[feats, rows], ds)
            if a == GROUP - 1:
                dv_t[feats, cols] = value_grad
                dk_t[feats, cols] = key_grad
            else:
                dv_t[feats, cols] += value_grad
                dk_t[feats, cols] += key_grad
        return query_grad

    units = [(a, h) for a in reversed(range(GROUP)) for h in range(2)]
    ahead = score(*units[0])
    held = None
    for at, (a, h) in enumerate(units):
        now = ahead
        if at + 1 < len(units):
            ahead = score(*units[at + 1])
        g = back(a, h, *now)
        if h == 0:
            held = g
        else:
            dq[a * PIECE : (a + 1) * PIECE, :] = held + g

    d = jnp.concatenate(
        [
            rotate(dq[...] * (1.0 / math.sqrt(HEAD_FEATURES)), table, -1).astype(bf16),
            rotate(jnp.transpose(dk_t[...]), table, -1).astype(bf16),
            jnp.transpose(dv_t[...].astype(bf16)),
        ],
        axis=1,
    )
    grads[p] = mm_tn(normed[...], d)
    w = jnp.concatenate([wq[...], wk[...], wv[...]], axis=1)
    step = mm_nt(d, w)

    @pl.when(p == 0)
    def _():
        dn[...] = step

    @pl.when(p > 0)
    def _():
        dn[...] += step

    rows = width // n_seq
    pairs = grads.shape[0]

    @pl.when(p == pairs - 1)
    def _():
        for half in range(2):
            norm_keep[half] = dn[piece_rows(half, core), :]
            norm_send[half] = dn[piece_rows(half, 1 - core), :].astype(bf16)
        if rows % 16:
            for m in range(3):
                qkv_keep[m] = jnp.concatenate(
                    [grads[b, :, m * PAIR : (m + 1) * PAIR] for b in range(pairs)], axis=1
                ).astype(bf16)
            out_keep[...] = out_grad[...].astype(bf16)
            return
        half_row, column = rows // 2, pairs * PAIR // 2

        def packed(block, at):
            lanes = slice(at, at + column)
            return jnp.concatenate([block[:half_row, lanes], block[half_row:, lanes]], axis=1).astype(bf16)

        for target_qkv, target_out, place in ((qkv_keep, out_keep, core), (qkv_send, out_send, 1 - core)):
            for z in range(n_seq // 2):
                at = pl.ds(pl.multiple_of((2 * z + place) * rows, 8), rows)
                for m in range(3):
                    block = jnp.concatenate(
                        [grads[b, at, m * PAIR : (m + 1) * PAIR] for b in range(pairs)], axis=1
                    )
                    for x in range(2):
                        target_qkv[z, x, m] = packed(block, x * column)
            for z in range(n_seq // 4):
                at = pl.ds(pl.multiple_of((2 * z + place) * rows, 8), rows)
                block = out_grad[at, :]
                for b in range(4):
                    target_out[z, b // 2, b % 2] = packed(block, b * column)


def attend_back(scalars, qkv, attn, lse, hidden, dyb, dn_mine, dn_theirs, gain, wo, weights, normed, table, n_seq):
    heads = attn.shape[1]
    pairs = heads // PAIR
    width = wo.shape[1]
    rows = width // n_seq
    spec = lambda m: pl.BlockSpec((MAXLEN, PAIR), lambda p, s, m=m: (0, m * pairs + p))
    weight_spec = pl.BlockSpec((width, PAIR), lambda p, s: (0, s[CORE] * pairs + p))
    if rows % 16 == 0:
        shapes = [(n_seq // 2, 2, 3, rows // 2, heads)] * 2 + [(n_seq // 4, 2, 2, rows // 2, heads)] * 2
    else:
        shapes = [(3, width, heads), (8, 128), (heads, width), (8, 128)]
    token_shape = (2, PIECE, width)
    return call(
        functools.partial(attend_back_body, n_seq),
        (pairs,),
        [
            spec(0),
            spec(1),
            spec(2),
            spec(0),
            pl.BlockSpec((1, MAXLEN, PAIR), lambda p, s: (p, 0, 0)),
            whole((MAXLEN, width)),
            whole((MAXLEN, width)),
            whole((MAXLEN, width)),
            whole((MAXLEN, width)),
            whole((1, width)),
            pl.BlockSpec((PAIR, width), lambda p, s: (s[CORE] * pairs + p, 0)),
            weight_spec,
            weight_spec,
            weight_spec,
            whole((MAXLEN, width)),
            whole((3, MAXLEN, PAIR)),
        ],
        [whole(a) for a in shapes] + [whole(token_shape)] * 3 + [whole((1, width))],
        [sds(a, bf16) for a in shapes]
        + [sds(token_shape, f32), sds(token_shape, bf16), sds(token_shape, f32), sds((1, width), f32)],
        scratch=[
            pltpu.VMEM((MAXLEN, width), bf16),
            pltpu.VMEM((MAXLEN, width), f32),
            pltpu.VMEM((MAXLEN, PAIR), bf16),
            pltpu.VMEM((PAIR, MAXLEN), bf16),
            pltpu.VMEM((PAIR, MAXLEN), bf16),
            pltpu.VMEM((PAIR, MAXLEN), f32),
            pltpu.VMEM((PAIR, MAXLEN), f32),
            pltpu.VMEM((MAXLEN, PAIR), f32),
            pltpu.VMEM((pairs, width, 3 * PAIR), f32),
            pltpu.VMEM((heads, width), f32),
            pltpu.VMEM((MAXLEN, width), f32),
        ],
    )(scalars, qkv, qkv, qkv, attn, lse, hidden, dyb, dn_mine, dn_theirs, gain, wo, *weights, normed, table)


def unit_block(step, s):
    return 2 * ((3 - step) ^ s[OWN_B]) + s[CORE]


def feed_body(
    packed, s, x, dy_mine, dy_mine_pair, dy_far, dy_far_pair, attn, attn_pair, wo_own, wo_pair, gain, wg, wu, wd, *rest
):
    (hidden, dyb, acts, dgs, dus, gate_send, gate_keep, up_send, up_keep, down_send, down_keep) = rest[:11]
    low, low_t, dyb_t, total = rest[11:]
    core = s[CORE]
    step = pl.program_id(0)
    width = x.shape[1]

    @pl.when(step == 0)
    def _():
        scale = gain[...].astype(f32)
        for source, half, place in (
            (dy_mine, s[CHIP], core),
            (dy_mine_pair, s[CHIP], 1 - core),
            (dy_far, s[OTHER_CHIP], core),
            (dy_far_pair, s[OTHER_CHIP], 1 - core),
        ):
            live = slots(half * 2 * PIECE + place * PIECE) < s[LENGTH]
            dyb[piece_rows(half, place), :] = jnp.where(live, source[0], jnp.zeros((), bf16))
        for t in range(GROUP):
            rows = slice(t * PIECE, (t + 1) * PIECE)
            h = x[rows, :].astype(f32) + mm(attn[rows, :], wo_own[0]) + mm(attn_pair[rows, :], wo_pair[0])
            hidden[rows, :] = h
            r = lax.rsqrt(jnp.mean(h * h, axis=-1, keepdims=True) + epsilon)
            low[rows, :] = (h * r * scale).astype(bf16)
        low_t[...] = jnp.transpose(low[...])
        dyb_t[...] = jnp.transpose(dyb[...])

    def products(t):
        rows = slice(t * PIECE, (t + 1) * PIECE)
        return mm(low[rows, :], wg[...]), mm(low[rows, :], wu[...]), mm_nt(dyb[rows, :], wd[...])

    def pointwise(t, gate, up, dact):
        rows = slice(t * PIECE, (t + 1) * PIECE)
        sig = 1.0 / (1.0 + jnp.exp2(gate * -LOG2E))
        silu = gate * sig
        acts[rows, :] = (silu * up).astype(bf16)
        dgs[rows, :] = (dact * up * (sig + silu * (1.0 - sig))).astype(bf16)
        dus[rows, :] = (dact * silu).astype(bf16)

    ahead = products(0)
    for t in range(GROUP):
        now = ahead
        if t + 1 < GROUP:
            ahead = products(t + 1)
        pointwise(t, *now)

    gate_grad = mm(low_t[...], dgs[...])
    up_grad = mm(low_t[...], dus[...])
    down_grad = mm(dyb_t[...], acts[...])
    if not packed:
        gate_keep[...] = gate_grad.astype(bf16)
        up_keep[...] = up_grad.astype(bf16)
        down_keep[...] = down_grad.astype(bf16)
        return

    def emit(grad, targets, own):
        total[...] = grad
        blocks = targets[0][1].shape[1]
        rows = width // blocks
        values = [
            total[pl.ds(pl.multiple_of((b ^ own) * rows, 16), rows), :].astype(bf16) for b in range(blocks)
        ]
        for when, target, index in targets:

            @pl.when(when)
            def _():
                for b in range(blocks):
                    target[index, b] = values[b]

    emit(gate_grad, [(step % 2 == 0, gate_send, 0), (step % 2 == 1, gate_keep, 0)], s[OWN_Z])
    emit(up_grad, [(step < 2, up_send, 0), (step >= 2, up_keep, 0)], s[OWN_Z])
    z = (unit_block(step, s) // 2) ^ s[OWN_Z]
    emit(down_grad, [(z % 2 == 1, down_send, z // 2), (z % 2 == 0, down_keep, z // 2)], s[OWN_B])


def feed(scalars, x, dy, dy_pair, dy_far, dy_far_pair, attn, attn_pair, wo, gain, wg, wu, wd, packed):
    tokens, width = x.shape
    heads = attn.shape[1]
    steps = 4
    cols = wg.shape[1] // 2 // steps
    piece = lambda which: pl.BlockSpec((1, PIECE, width), lambda f, s: (which(s), 0, 0))
    if packed:
        rows = width // 4
        shape = (2, 4, rows, cols)
        side = lambda index: pl.BlockSpec((1, 4, rows, cols), lambda f, s: (index(f), 0, 0, 0))
        late = lambda f: 1 - f // 2
        specs = [
            side(late),
            side(late),
            side(lambda f: 1 - jnp.minimum(f, 1)),
            side(lambda f: 1 - jnp.maximum(f - 2, 0)),
            whole(shape),
            whole(shape),
        ]
        shapes = [shape] * 6
    else:
        unused = pl.BlockSpec((8, 128), lambda f, s: (0, 0))
        plain = pl.BlockSpec((width, cols), lambda f, s: (0, unit_block(f, s) // 2))
        specs = [unused, plain] * 3
        shapes = [(8, 128), (width, steps * cols)] * 3
    wo_parts = wo.reshape(2, heads, width)
    return call(
        functools.partial(feed_body, packed),
        (steps,),
        [
            whole((tokens, width)),
            piece(lambda s: s[CHIP]),
            piece(lambda s: s[CHIP]),
            piece(lambda s: 0),
            piece(lambda s: 0),
            whole((tokens, heads)),
            whole((tokens, heads)),
            pl.BlockSpec((1, heads, width), lambda f, s: (s[CORE], 0, 0)),
            pl.BlockSpec((1, heads, width), lambda f, s: (1 - s[CORE], 0, 0)),
            whole((1, width)),
            pl.BlockSpec((width, cols), lambda f, s: (0, unit_block(f, s))),
            pl.BlockSpec((width, cols), lambda f, s: (0, unit_block(f, s))),
            pl.BlockSpec((cols, width), lambda f, s: (unit_block(f, s), 0)),
        ],
        [whole((tokens, width))] * 2 + [pl.BlockSpec((tokens, cols), lambda f, s: (0, f))] * 3 + specs,
        [sds((tokens, width), f32), sds((tokens, width), bf16)]
        + [sds((tokens, steps * cols), bf16)] * 3
        + [sds(a, bf16) for a in shapes],
        scratch=[
            pltpu.VMEM((tokens, width), bf16),
            pltpu.VMEM((width, tokens), bf16),
            pltpu.VMEM((width, tokens), bf16),
            pltpu.VMEM((width, cols), f32),
        ],
    )(scalars, x, dy, dy_pair, dy_far, dy_far_pair, attn, attn_pair, wo_parts, wo_parts, gain, wg, wu, wd)


def settle_body(s, acts, dgs, dus, wg, wu, wd, dn, down_keep, down_send, down, back):
    f = pl.program_id(0)
    for t in range(GROUP):
        rows = slice(t * PIECE, (t + 1) * PIECE)
        a = mm(acts[rows, :], wd[...])
        b = mm_nt(dgs[rows, :], wg[...]) + mm_nt(dus[rows, :], wu[...])

        @pl.when(f == 0)
        def _():
            down[rows, :] = a
            back[rows, :] = b

        @pl.when(f > 0)
        def _():
            down[rows, :] += a
            back[rows, :] += b

    @pl.when(f == pl.num_programs(0) - 1)
    def _():
        dn[...] = back[...].astype(bf16)
        for half in range(2):
            down_keep[half] = down[piece_rows(half, s[CORE]), :]
            down_send[half] = down[piece_rows(half, 1 - s[CORE]), :].astype(bf16)


def settle(scalars, acts, dgs, dus, wg, wu, wd):
    tokens, units = acts.shape
    width = wg.shape[0]
    steps = 4
    cols = units // steps
    unit_spec = pl.BlockSpec((tokens, cols), lambda f, s: (0, f))
    token_shape = (2, PIECE, width)
    return call(
        settle_body,
        (steps,),
        [
            unit_spec,
            unit_spec,
            unit_spec,
            pl.BlockSpec((width, cols), lambda f, s: (0, unit_block(f, s))),
            pl.BlockSpec((width, cols), lambda f, s: (0, unit_block(f, s))),
            pl.BlockSpec((cols, width), lambda f, s: (unit_block(f, s), 0)),
        ],
        [whole((tokens, width)), whole(token_shape), whole(token_shape)],
        [sds((tokens, width), bf16), sds(token_shape, f32), sds(token_shape, bf16)],
        scratch=[pltpu.VMEM((tokens, width), f32)] * 2,
    )(scalars, acts, dgs, dus, wg, wu, wd)


def finish_body(s, x, keep, recv, dh, gain, stay, leave, first):
    scale = gain[...].astype(f32)
    sums = jnp.zeros((1, x.shape[-1]), f32)
    for out, half in ((leave, s[OTHER_CHIP]), (stay, s[CHIP])):
        h = x[half, 0].astype(f32)
        dn = keep[half] + recv[half].astype(f32)
        r = lax.rsqrt(jnp.mean(h * h, axis=-1, keepdims=True) + epsilon)
        sums = sums + jnp.sum(dn * h * r, axis=0, keepdims=True)
        scaled = dn * scale
        inner = jnp.mean(scaled * h, axis=-1, keepdims=True)
        out[...] = (dh[half] + r * scaled - h * (r * r * r) * inner).astype(bf16)
    first[...] = sums


def finish(scalars, x, keep, recv, dh, gain):
    width = x.shape[1]
    shape = (2, PIECE, width)
    return call(
        finish_body,
        (1,),
        [
            pl.BlockSpec((2, 1, PIECE, width), lambda f, s: (0, s[CORE], 0, 0)),
            whole(shape),
            whole(shape),
            whole(shape),
            whole((1, width)),
        ],
        [whole((PIECE, width)), whole((PIECE, width)), whole((1, width))],
        [sds((PIECE, width), bf16), sds((PIECE, width), bf16), sds((1, width), f32)],
    )(scalars, x.reshape(2, 2, PIECE, width), keep, recv, dh, gain)


def exchange(block, axis, bit):
    count = lax.axis_size(axis)
    return lax.ppermute(block, axis, [(a, a ^ (1 << bit)) for a in range(count)])


def pick(block, index, dim):
    return lax.dynamic_index_in_dim(block, index, dim, keepdims=False)


def together(*values):
    return lax.optimization_barrier(values)


X, Y, Z0, Z1 = ("batch", 0), ("batch", 1), ("seq", 1), ("seq", 2)


class Reduction:
    def __init__(self, names, keep, send, first):
        self.names, self.keep, self.send, self.bit = list(names), keep, send, first

    @staticmethod
    def of(names, array, first):
        r = Reduction(names, None, None, first)
        r.keep, r.send = r.split(array, first)
        return r

    def split(self, array, bit):
        dim = self.names.index(bit)
        self.names = self.names[:dim] + self.names[dim + 1 :]
        return lax.index_in_dim(array, 0, dim, False), lax.index_in_dim(array, 1, dim, False)

    def go(self):
        self.arrived = exchange(self.send, *self.bit)
        return self

    def take(self, bit):
        self.bit = bit
        kept, sent = self.split(self.keep, bit) if False else (None, None)
        dim = self.names.index(bit)
        parts = []
        for index in range(2):
            a = lax.index_in_dim(self.keep, index, dim, False).astype(f32)
            b = lax.index_in_dim(self.arrived, index, dim, False).astype(f32)
            parts.append((a + b).astype(bf16))
        self.names = self.names[:dim] + self.names[dim + 1 :]
        self.keep, self.send = parts
        return self

    def total(self):
        return self.keep.astype(f32) + self.arrived.astype(f32)


def body(
    states,
    lengths,
    first_gain,
    query_weight,
    key_weight,
    value_weight,
    output_weight,
    second_gain,
    gate_weight,
    up_weight,
    down_weight,
    cotangent,
):
    tokens, width = states.shape
    n_seq, n_batch = lax.axis_size("seq"), lax.axis_size("batch")
    packed = n_seq == 8 and n_batch == 4
    place = lax.axis_index("seq")
    batch = lax.axis_index("batch")
    core = place & 1
    chip = place >> 1 & 1
    sequence = (batch * (n_seq // GROUP) + place // GROUP) * 2 + chip
    length = pick(lengths, sequence, 0)
    own_b, own_z = batch & 3, place >> 1 & 3
    scalars = jnp.stack([core, chip, length, 1 - chip, own_b, own_z]).astype(jnp.int32)
    table = jnp.asarray(rope_tables())
    gain_first = first_gain.reshape(1, width)
    gain_second = second_gain.reshape(1, width)
    weights = (query_weight, key_weight, value_weight)

    held = states.reshape(2, PIECE, width)
    held_back = cotangent.reshape(2, PIECE, width)
    far = exchange(pick(held, 1 - chip, 0), *Z0)[None]
    held_pair = exchange(held, "seq", 0)
    filled = project(scalars, held, held_pair, CHIP, gain_first, weights, table, None)
    far, *filled = together(far, *filled)
    far_pair = exchange(far, "seq", 0)
    leaving, far_pair = together(pick(held_back, 1 - chip, 0), far_pair)
    back_far = exchange(leaving, *Z0)[None]
    back_pair = exchange(held_back, "seq", 0)
    qkv, normed, x = project(scalars, far, far_pair, OTHER_CHIP, gain_first, weights, table, filled)
    attn, lse = attend(scalars, qkv)
    attn_pair = exchange(attn, "seq", 0)
    back_far, attn = together(back_far, attn)
    back_far_pair = exchange(back_far, "seq", 0)
    hidden, dyb, acts, dgs, dus, gate_send, gate_keep, up_send, up_keep, down_send, down_keep = feed(
        scalars,
        x,
        held_back,
        back_pair,
        back_far,
        back_far_pair,
        attn,
        attn_pair,
        output_weight,
        gain_second,
        gate_weight,
        up_weight,
        down_weight,
        packed,
    )
    if packed:
        two = lambda a: a.reshape((a.shape[0], 2, 2) + a.shape[2:])
        gate = Reduction([Y, Z1, Z0], two(gate_keep), two(gate_send), X).go()
        up = Reduction([X, Z1, Z0], two(up_keep), two(up_send), Y).go()
        down = Reduction([Z1, Y, X], two(down_keep), two(down_send), Z0).go()

    dn, layer_keep, layer_send = settle(scalars, acts, dgs, dus, gate_weight, up_weight, down_weight)
    dn_pair = exchange(dn, "seq", 0)
    layer_arrived = exchange(layer_send, "seq", 0)

    (
        qkv_keep,
        qkv_send,
        out_keep,
        out_send,
        norm_keep,
        norm_send,
        dh,
        second,
    ) = attend_back(
        scalars,
        qkv,
        attn,
        lse,
        hidden,
        dyb,
        dn,
        dn_pair,
        gain_second,
        output_weight,
        weights,
        normed,
        table,
        n_seq,
    )
    norm_arrived = exchange(norm_send, "seq", 0)

    at = lambda half: (
        pick(pick(hidden.reshape(2, 2, PIECE, width), core, 1), half, 0)
        + pick(layer_keep, half, 0)
        + pick(layer_arrived, half, 0).astype(f32)
    )
    own_slots = lambda half: half * 2 * PIECE + core * PIECE + jnp.arange(PIECE, dtype=jnp.int32)[:, None]
    layer_half = lambda half: jnp.where(own_slots(half) < length, at(half), 0.0).astype(bf16)

    def in_order(kept, arrived):
        return jnp.concatenate(
            [jnp.where(chip == 0, kept, arrived), jnp.where(chip == 0, arrived, kept)], axis=0
        )

    if packed:
        qkv_arrived = exchange(qkv_send, "seq", 0)
        out_arrived = exchange(out_send, "seq", 0)
        gate.take(Y).go()
        up.take(Z0).go()
        down.take(X).go()
        rows = width // n_seq // 2
        first_half = lambda a, b: (jnp.where(core == 0, a, b), jnp.where(core == 0, b, a))
        joined = jnp.concatenate(
            [
                jnp.stack(first_half(qkv_keep, qkv_arrived), axis=1),
                jnp.concatenate(first_half(out_keep, out_arrived), axis=0)[:, :, :, None],
            ],
            axis=3,
        )
        joined = joined.reshape(2, 2, 2, 2, 4 * rows, joined.shape[-1])
        names = [Z1, Z0, Y, X]
        flags = [own_z >> 1 & 1, own_z & 1, own_b >> 1 & 1, own_b & 1]
        flows = []
        for index, bit in enumerate((X, Y, Z0)):
            step = 4 * rows // 3
            part = joined[..., index * step : (index + 1) * step, :]
            flows.append(start_flow(names, flags, part, bit))
        orders = [(Y, Z0, Z1), (Z0, X, Z1), (X, Y, Z1)]
        gate.take(Z0).go()
        up.take(X).go()
        down.take(Y).go()
        for level in range(3):
            for flow, order in zip(flows, orders):
                flow.take_absolute(order[level], flags_of(names, flags)).go()
            if level == 0:
                for r in (gate, up, down):
                    r.take(Z1).go()
        sums = jnp.concatenate([flow.total() for flow in flows], axis=0).reshape(4, rows, -1)
        half = sums.shape[-1] // 2
        sums = jnp.concatenate([sums[..., :half], sums[..., half:]], axis=1)
        shards = [sums[m] for m in range(4)]
        sides = jnp.stack([gate.total(), up.total()])
        sides = sides.reshape(2, 2, sides.shape[1] // 2, sides.shape[2])
        side_keep, side_send = pick(sides, core, 1), pick(sides, 1 - core, 1).astype(bf16)
        side_arrived = exchange(side_send, "seq", 0).astype(f32)
        sides = jnp.concatenate(first_half(side_keep, side_arrived), axis=2)
        gate_grad, up_grad, down_grad = sides[0], sides[1], jnp.transpose(down.total())
    else:
        units = gate_keep.shape[1]
        zeros = lambda shape: jnp.zeros(shape, bf16)
        blocks = 4

        def spread(array):
            parts = array.reshape(width, blocks, 1, units // blocks)
            full = zeros((width, blocks, 2, units // blocks))
            return lax.dynamic_update_slice_in_dim(full, parts, core, 2).reshape(width, 2 * units)

        heads = attn.shape[1]
        columns = lambda a: lax.dynamic_update_slice_in_dim(zeros((width, width)), a, core * heads, 1)
        full = [columns(qkv_keep[m]) for m in range(3)]
        full.append(lax.dynamic_update_slice_in_dim(zeros((width, width)), out_keep, core * heads, 0))
        full += [spread(gate_keep), spread(up_keep), jnp.transpose(spread(down_keep))]
        full = [lax.psum_scatter(a.astype(f32), "seq", scatter_dimension=0, tiled=True) for a in full]
        full = [lax.psum_scatter(a, "batch", scatter_dimension=1, tiled=True) for a in full]
        shards, (gate_grad, up_grad, down_grad) = full[:4], full[4:]

    stay, leave, first = finish(scalars, x, norm_keep, norm_arrived, dh, gain_first)
    input_grad = in_order(stay, exchange(leave, *Z0))
    layer_out = in_order(layer_half(chip), exchange(layer_half(1 - chip), *Z0))

    gains = jnp.concatenate([first, second], axis=0)
    for axis in ("seq", "batch"):
        for bit in range(int(math.log2(lax.axis_size(axis)))):
            gains = gains + exchange(gains, axis, bit)

    return (
        layer_out,
        input_grad,
        gains[0],
        shards[0],
        shards[1],
        shards[2],
        shards[3],
        gains[1],
        gate_grad,
        up_grad,
        down_grad,
    )


def flags_of(names, flags):
    return dict(zip(names, flags))


class Flow:
    def __init__(self, names, flags, array, bit):
        self.names, self.flags, self.bit = list(names), dict(zip(names, flags)), bit
        dim = self.names.index(bit)
        own = self.flags[bit]
        self.keep, self.send = pick(array, own, dim), pick(array, 1 - own, dim)
        self.names.remove(bit)

    def go(self):
        self.arrived = exchange(self.send, *self.bit)
        return self

    def take_absolute(self, bit, _):
        dim = self.names.index(bit)
        own = self.flags[bit]
        pair = []
        for index in (own, 1 - own):
            a, b = pick(self.keep, index, dim), pick(self.arrived, index, dim)
            pair.append((a.astype(f32) + b.astype(f32)).astype(bf16))
        self.keep, self.send = pair
        self.names.remove(bit)
        self.bit = bit
        return self

    def total(self):
        return self.keep.astype(f32) + self.arrived.astype(f32)


def start_flow(names, flags, array, bit):
    return Flow(names, flags, array, bit).go()


def solution(mesh):
    split = P(("batch", "seq"), None)
    in_specs = (split,) + (P(),) * 10 + (split,)
    shard = P("seq", "batch")
    out_specs = (split, split, P(), shard, shard, shard, shard, P(), shard, shard, shard)
    return jax.shard_map(body, mesh=mesh, in_specs=in_specs, out_specs=out_specs, check_vma=False)
```

time: 259 us -> 216 us (0.83)
  waiting for transfers between devices: 73.7 us -> 55.2 us
  starting transfers between devices: 47.9 us -> 37.7 us
  other arithmetic: 22.5 us -> 13.7 us
  local copies, waits for them, and re-layouts: 16.6 us -> 12.4 us
    ppermute x47 -> x44, waiting for transfers between devices: 73.7 us -> 55.2 us  [exchange(): return lax.ppermute(block, axis, [(a, a ^ 1 << bit) for a in range(count)])]
    ppermute x47 -> x44, starting transfers between devices: 47.9 us -> 37.7 us  [exchange(): return lax.ppermute(block, axis, [(a, a ^ 1 << bit) for a in range(count)])]
    squeeze x25 -> x5, local copies, waits for them, and re-layouts: 5.91 us -> 1.18 us  [pick(): return lax.dynamic_index_in_dim(block, index, dim, keepdims=False)]
    pallas_call x1, Pallas kernels: 12.3 us -> 9.13 us  [attend(): call(attend_body, (pairs,), [spec(0), spec(1), spec(2)], [pl.BlockSpec((M...]
    convert_element_type x24 -> x23, other arithmetic: 8.2 us -> 5.08 us  [the longest x10 4.36 us: take(): parts.append((a + b).astype(bf16))]
    dynamic_slice x9 -> x1, local copies, waits for them, and re-layouts: 3.94 us -> 1.24 us  [pick(): return lax.dynamic_index_in_dim(block, index, dim, keepdims=False)]
    another operation x3 -> x1, other arithmetic: 2.77 us -> 0.17 us  [body(): jnp.stack(first_half(qkv_keep, qkv_arrived), axis=1)]
    pallas_call x6 -> x4, Pallas kernels: 74 us -> 75 us  [the longest x1 32.1 us: attend_back(): call(functools.partial(attend_back_body, n_seq), (pairs,), [spec(0), spec...]
  transfers between devices with their start and end apart: 47 -> 44, of which waited for: 26 -> 21; matrix products, arithmetic and copies ran while one was open for 13% -> 9% of each run, Pallas kernels for 28% -> 34%
where the time goes in v2:
time: 216 us; the launch traced here: 215 us
  Pallas kernels  95 us (44%)
  waiting for transfers between devices  55.2 us (26%)
  starting transfers between devices  37.7 us (17%)
  other arithmetic  13.7 us (6%)
  local copies, waits for them, and re-layouts  12.4 us (6%)
    ppermute x44, waiting for transfers between devices, exchange(): return lax.ppermute(block, axis, [(a, a ^ 1 << bit) for a in range(count)])  55.2 us
    ppermute x44, starting transfers between devices, exchange(): return lax.ppermute(block, axis, [(a, a ^ 1 << bit) for a in range(count)])  37.7 us
    pallas_call x1, Pallas kernels, attend_back(): call(functools.partial(attend_back_body, n_seq), (pairs,), [spec(0), spec...  32.1 us
    pallas_call x1, Pallas kernels, feed(): call(functools.partial(feed_body, packed), (steps,), [whole((tokens, widt...  21.9 us
    pallas_call x1, Pallas kernels, settle(): call(settle_body, (steps,), [unit_spec, unit_spec, unit_spec, pl.BlockSpe...  16.3 us
    pallas_call x2, Pallas kernels, project(): call(project_body, (2,), in_specs, [pl.BlockSpec((PIECE, 3 * cols), place...  10.9 us
    pallas_call x1, Pallas kernels, attend(): call(attend_body, (pairs,), [spec(0), spec(1), spec(2)], [pl.BlockSpec((M...  9.13 us
    pallas_call x1, Pallas kernels, finish(): call(finish_body, (1,), [pl.BlockSpec((2, 1, PIECE, width), lambda f, s:...  4.68 us
  transfers between devices with their start and end apart: 44, of which 21 were waited for; matrix products, arithmetic and copies ran while one was open for 9% of the time, Pallas kernels for 34%

profile of v2, /device:TPU:0, one launch (start us, length us, event | category | flops | bytes accessed | tf_op | source)
XLA Modules:
  0.0 215.1 jit_solution(608229967527017657)
XLA Ops:
  1.2 1.0 dynamic-slice_bitcast_fusion.2
  2.2 2.7 %collective-permute-start = (bf16[256,768]{1,0:T(8,128)(2,1)S(1)}, bf16[256,768]{1,0:T(8,128)(2,1)S(1)}, u32[]{:S(2)}, u32[]{:S(2)}) collective-permute-start(bf16[256,768]{1,0:T(8,128)(2,1)S(1)} %dynamic-slice_bitcast_fusion.2), channel_id=1, source_target_pairs={{0,2},{1,3},{2,0},{3,1},{4,6},{5,7},{6,4},{7,5},{8,10},{9,11},{10,... | collective-permute-start | bytes 1179656 | tf_op jit(solution)/shard_map/ppermute | solution.py:633
  4.8 1.3 reshape.309.gain
  6.1 1.2 dynamic_slice.167
  7.3 1.2 stack.42.s
  8.6 0.9 copy-done.11
  9.5 5.5 %shard_map.212 = (bf16[1024,1152]{1,0:T(8,128)(2,1)}, bf16[1024,768]{1,0:T(8,128)(2,1)}, bf16[1024,768]{1,0:T(8,128)(2,1)}) custom-call(s32[6]{0:T(128)} %stack.42.s, bf16[2,256,768]{2,1,0:T(8,128)(2,1)} %bitcast.301, bf16[2,256,768]{2,1,0:T(8,128)(2,1)} %copy-done.11, bf16[1,768]{1,0:T(2,128)(2,1)} %reshape.309.gain, bf16[768,768]{1,0:T(8,128)(2,1)} %wq.5, ...), custom_call_target="tpu_custom_call" | custom-call | flops 1000 | bytes 1000 | tf_op jit(solution)/shard_map/pallas_call | solution.py:142
  15.6 1.2 collective-permute-done.2.part
  16.8 1.3 collective-permute-start.4
  18.1 5.4 %shard_map.213 = (bf16[1024,1152]{1,0:T(8,128)(2,1)}, bf16[1024,768]{1,0:T(8,128)(2,1)}, bf16[1024,768]{1,0:T(8,128)(2,1)}) custom-call(s32[6]{0:T(128)} %stack.42.s, bf16[1,256,768]{2,1,0:T(8,128)(2,1)} %bitcast.311, bf16[1,256,768]{2,1,0:T(8,128)(2,1)} %copy-done.14, ...), custom_call_target="tpu_custom_call", output_to_operand_aliasing={{0}: (8, {}), {1}: (9, {}), {2}: (10, {})} | custom-call | flops 1000 | bytes 1000 | tf_op jit(solution)/shard_map/pallas_call | solution.py:142
  23.5 9.1 %shard_map.214 = (bf16[1024,384]{1,0:T(8,128)(2,1)}, f32[3,1024,128]{2,1,0:T(8,128)}) custom-call(s32[6]{0:T(128)} %stack.42.s, bf16[1024,1152]{1,0:T(8,128)(2,1)} %get-tuple-element.62.q.k.v, bf16[1024,1152]{1,0:T(8,128)(2,1)} %get-tuple-element.62.q.k.v, bf16[1024,1152]{1,0:T(8,128)(2,1)} %get-tuple-element.62.q.k.v), custom_call_target="tpu_custom_call" | custom-call | flops 1000 | bytes 1000 | tf_op jit(solution)/shard_map/pallas_call | solution.py:204
  33.7 1.7 collective-permute-done.5.dy_far_pair
  35.5 0.7 copy-done.17
  36.5 21.9 %shard_map.215 = (f32[1024,768]{1,0:T(8,128)}, bf16[1024,768]{1,0:T(8,128)(2,1)}, bf16[1024,1024]{1,0:T(8,128)(2,1)}, bf16[1024,1024]{1,0:T(8,128)(2,1)}, bf16[1...) custom-call(s32[6]{0:T(128)} %stack.42.s, ...), custom_call_target="tpu_custom_call" | custom-call | flops 1000 | bytes 1000 | tf_op jit(solution)/shard_map/pallas_call | solution.py:519
  58.4 1.3 copy.39
  59.7 0.8 collective-permute-start.40
  60.5 1.5 collective-permute-start.31
  63.4 1.6 collective-permute-start.35
  65.0 16.3 %shard_map.216 = (bf16[1024,768]{1,0:T(8,128)(2,1)}, f32[2,256,768]{2,1,0:T(8,128)}, bf16[2,256,768]{2,1,0:T(8,128)(2,1)}) custom-call(s32[6]{0:T(128)} %stack.42.s, bf16[1024,1024]{1,0:T(8,128)(2,1)} %get-tuple-element.67.acts, bf16[1024,1024]{1,0:T(8,128)(2,1)} %get-tuple-element.68.dgs, bf16[1024,1024]{1,0:T(8,128)(2,1)} %get-tuple-element.69.dus, ...), custom_call_target="tpu_custom_call" | custom-call | flops 1000 | bytes 1000 | tf_op jit(solution)/shard_map/pallas_call | solution.py:582
  82.4 1.5 fusion.7
  85.3 1.3 fusion.9
  86.5 1.3 collective-permute-start.36
  88.0 0.8 collective-permute-start.8
  88.9 1.1 add_convert_fusion.2
  90.0 4.6 %collective-permute-done.41 = bf16[2,2,192,256]{3,2,1,0:T(8,128)(2,1)S(1)} collective-permute-done((bf16[2,2,192,256]{3,2,1,0:T(8,128)(2,1)S(1)}, bf16[2,2,192,256]{3,2,1,0:T(8,128)(2,1)S(1)}, u32[]{:S(2)}, u32[]{:S(2)}) %collective-permute-start.41) | collective-permute-done | bytes 393248 | tf_op jit(solution)/shard_map/ppermute | solution.py:633
  95.3 1.3 collective-permute-start.33
  96.6 2.0 collective-permute-done.36
  98.8 1.6 collective-permute-start.37
  100.3 6.8 %collective-permute-done.8 = bf16[256,768]{1,0:T(8,128)(2,1)S(1)} collective-permute-done((bf16[256,768]{1,0:T(8,128)(2,1)S(1)}, bf16[256,768]{1,0:T(8,128)(2,1)S(1)}, u32[]{:S(2)}, u32[]{:S(2)}) %collective-permute-start.8) | collective-permute-done | bytes 393248 | tf_op jit(solution)/shard_map/ppermute | solution.py:633
  107.4 0.9 pad_maximum_fusion.1
  108.3 2.6 %collective-permute-start.43 = (bf16[192,256]{1,0:T(8,128)(2,1)S(1)}, bf16[192,256]{1,0:T(8,128)(2,1)S(1)}, u32[]{:S(2)}, u32[]{:S(2)}) collective-permute-start(bf16[192,256]{1,0:T(8,128)(2,1)S(1)} %fusion.44), channel_id=1, source_target_pairs={{0,4},{1,5},{2,6},{3,7},{4,0},{5,1},{6,2},{7,3},{8,12},{9,13},{10,... | collective-permute-start | bytes 294920 | tf_op jit(solution)/shard_map/ppermute | solution.py:633
  111.0 1.1 copy-done.2
  112.1 32.1 %shard_map.217 = (bf16[4,2,3,48,384]{4,3,2,1,0:T(8,128)(2,1)}, bf16[4,2,3,48,384]{4,3,2,1,0:T(8,128)(2,1)}, bf16[2,2,2,48,384]{4,3,2,1,0:T(8,128)(2,1)}, bf16[2,...) custom-call(s32[6]{0:T(128)} %stack.42.s, ...), custom_call_target="tpu_custom_call" | custom-call | flops 1000 | bytes 1000 | tf_op jit(solution)/shard_map/pallas_call | solution.py:372
  144.7 2.6 %collective-permute-start.38 = (bf16[192,256]{1,0:T(8,128)(2,1)S(1)}, bf16[192,256]{1,0:T(8,128)(2,1)S(1)}, u32[]{:S(2)}, u32[]{:S(2)}) collective-permute-start(bf16[192,256]{1,0:T(8,128)(2,1)S(1)} %fusion.42), channel_id=1, source_target_pairs={{0,4},{1,5},{2,6},{3,7},{4,0},{5,1},{6,2},{7,3},{8,12},{9,13},{10,... | collective-permute-start | bytes 294920 | tf_op jit(solution)/shard_map/ppermute | solution.py:633
  147.4 7.7 %collective-permute-done.34 = bf16[192,256]{1,0:T(8,128)(2,1)S(1)} collective-permute-done((bf16[192,256]{1,0:T(8,128)(2,1)S(1)}, bf16[192,256]{1,0:T(8,128)(2,1)S(1)}, u32[]{:S(2)}, u32[]{:S(2)}) %collective-permute-start.34) | collective-permute-done | bytes 98336 | tf_op jit(solution)/shard_map/ppermute | solution.py:633
  155.1 1.7 collective-permute-done.38
  156.8 0.9 copy-done.12
  157.7 4.7 %shard_map.218 = (bf16[256,768]{1,0:T(8,128)(2,1)}, bf16[256,768]{1,0:T(8,128)(2,1)}, f32[1,768]{1,0:T(1,128)}) custom-call(s32[6]{0:T(128)} %stack.42.s, bf16[2,2,256,768]{3,2,1,0:T(8,128)(2,1)} %bitcast.286, f32[2,256,768]{2,1,0:T(8,128)} %get-tuple-element.76.keep, bf16[2,256,768]{2,1,0:T(8,128)(2,1)} %copy-done.12, f32[2,256,768]{2,1,0:T(8,128)} %get-tuple-element.78.dh, ...), custom_call_target="tpu_custom_call" | custom-call | flops 1000 | bytes 1000 | tf_op jit(solution)/shard_map/pallas_call | solution.py:616
  162.4 0.7 pad_maximum_fusion.6
  164.4 0.7 fusion.65
  165.2 0.7 fusion.29
  166.4 2.4 %collective-permute-done.13 = f32[2,768]{1,0:T(2,128)S(1)} collective-permute-done((f32[2,768]{1,0:T(2,128)S(1)}, f32[2,768]{1,0:T(2,128)S(1)}, u32[]{:S(2)}, u32[]{:S(2)}) %collective-permute-start.13) | collective-permute-done | bytes 6176 | tf_op jit(solution)/shard_map/ppermute | solution.py:633
  168.8 0.7 fusion.70
  169.6 4.5 %collective-permute-done.14 = f32[2,768]{1,0:T(2,128)S(1)} collective-permute-done((f32[2,768]{1,0:T(2,128)S(1)}, f32[2,768]{1,0:T(2,128)S(1)}, u32[]{:S(2)}, u32[]{:S(2)}) %collective-permute-start.14) | collective-permute-done | bytes 6176 | tf_op jit(solution)/shard_map/ppermute | solution.py:633
  174.1 1.5 collective-permute-start.15
  175.6 0.8 fusion.27
  176.3 1.3 collective-permute-done.15
  177.7 1.4 collective-permute-start.16
  179.2 2.1 collective-permute-done.16
  182.8 1.6 collective-permute-start.19
  184.4 1.4 collective-permute-start.23
  185.9 4.5 %collective-permute-done.11 = bf16[256,768]{1,0:T(8,128)(2,1)S(1)} collective-permute-done((bf16[256,768]{1,0:T(8,128)(2,1)S(1)}, bf16[256,768]{1,0:T(8,128)(2,1)S(1)}, u32[]{:S(2)}, u32[]{:S(2)}) %collective-permute-start.11) | collective-permute-done | bytes 393248 | tf_op jit(solution)/shard_map/ppermute | solution.py:633
  190.6 0.9 pad_maximum_fusion.2
  191.6 0.7 collective-permute-start.20
  192.3 2.0 collective-permute-done.23
  194.5 4.0 %collective-permute-done.27 = bf16[2,2,2,64,384]{4,3,1,0,2:T(8,128)(2,1)S(1)} collective-permute-done((bf16[2,2,2,64,384]{4,3,1,0,2:T(8,128)(2,1)S(1)}, bf16[2,2,2,64,384]{4,3,1,0,2:T(8,128)(2,1)S(1)}, u32[]{:S(2)}, u32[]{:S(2)}) %collective-permute-start.27) | collective-permute-done | bytes 393248 | tf_op jit(solution)/shard_map/ppermute | solution.py:633
  198.6 1.4 collective-permute-start.28
  200.8 1.3 collective-permute-start.25
  202.1 2.3 %collective-permute-done.28 = bf16[2,2,64,384]{3,2,0,1:T(8,128)(2,1)S(1)} collective-permute-done((bf16[2,2,64,384]{3,2,0,1:T(8,128)(2,1)S(1)}, bf16[2,2,64,384]{3,2,0,1:T(8,128)(2,1)S(1)}, u32[]{:S(2)}, u32[]{:S(2)}) %collective-permute-start.28) | collective-permute-done | bytes 196640 | tf_op jit(solution)/shard_map/ppermute | solution.py:633
  204.4 0.7 collective-permute-start.29
  205.6 3.0 %collective-permute-start.26 = (bf16[64,384]{1,0:T(8,128)(2,1)S(1)}, bf16[64,384]{1,0:T(8,128)(2,1)S(1)}, u32[]{:S(2)}, u32[]{:S(2)}) collective-permute-start(bf16[64,384]{1,0:T(8,128)(2,1)S(1)} %fusion.62), channel_id=1, source_target_pairs={{0,4},{1,5},{2,6},{3,7},{4,0},{5,1},{6,2},{7,3},{8,12},{9,13},{10,... | collective-permute-start | bytes 147464 | tf_op jit(solution)/shard_map/ppermute | solution.py:633
  209.2 1.3 collective-permute-done.22
  211.1 3.1 %collective-permute-done.30 = bf16[64,384]{1,0:T(8,128)(2,1)S(1)} collective-permute-done((bf16[64,384]{1,0:T(8,128)(2,1)S(1)}, bf16[64,384]{1,0:T(8,128)(2,1)S(1)}, u32[]{:S(2)}, u32[]{:S(2)}) %collective-permute-start.30) | collective-permute-done | bytes 49184 | tf_op jit(solution)/shard_map/ppermute | solution.py:633
  214.3 0.8 fusion.52
  (143 shorter events, 15.0 us)
Async XLA Ops:
  0.6 8.0 %collective-permute-start.1 = (bf16[2,256,768]{2,1,0:T(8,128)(2,1)}, bf16[2,256,768]{2,1,0:T(8,128)(2,1)S(1)}, u32[]{:S(2)}, u32[]{:S(2)}) collective-permute-start(bf16[2,256,768]{2,1,0:T(8,128)(2,1)} %bitcast.299), channel_id=1, source_target_pairs={{0,1},{1,0},{2,3},{3,2},{4,5},{5,4},{6,7},{7,6},{8,9},{9,8},{10,11... | collective-permute-start | bytes 2359304 | tf_op jit(solution)/shard_map/ppermute | solution.py:633
  2.2 12.8 %collective-permute-start = (bf16[256,768]{1,0:T(8,128)(2,1)S(1)}, bf16[256,768]{1,0:T(8,128)(2,1)S(1)}, u32[]{:S(2)}, u32[]{:S(2)}) collective-permute-start(bf16[256,768]{1,0:T(8,128)(2,1)S(1)} %dynamic-slice_bitcast_fusion.2), channel_id=1, source_target_pairs={{0,2},{1,3},{2,0},{3,1},{4,6},{5,7},{6,4},{7,5},{8,10},{9,11},{10,... | collective-permute-start | bytes 1179656 | tf_op jit(solution)/shard_map/ppermute | solution.py:633
  8.6 6.6 %copy-start.1 = (bf16[512,768]{1,0:T(8,128)(2,1)S(1)}, bf16[512,768]{1,0:T(8,128)(2,1)}, u32[]{:S(2)}) copy-start(bf16[512,768]{1,0:T(8,128)(2,1)} %param.24) | copy-start | bytes 2359300
  14.9 3.1 %copy-start.13 = (bf16[256,768]{1,0:T(8,128)(2,1)}, bf16[256,768]{1,0:T(8,128)(2,1)S(1)}, u32[]{:S(2)}) copy-start(bf16[256,768]{1,0:T(8,128)(2,1)S(1)} %collective-permute-done) | copy-start | bytes 1179652
  15.0 1.8 collective-permute-start.2
  15.2 18.5 %collective-permute-start.3 = (bf16[2,256,768]{2,1,0:T(8,128)(2,1)S(1)}, bf16[2,256,768]{2,1,0:T(8,128)(2,1)S(1)}, u32[]{:S(2)}, u32[]{:S(2)}) collective-permute-start(bf16[2,256,768]{2,1,0:T(8,128)(2,1)S(1)} %bitcast.293), channel_id=1, source_target_pairs={{0,1},{1,0},{2,3},{3,2},{4,5},{5,4},{6,7},{7,6},{8,9},{9,8},{10,11... | collective-permute-start | bytes 2359304 | tf_op jit(solution)/shard_map/ppermute | solution.py:633
  16.8 1.3 copy-start.14
  16.8 15.9 %collective-permute-start.4 = (bf16[256,768]{1,0:T(8,128)(2,1)S(1)}, bf16[256,768]{1,0:T(8,128)(2,1)S(1)}, u32[]{:S(2)}, u32[]{:S(2)}) collective-permute-start(bf16[256,768]{1,0:T(8,128)(2,1)S(1)} %dynamic-slice_bitcast_fusion.1), channel_id=1, source_target_pairs={{0,2},{1,3},{2,0},{3,1},{4,6},{5,7},{6,4},{7,5},{8,10},{9,11},{10,... | collective-permute-start | bytes 1179656 | tf_op jit(solution)/shard_map/ppermute | solution.py:633
  23.5 9.7 %copy-start.20 = (bf16[768]{0:T(1024)(128)(2,1)S(1)}, bf16[768]{0:T(1024)(128)(2,1)}, u32[]{:S(2)}) copy-start(bf16[768]{0:T(1024)(128)(2,1)} %param.20) | copy-start | bytes 4612
  32.6 2.9 %collective-permute-start.6 = (bf16[1024,384]{1,0:T(8,128)(2,1)}, bf16[1024,384]{1,0:T(8,128)(2,1)S(1)}, u32[]{:S(2)}, u32[]{:S(2)}) collective-permute-start(bf16[1024,384]{1,0:T(8,128)(2,1)} %get-tuple-element.65.attn.o), channel_id=1, source_target_pairs={{0,1},{1,0},{2,3},{3,2},{4,5},{5,4},{6,7},{7,6},{8,9},{9,8},{10,11... | collective-permute-start | bytes 2359304 | tf_op jit(solution)/shard_map/ppermute | solution.py:633
  32.6 2.8 %copy-start.16 = (bf16[256,768]{1,0:T(8,128)(2,1)}, bf16[256,768]{1,0:T(8,128)(2,1)S(1)}, u32[]{:S(2)}) copy-start(bf16[256,768]{1,0:T(8,128)(2,1)S(1)} %collective-permute-done.4) | copy-start | bytes 1179652
  32.7 2.8 %collective-permute-start.5 = (bf16[1,256,768]{2,1,0:T(8,128)(2,1)S(1)}, bf16[1,256,768]{2,1,0:T(8,128)(2,1)S(1)}, u32[]{:S(2)}, u32[]{:S(2)}) collective-permute-start(bf16[1,256,768]{2,1,0:T(8,128)(2,1)S(1)} %bitcast.312), channel_id=1, source_target_pairs={{0,1},{1,0},{2,3},{3,2},{4,5},{5,4},{6,7},{7,6},{8,9},{9,8},{10,11... | collective-permute-start | bytes 1179656 | tf_op jit(solution)/shard_map/ppermute | solution.py:633
  33.7 1.8 copy-start.5
  58.4 4.9 %copy-start.8 = (bf16[2,4,192,256]{3,2,1,0:T(8,128)(2,1)S(1)}, bf16[2,4,192,256]{3,2,1,0:T(8,128)(2,1)}, u32[]{:S(2)}) copy-start(bf16[2,4,192,256]{3,2,1,0:T(8,128)(2,1)} %get-tuple-element.90) | copy-start | bytes 2359300
  59.7 22.2 %collective-permute-start.40 = (bf16[2,2,2,192,256]{4,3,1,0,2:T(8,128)(2,1)S(1)}, bf16[2,2,2,192,256]{4,3,1,0,2:T(8,128)(2,1)}, u32[]{:S(2)}, u32[]{:S(2)}) collective-permute-start(bf16[2,2,2,192,256]{4,3,1,0,2:T(8,128)(2,1)S(1)} %copy.39), channel_id=1, source_target_pairs={{0,2},{1,3},{2,0},{3,1},{4,6},{5,7},{6,4},{7,5},{8,10},{9,11},{10,... | collective-permute-start | bytes 2359304 | tf_op jit(solution)/shard_map/ppermute | solution.py:633
  60.5 24.0 %collective-permute-start.31 = (bf16[2,2,2,192,256]{4,3,2,1,0:T(8,128)(2,1)}, bf16[2,2,2,192,256]{4,3,2,1,0:T(8,128)(2,1)S(1)}, u32[]{:S(2)}, u32[]{:S(2)}) collective-permute-start(bf16[2,2,2,192,256]{4,3,2,1,0:T(8,128)(2,1)} %bitcast.62), channel_id=1, source_target_pairs={{0,8},{8,0},{16,24},{24,16},{1,9},{9,1},{17,25},{25,17},{2,10},{10... | collective-permute-start | bytes 2359304 | tf_op jit(solution)/shard_map/ppermute | solution.py:633
  63.4 21.9 %collective-permute-start.35 = (bf16[2,2,2,192,256]{4,3,1,2,0:T(8,128)(2,1)S(1)}, bf16[2,2,2,192,256]{4,3,1,2,0:T(8,128)(2,1)}, u32[]{:S(2)}, u32[]{:S(2)}) collective-permute-start(bf16[2,2,2,192,256]{4,3,1,2,0:T(8,128)(2,1)S(1)} %copy.36), channel_id=1, source_target_pairs={{0,16},{8,24},{16,0},{24,8},{1,17},{9,25},{17,1},{25,9},{2,18},{10... | collective-permute-start | bytes 2359304 | tf_op jit(solution)/shard_map/ppermute | solution.py:633
  65.0 16.8 %copy-start.7 = (bf16[2,4,192,256]{3,2,1,0:T(8,128)(2,1)S(1)}, bf16[2,4,192,256]{3,2,1,0:T(8,128)(2,1)}, u32[]{:S(2)}) copy-start(bf16[2,4,192,256]{3,2,1,0:T(8,128)(2,1)} %get-tuple-element.87) | copy-start | bytes 2359300
  81.3 1.1 copy-start.10
  81.3 29.7 %collective-permute-start.9 = (bf16[1024,768]{1,0:T(8,128)(2,1)}, bf16[1024,768]{1,0:T(8,128)(2,1)S(1)}, u32[]{:S(2)}, u32[]{:S(2)}) collective-permute-start(bf16[1024,768]{1,0:T(8,128)(2,1)} %get-tuple-element.74.dn_mine), channel_id=1, source_target_pairs={{0,1},{1,0},{2,3},{3,2},{4,5},{5,4},{6,7},{7,6},{8,9},{9,8},{10,11... | collective-permute-start | bytes 4718600 | tf_op jit(solution)/shard_map/ppermute | solution.py:633
  81.3 6.6 %collective-permute-start.7 = (bf16[2,256,768]{2,1,0:T(8,128)(2,1)}, bf16[2,256,768]{2,1,0:T(8,128)(2,1)S(1)}, u32[]{:S(2)}, u32[]{:S(2)}) collective-permute-start(bf16[2,256,768]{2,1,0:T(8,128)(2,1)} %get-tuple-element.71), channel_id=1, source_target_pairs={{0,1},{1,0},{2,3},{3,2},{4,5},{5,4},{6,7},{7,6},{8,9},{9,8},{10,11... | collective-permute-start | bytes 2359304 | tf_op jit(solution)/shard_map/ppermute | solution.py:633
  82.4 2.8 %copy-start.9 = (bf16[2,4,192,256]{3,2,1,0:T(8,128)(2,1)S(1)}, bf16[2,4,192,256]{3,2,1,0:T(8,128)(2,1)}, u32[]{:S(2)}) copy-start(bf16[2,4,192,256]{3,2,1,0:T(8,128)(2,1)} %get-tuple-element.89) | copy-start | bytes 2359300
  82.4 5.4 %copy-start.3 = (f32[2,256,768]{2,1,0:T(8,128)S(1)}, f32[2,256,768]{2,1,0:T(8,128)}, u32[]{:S(2)}) copy-start(f32[2,256,768]{2,1,0:T(8,128)} %get-tuple-element.70) | copy-start | bytes 4718596
  83.9 10.6 %collective-permute-start.41 = (bf16[2,2,192,256]{3,2,1,0:T(8,128)(2,1)S(1)}, bf16[2,2,192,256]{3,2,1,0:T(8,128)(2,1)S(1)}, u32[]{:S(2)}, u32[]{:S(2)}) collective-permute-start(bf16[2,2,192,256]{3,2,1,0:T(8,128)(2,1)S(1)} %get-tuple-element.103), channel_id=1, source_target_pairs={{0,8},{8,0},{16,24},{24,16},{1,9},{9,1},{17,25},{25,17},{2,10},{10... | collective-permute-start | bytes 1179656 | tf_op jit(solution)/shard_map/ppermute | solution.py:633
  84.5 3.4 %copy-start = (f32[1024,768]{1,0:T(8,128)S(1)}, f32[1024,768]{1,0:T(8,128)}, u32[]{:S(2)}) copy-start(f32[1024,768]{1,0:T(8,128)} %get-tuple-element.66.hidden) | copy-start | bytes 9437188
  84.7 10.5 %collective-permute-start.32 = (bf16[2,2,192,256]{3,2,1,0:T(8,128)(2,1)S(1)}, bf16[2,2,192,256]{3,2,1,0:T(8,128)(2,1)S(1)}, u32[]{:S(2)}, u32[]{:S(2)}) collective-permute-start(bf16[2,2,192,256]{3,2,1,0:T(8,128)(2,1)S(1)} %get-tuple-element.113), channel_id=1, source_target_pairs={{0,16},{8,24},{16,0},{24,8},{1,17},{9,25},{17,1},{25,9},{2,18},{10... | collective-permute-start | bytes 1179656 | tf_op jit(solution)/shard_map/ppermute | solution.py:633
  86.5 12.1 %collective-permute-start.36 = (bf16[2,2,192,256]{3,2,1,0:T(8,128)(2,1)S(1)}, bf16[2,2,192,256]{3,2,1,0:T(8,128)(2,1)S(1)}, u32[]{:S(2)}, u32[]{:S(2)}) collective-permute-start(bf16[2,2,192,256]{3,2,1,0:T(8,128)(2,1)S(1)} %fusion.9), channel_id=1, source_target_pairs={{0,2},{1,3},{2,0},{3,1},{4,6},{5,7},{6,4},{7,5},{8,10},{9,11},{10,... | collective-permute-start | bytes 1179656 | tf_op jit(solution)/shard_map/ppermute | solution.py:633
  88.0 19.0 %collective-permute-start.8 = (bf16[256,768]{1,0:T(8,128)(2,1)S(1)}, bf16[256,768]{1,0:T(8,128)(2,1)S(1)}, u32[]{:S(2)}, u32[]{:S(2)}) collective-permute-start(bf16[256,768]{1,0:T(8,128)(2,1)S(1)} %fusion.4), channel_id=1, source_target_pairs={{0,2},{1,3},{2,0},{3,1},{4,6},{5,7},{6,4},{7,5},{8,10},{9,11},{10,... | collective-permute-start | bytes 1179656 | tf_op jit(solution)/shard_map/ppermute | solution.py:633
  94.6 13.7 %collective-permute-start.42 = (bf16[2,192,256]{2,1,0:T(8,128)(2,1)S(1)}, bf16[2,192,256]{2,1,0:T(8,128)(2,1)S(1)}, u32[]{:S(2)}, u32[]{:S(2)}) collective-permute-start(bf16[2,192,256]{2,1,0:T(8,128)(2,1)S(1)} %get-tuple-element.109), channel_id=1, source_target_pairs={{0,16},{8,24},{16,0},{24,8},{1,17},{9,25},{17,1},{25,9},{2,18},{10... | collective-permute-start | bytes 589832 | tf_op jit(solution)/shard_map/ppermute | solution.py:633
  95.3 49.0 %collective-permute-start.33 = (bf16[2,192,256]{2,1,0:T(8,128)(2,1)S(1)}, bf16[2,192,256]{2,1,0:T(8,128)(2,1)S(1)}, u32[]{:S(2)}, u32[]{:S(2)}) collective-permute-start(bf16[2,192,256]{2,1,0:T(8,128)(2,1)S(1)} %get-tuple-element.111), channel_id=1, source_target_pairs={{0,2},{1,3},{2,0},{3,1},{4,6},{5,7},{6,4},{7,5},{8,10},{9,11},{10,... | collective-permute-start | bytes 589832 | tf_op jit(solution)/shard_map/ppermute | solution.py:633
  98.8 46.0 %collective-permute-start.37 = (bf16[2,192,256]{2,1,0:T(8,128)(2,1)S(1)}, bf16[2,192,256]{2,1,0:T(8,128)(2,1)S(1)}, u32[]{:S(2)}, u32[]{:S(2)}) collective-permute-start(bf16[2,192,256]{2,1,0:T(8,128)(2,1)S(1)} %get-tuple-element.117), channel_id=1, source_target_pairs={{0,8},{8,0},{16,24},{24,16},{1,9},{9,1},{17,25},{25,17},{2,10},{10... | collective-permute-start | bytes 589832 | tf_op jit(solution)/shard_map/ppermute | solution.py:633
  108.3 56.8 %collective-permute-start.43 = (bf16[192,256]{1,0:T(8,128)(2,1)S(1)}, bf16[192,256]{1,0:T(8,128)(2,1)S(1)}, u32[]{:S(2)}, u32[]{:S(2)}) collective-permute-start(bf16[192,256]{1,0:T(8,128)(2,1)S(1)} %fusion.44), channel_id=1, source_target_pairs={{0,4},{1,5},{2,6},{3,7},{4,0},{5,1},{6,2},{7,3},{8,12},{9,13},{10,... | collective-permute-start | bytes 294920 | tf_op jit(solution)/shard_map/ppermute | solution.py:633
  111.0 1.1 copy-start.2
  144.2 12.6 %collective-permute-start.10 = (bf16[2,256,768]{2,1,0:T(8,128)(2,1)}, bf16[2,256,768]{2,1,0:T(8,128)(2,1)S(1)}, u32[]{:S(2)}, u32[]{:S(2)}) collective-permute-start(bf16[2,256,768]{2,1,0:T(8,128)(2,1)} %get-tuple-element.77), channel_id=1, source_target_pairs={{0,1},{1,0},{2,3},{3,2},{4,5},{5,4},{6,7},{7,6},{8,9},{9,8},{10,11... | collective-permute-start | bytes 2359304 | tf_op jit(solution)/shard_map/ppermute | solution.py:633
  144.3 10.8 %collective-permute-start.34 = (bf16[192,256]{1,0:T(8,128)(2,1)S(1)}, bf16[192,256]{1,0:T(8,128)(2,1)S(1)}, u32[]{:S(2)}, u32[]{:S(2)}) collective-permute-start(bf16[192,256]{1,0:T(8,128)(2,1)S(1)} %fusion.40), channel_id=1, source_target_pairs={{0,4},{1,5},{2,6},{3,7},{4,0},{5,1},{6,2},{7,3},{8,12},{9,13},{10,... | collective-permute-start | bytes 294920 | tf_op jit(solution)/shard_map/ppermute | solution.py:633
  144.7 12.0 %collective-permute-start.38 = (bf16[192,256]{1,0:T(8,128)(2,1)S(1)}, bf16[192,256]{1,0:T(8,128)(2,1)S(1)}, u32[]{:S(2)}, u32[]{:S(2)}) collective-permute-start(bf16[192,256]{1,0:T(8,128)(2,1)S(1)} %fusion.42), channel_id=1, source_target_pairs={{0,4},{1,5},{2,6},{3,7},{4,0},{5,1},{6,2},{7,3},{8,12},{9,13},{10,... | collective-permute-start | bytes 294920 | tf_op jit(solution)/shard_map/ppermute | solution.py:633
  157.7 4.7 %copy-start.19 = (f32[1,768]{1,0:T(1,128)S(1)}, f32[1,768]{1,0:T(1,128)}, u32[]{:S(2)}) copy-start(f32[1,768]{1,0:T(1,128)} %get-tuple-element.82) | copy-start | bytes 9220
  157.7 8.2 %copy-start.23 = (bf16[2,2,2,48,384]{4,3,2,1,0:T(8,128)(2,1)S(1)}, bf16[2,2,2,48,384]{4,3,2,1,0:T(8,128)(2,1)}, u32[]{:S(2)}) copy-start(bf16[2,2,2,48,384]{4,3,2,1,0:T(8,128)(2,1)} %get-tuple-element.86) | copy-start | bytes 884740
  157.7 8.3 %copy-start.21 = (bf16[4,2,3,48,384]{4,3,2,1,0:T(8,128)(2,1)S(1)}, bf16[4,2,3,48,384]{4,3,2,1,0:T(8,128)(2,1)}, u32[]{:S(2)}) copy-start(bf16[4,2,3,48,384]{4,3,2,1,0:T(8,128)(2,1)} %get-tuple-element.84) | copy-start | bytes 2654212
  162.4 16.7 %copy-start.18 = (bf16[2,2,2,48,384]{4,3,2,1,0:T(8,128)(2,1)S(1)}, bf16[2,2,2,48,384]{4,3,2,1,0:T(8,128)(2,1)}, u32[]{:S(2)}) copy-start(bf16[2,2,2,48,384]{4,3,2,1,0:T(8,128)(2,1)} %get-tuple-element.85) | copy-start | bytes 884740
  163.1 1.2 collective-permute-start.12
  163.2 6.3 %collective-permute-start.39 = (bf16[2,96,256]{2,1,0:T(8,128)(2,1)S(1)}, bf16[2,96,256]{2,1,0:T(8,128)(2,1)S(1)}, u32[]{:S(2)}, u32[]{:S(2)}) collective-permute-start(bf16[2,96,256]{2,1,0:T(8,128)(2,1)S(1)} %fusion.45), channel_id=1, source_target_pairs={{0,1},{1,0},{2,3},{3,2},{4,5},{5,4},{6,7},{7,6},{8,9},{9,8},{10,11... | collective-permute-start | bytes 294920 | tf_op jit(solution)/shard_map/ppermute | solution.py:633
  165.1 3.7 %collective-permute-start.13 = (f32[2,768]{1,0:T(2,128)S(1)}, f32[2,768]{1,0:T(2,128)S(1)}, u32[]{:S(2)}, u32[]{:S(2)}) collective-permute-start(f32[2,768]{1,0:T(2,128)S(1)} %fusion.65), channel_id=1, source_target_pairs={{0,2},{1,3},{2,0},{3,1},{4,6},{5,7},{6,4},{7,5},{8,10},{9,11},{10,... | collective-permute-start | bytes 18440 | tf_op jit(solution)/shard_map/ppermute | solution.py:633
  165.9 13.3 %copy-start.22 = (bf16[256,768]{1,0:T(8,128)(2,1)S(1)}, bf16[256,768]{1,0:T(8,128)(2,1)}, u32[]{:S(2)}) copy-start(bf16[256,768]{1,0:T(8,128)(2,1)} %get-tuple-element.80) | copy-start | bytes 1179652
  165.9 16.1 %copy-start.4 = (bf16[4,2,3,48,384]{4,3,2,1,0:T(8,128)(2,1)S(1)}, bf16[4,2,3,48,384]{4,3,2,1,0:T(8,128)(2,1)}, u32[]{:S(2)}) copy-start(bf16[4,2,3,48,384]{4,3,2,1,0:T(8,128)(2,1)} %get-tuple-element.83) | copy-start | bytes 2654212
  165.9 13.2 %collective-permute-start.18 = (bf16[2,2,2,48,384]{4,3,2,1,0:T(8,128)(2,1)S(1)}, bf16[2,2,2,48,384]{4,3,2,1,0:T(8,128)(2,1)S(1)}, u32[]{:S(2)}, u32[]{:S(2)}) collective-permute-start(bf16[2,2,2,48,384]{4,3,2,1,0:T(8,128)(2,1)S(1)} %copy-done.23), channel_id=1, source_target_pairs={{0,1},{1,0},{2,3},{3,2},{4,5},{5,4},{6,7},{7,6},{8,9},{9,8},{10,11... | collective-permute-start | bytes 884744 | tf_op jit(solution)/shard_map/ppermute | solution.py:633
  166.0 15.9 %collective-permute-start.17 = (bf16[4,2,3,48,384]{4,3,2,1,0:T(8,128)(2,1)S(1)}, bf16[4,2,3,48,384]{4,3,2,1,0:T(8,128)(2,1)S(1)}, u32[]{:S(2)}, u32[]{:S(2)}) collective-permute-start(bf16[4,2,3,48,384]{4,3,2,1,0:T(8,128)(2,1)S(1)} %copy-done.21), channel_id=1, source_target_pairs={{0,1},{1,0},{2,3},{3,2},{4,5},{5,4},{6,7},{7,6},{8,9},{9,8},{10,11... | collective-permute-start | bytes 2654216 | tf_op jit(solution)/shard_map/ppermute | solution.py:633
  169.5 4.6 %collective-permute-start.14 = (f32[2,768]{1,0:T(2,128)S(1)}, f32[2,768]{1,0:T(2,128)S(1)}, u32[]{:S(2)}, u32[]{:S(2)}) collective-permute-start(f32[2,768]{1,0:T(2,128)S(1)} %fusion.70), channel_id=1, source_target_pairs={{0,4},{1,5},{2,6},{3,7},{4,0},{5,1},{6,2},{7,3},{8,12},{9,13},{10,... | collective-permute-start | bytes 18440 | tf_op jit(solution)/shard_map/ppermute | solution.py:633
  174.1 3.6 %collective-permute-start.15 = (f32[2,768]{1,0:T(2,128)S(1)}, f32[2,768]{1,0:T(2,128)S(1)}, u32[]{:S(2)}, u32[]{:S(2)}) collective-permute-start(f32[2,768]{1,0:T(2,128)S(1)} %add.377), channel_id=1, source_target_pairs={{0,8},{8,0},{16,24},{24,16},{1,9},{9,1},{17,25},{25,17},{2,10},{10... | collective-permute-start | bytes 18440 | tf_op jit(solution)/shard_map/ppermute | solution.py:633
  177.7 3.6 %collective-permute-start.16 = (f32[2,768]{1,0:T(2,128)S(1)}, f32[2,768]{1,0:T(2,128)S(1)}, u32[]{:S(2)}, u32[]{:S(2)}) collective-permute-start(f32[2,768]{1,0:T(2,128)S(1)} %add.378), channel_id=1, source_target_pairs={{0,16},{8,24},{16,0},{24,8},{1,17},{9,25},{17,1},{25,9},{2,18},{10... | collective-permute-start | bytes 18440 | tf_op jit(solution)/shard_map/ppermute | solution.py:633
  179.1 11.3 %collective-permute-start.11 = (bf16[256,768]{1,0:T(8,128)(2,1)S(1)}, bf16[256,768]{1,0:T(8,128)(2,1)S(1)}, u32[]{:S(2)}, u32[]{:S(2)}) collective-permute-start(bf16[256,768]{1,0:T(8,128)(2,1)S(1)} %copy-done.22), channel_id=1, source_target_pairs={{0,2},{1,3},{2,0},{3,1},{4,6},{5,7},{6,4},{7,5},{8,10},{9,11},{10,... | collective-permute-start | bytes 1179656 | tf_op jit(solution)/shard_map/ppermute | solution.py:633
  182.7 7.7 %copy-start.15 = (bf16[256,768]{1,0:T(8,128)(2,1)S(1)}, bf16[256,768]{1,0:T(8,128)(2,1)}, u32[]{:S(2)}) copy-start(bf16[256,768]{1,0:T(8,128)(2,1)} %get-tuple-element.79) | copy-start | bytes 1179652
  182.8 8.7 %collective-permute-start.19 = (bf16[2,2,2,64,384]{4,3,1,0,2:T(8,128)(2,1)S(1)}, bf16[2,2,2,64,384]{4,3,1,0,2:T(8,128)(2,1)S(1)}, u32[]{:S(2)}, u32[]{:S(2)}) collective-permute-start(bf16[2,2,2,64,384]{4,3,1,0,2:T(8,128)(2,1)S(1)} %dynamic-slice_bitcast_fusion), channel_id=1, source_target_pairs={{0,8},{8,0},{16,24},{24,16},{1,9},{9,1},{17,25},{25,17},{2,10},{10... | collective-permute-start | bytes 1179656 | tf_op jit(solution)/shard_map/ppermute | solution.py:633
  184.4 9.9 %collective-permute-start.23 = (bf16[2,2,2,64,384]{4,3,2,0,1:T(8,128)(2,1)S(1)}, bf16[2,2,2,64,384]{4,3,2,0,1:T(8,128)(2,1)S(1)}, u32[]{:S(2)}, u32[]{:S(2)}) collective-permute-start(bf16[2,2,2,64,384]{4,3,2,0,1:T(8,128)(2,1)S(1)} %copy_bitcast_fusion), channel_id=1, source_target_pairs={{0,16},{8,24},{16,0},{24,8},{1,17},{9,25},{17,1},{25,9},{2,18},{10... | collective-permute-start | bytes 1179656 | tf_op jit(solution)/shard_map/ppermute | solution.py:633
  185.9 12.7 %collective-permute-start.27 = (bf16[2,2,2,64,384]{4,3,1,0,2:T(8,128)(2,1)S(1)}, bf16[2,2,2,64,384]{4,3,1,0,2:T(8,128)(2,1)S(1)}, u32[]{:S(2)}, u32[]{:S(2)}) collective-permute-start(bf16[2,2,2,64,384]{4,3,1,0,2:T(8,128)(2,1)S(1)} %copy_bitcast_fusion.1), channel_id=1, source_target_pairs={{0,2},{1,3},{2,0},{3,1},{4,6},{5,7},{6,4},{7,5},{8,10},{9,11},{10,... | collective-permute-start | bytes 1179656 | tf_op jit(solution)/shard_map/ppermute | solution.py:633
  191.6 8.5 %collective-permute-start.20 = (bf16[2,2,64,384]{3,2,1,0:T(8,128)(2,1)S(1)}, bf16[2,2,64,384]{3,2,1,0:T(8,128)(2,1)S(1)}, u32[]{:S(2)}, u32[]{:S(2)}) collective-permute-start(bf16[2,2,64,384]{3,2,1,0:T(8,128)(2,1)S(1)} %get-tuple-element.105), channel_id=1, source_target_pairs={{0,16},{8,24},{16,0},{24,8},{1,17},{9,25},{17,1},{25,9},{2,18},{10... | collective-permute-start | bytes 589832 | tf_op jit(solution)/shard_map/ppermute | solution.py:633
  194.5 6.3 %collective-permute-start.24 = (bf16[2,2,64,384]{3,2,1,0:T(8,128)(2,1)S(1)}, bf16[2,2,64,384]{3,2,1,0:T(8,128)(2,1)S(1)}, u32[]{:S(2)}, u32[]{:S(2)}) collective-permute-start(bf16[2,2,64,384]{3,2,1,0:T(8,128)(2,1)S(1)} %get-tuple-element.107), channel_id=1, source_target_pairs={{0,2},{1,3},{2,0},{3,1},{4,6},{5,7},{6,4},{7,5},{8,10},{9,11},{10,... | collective-permute-start | bytes 589832 | tf_op jit(solution)/shard_map/ppermute | solution.py:633
  198.6 5.7 %collective-permute-start.28 = (bf16[2,2,64,384]{3,2,0,1:T(8,128)(2,1)S(1)}, bf16[2,2,64,384]{3,2,0,1:T(8,128)(2,1)S(1)}, u32[]{:S(2)}, u32[]{:S(2)}) collective-permute-start(bf16[2,2,64,384]{3,2,0,1:T(8,128)(2,1)S(1)} %fusion.12), channel_id=1, source_target_pairs={{0,8},{8,0},{16,24},{24,16},{1,9},{9,1},{17,25},{25,17},{2,10},{10... | collective-permute-start | bytes 589832 | tf_op jit(solution)/shard_map/ppermute | solution.py:633
  200.1 5.3 %collective-permute-start.21 = (bf16[2,64,384]{2,1,0:T(8,128)(2,1)S(1)}, bf16[2,64,384]{2,1,0:T(8,128)(2,1)S(1)}, u32[]{:S(2)}, u32[]{:S(2)}) collective-permute-start(bf16[2,64,384]{2,1,0:T(8,128)(2,1)S(1)} %get-tuple-element.131), channel_id=1, source_target_pairs={{0,2},{1,3},{2,0},{3,1},{4,6},{5,7},{6,4},{7,5},{8,10},{9,11},{10,... | collective-permute-start | bytes 294920 | tf_op jit(solution)/shard_map/ppermute | solution.py:633
  200.8 4.7 %collective-permute-start.25 = (bf16[2,64,384]{2,1,0:T(8,128)(2,1)S(1)}, bf16[2,64,384]{2,1,0:T(8,128)(2,1)S(1)}, u32[]{:S(2)}, u32[]{:S(2)}) collective-permute-start(bf16[2,64,384]{2,1,0:T(8,128)(2,1)S(1)} %get-tuple-element.133), channel_id=1, source_target_pairs={{0,8},{8,0},{16,24},{24,16},{1,9},{9,1},{17,25},{25,17},{2,10},{10... | collective-permute-start | bytes 294920 | tf_op jit(solution)/shard_map/ppermute | solution.py:633
  204.4 4.7 %collective-permute-start.29 = (bf16[2,64,384]{2,1,0:T(8,128)(2,1)S(1)}, bf16[2,64,384]{2,1,0:T(8,128)(2,1)S(1)}, u32[]{:S(2)}, u32[]{:S(2)}) collective-permute-start(bf16[2,64,384]{2,1,0:T(8,128)(2,1)S(1)} %fusion.38), channel_id=1, source_target_pairs={{0,16},{8,24},{16,0},{24,8},{1,17},{9,25},{17,1},{25,9},{2,18},{10... | collective-permute-start | bytes 294920 | tf_op jit(solution)/shard_map/ppermute | solution.py:633
  205.5 5.1 %collective-permute-start.22 = (bf16[64,384]{1,0:T(8,128)(2,1)S(1)}, bf16[64,384]{1,0:T(8,128)(2,1)S(1)}, u32[]{:S(2)}, u32[]{:S(2)}) collective-permute-start(bf16[64,384]{1,0:T(8,128)(2,1)S(1)} %fusion.60), channel_id=1, source_target_pairs={{0,4},{1,5},{2,6},{3,7},{4,0},{5,1},{6,2},{7,3},{8,12},{9,13},{10,... | collective-permute-start | bytes 147464 | tf_op jit(solution)/shard_map/ppermute | solution.py:633
  205.6 5.5 %collective-permute-start.26 = (bf16[64,384]{1,0:T(8,128)(2,1)S(1)}, bf16[64,384]{1,0:T(8,128)(2,1)S(1)}, u32[]{:S(2)}, u32[]{:S(2)}) collective-permute-start(bf16[64,384]{1,0:T(8,128)(2,1)S(1)} %fusion.62), channel_id=1, source_target_pairs={{0,4},{1,5},{2,6},{3,7},{4,0},{5,1},{6,2},{7,3},{8,12},{9,13},{10,... | collective-permute-start | bytes 147464 | tf_op jit(solution)/shard_map/ppermute | solution.py:633
  209.1 5.1 %collective-permute-start.30 = (bf16[64,384]{1,0:T(8,128)(2,1)S(1)}, bf16[64,384]{1,0:T(8,128)(2,1)S(1)}, u32[]{:S(2)}, u32[]{:S(2)}) collective-permute-start(bf16[64,384]{1,0:T(8,128)(2,1)S(1)} %fusion.64), channel_id=1, source_target_pairs={{0,4},{1,5},{2,6},{3,7},{4,0},{5,1},{6,2},{7,3},{8,12},{9,13},{10,... | collective-permute-start | bytes 147464 | tf_op jit(solution)/shard_map/ppermute | solution.py:633
  (4 other events, 3.5 us)

commit v3 on v2

v3 whole, which is shorter than its diff:
```python
import functools
import math

import jax
import jax.numpy as jnp
import numpy as np
from jax import lax
from jax.experimental import pallas as pl
from jax.experimental.pallas import tpu as pltpu
from jax.sharding import PartitionSpec as P

HEADS = 12
HEAD_FEATURES = 64
MAXLEN = 1024
GROUP = 4
PIECE = MAXLEN // GROUP
PAIR = 2 * HEAD_FEATURES
LOG2E = math.log2(math.e)

epsilon = 1e-06
masked_score = -1e30
f32 = jnp.float32
bf16 = jnp.bfloat16
MIB = 1024 * 1024

SIDES = ((0, 1), (2, 0), (1, 2))
HEAD_ORDER = tuple(h for left, right in SIDES for h in (2 * left, 2 * right + 1))

CORE, CHIP, LENGTH, OTHER_CHIP, OWN_B, OWN_Z = range(6)


def mm(a, b):
    return lax.dot_general(a, b, (((1,), (0,)), ((), ())), preferred_element_type=f32)


def mm_nt(a, b):
    return lax.dot_general(a, b, (((1,), (1,)), ((), ())), preferred_element_type=f32)


def mm_tn(a, b):
    return lax.dot_general(a, b, (((0,), (0,)), ((), ())), preferred_element_type=f32)


def call(body, grid, in_specs, out_specs, out_shape, scratch=(), aliases=None, vmem=64):
    return pl.pallas_call(
        body,
        grid_spec=pltpu.PrefetchScalarGridSpec(
            num_scalar_prefetch=1,
            grid=grid,
            in_specs=in_specs,
            out_specs=out_specs,
            scratch_shapes=list(scratch),
        ),
        out_shape=out_shape,
        input_output_aliases=aliases or {},
        compiler_params=pltpu.CompilerParams(
            dimension_semantics=("arbitrary",) * len(grid), vmem_limit_bytes=vmem * MIB
        ),
        cost_estimate=pl.CostEstimate(flops=1000, bytes_accessed=1000, transcendentals=0),
    )


def whole(shape):
    return pl.BlockSpec(shape, lambda *a: (0,) * len(shape))


def sds(shape, dtype):
    return jax.ShapeDtypeStruct(shape, dtype)


def rope_tables():
    middle = HEAD_FEATURES // 2
    frequency = 10000.0 ** (-np.arange(middle, dtype=np.float64) * 2.0 / HEAD_FEATURES)
    angles = np.arange(MAXLEN, dtype=np.float64)[:, None] * frequency[None, :]
    cosine, sine = np.cos(angles), np.sin(angles)
    none = np.zeros_like(sine)
    table = np.stack(
        [
            np.concatenate([cosine, cosine] * 2, axis=1),
            np.concatenate([-sine, none] * 2, axis=1),
            np.concatenate([none, sine] * 2, axis=1),
        ]
    )
    return table.astype(np.float32)


def rotate(u, table, sign):
    up = pltpu.roll(u, PAIR - HEAD_FEATURES // 2, 1)
    down = pltpu.roll(u, HEAD_FEATURES // 2, 1)
    if sign > 0:
        return u * table[0] + (up * table[1] + down * table[2])
    return u * table[0] - (up * table[1] + down * table[2])


def pair_of(value, side):
    left, right = (value[:, a * PAIR : (a + 1) * PAIR] for a in side)
    lane = lax.broadcasted_iota(jnp.int32, (1, PAIR), 1)
    return jnp.where(lane < HEAD_FEATURES, left, right)


def slots(start):
    return start + lax.broadcasted_iota(jnp.int32, (PIECE, 1), 0)


def piece_rows(half, place):
    return pl.ds(pl.multiple_of(half * 2 * PIECE + place * PIECE, PIECE), PIECE)


def project_body(s, own, part, gain, wq, wk, wv, table, *rest):
    qkv, normed, copy = rest[-3:]
    low_x = jnp.where(pl.program_id(0) == s[CORE], own[0], part[0])
    copy[...] = low_x
    x = low_x.astype(f32)
    r = lax.rsqrt(jnp.mean(x * x, axis=-1, keepdims=True) + epsilon)
    low = (x * r * gain[0:1, :].astype(f32)).astype(bf16)
    normed[...] = low
    width = wq.shape[1]
    for m, w in enumerate((wq, wk, wv)):
        u = mm(low, w[...])
        if m == 0:
            u = u * (1.0 / math.sqrt(HEAD_FEATURES))
        for p in range(width // PAIR):
            v = pair_of(u, SIDES[p])
            if m < 2:
                v = rotate(v, table, 1)
            at = m * width + p * PAIR
            qkv[:, at : at + PAIR] = v.astype(bf16)


def project(scalars, own, part, half, gain, weights, table, filled):
    width = weights[0].shape[0]
    cols = width // 2
    place = lambda t, s: (s[half] * 2 + t, 0)
    source = lambda a: pl.BlockSpec((1, PIECE, width), lambda t, s: (s[CHIP] if a.shape[0] > 1 else 0, 0, 0))
    weight_spec = pl.BlockSpec((width, cols), lambda t, s: (0, s[CORE]))
    in_specs = [
        source(own),
        source(part),
        whole((2, width)),
        weight_spec,
        weight_spec,
        weight_spec,
        pl.BlockSpec((3, PIECE, PAIR), lambda t, s: (0, s[half] * 2 + t, 0)),
    ]
    args = [scalars, own, part, gain, *weights, table]
    aliases = None
    if filled is not None:
        in_specs += [pl.BlockSpec(memory_space=pl.ANY)] * 3
        aliases = {len(args) + a: a for a in range(3)}
        args += list(filled)
    return call(
        project_body,
        (2,),
        in_specs,
        [pl.BlockSpec((PIECE, 3 * cols), place), pl.BlockSpec((PIECE, width), place), pl.BlockSpec((PIECE, width), place)],
        [sds((MAXLEN, 3 * cols), bf16), sds((MAXLEN, width), bf16), sds((MAXLEN, width), bf16)],
        aliases=aliases,
    )(*args)


def head_mask(h):
    lane = lax.broadcasted_iota(jnp.int32, (1, PAIR), 1)
    return lane < HEAD_FEATURES if h == 0 else lane >= HEAD_FEATURES


def attend_body(s, q, k, v, out, lse):
    row = lax.broadcasted_iota(jnp.int32, (PIECE, PIECE), 0)
    col = lax.broadcasted_iota(jnp.int32, (PIECE, PIECE), 1)
    lane = lax.broadcasted_iota(jnp.int32, (PIECE, PAIR), 1)
    ones = jnp.ones((MAXLEN, PAIR), bf16)

    def score(b, h):
        at = b * PIECE
        qh = jnp.where(head_mask(h), q[at : at + PIECE, :], jnp.zeros((), bf16))
        near = mm_nt(qh, k[at : at + PIECE, :])
        return near, mm_nt(qh, k[:at, :]) if b else None

    def mix(b, near, far):
        at = b * PIECE
        near = jnp.where(row >= col, near, masked_score)
        top = jnp.max(near, axis=-1, keepdims=True)
        if b:
            top = jnp.maximum(top, jnp.max(far, axis=-1, keepdims=True))
        shift = top * LOG2E
        near = jnp.exp2(near * LOG2E - shift).astype(bf16)
        mixed = mm(near, jnp.concatenate([v[at : at + PIECE, :], ones[:PIECE]], axis=1))
        if b:
            far = jnp.exp2(far * LOG2E - shift).astype(bf16)
            mixed = mixed + mm(far, jnp.concatenate([v[:at, :], ones[:at]], axis=1))
        total = mixed[:, PAIR:]
        return mixed[:, :PAIR] * (1.0 / total), top + jnp.log(total)

    units = [(b, h) for b in range(GROUP) for h in range(2)]
    ahead = score(*units[0])
    done = []
    for at, (b, h) in enumerate(units):
        now = ahead
        if at + 1 < len(units):
            ahead = score(*units[at + 1])
        done.append(mix(b, *now))
        if h == 1:
            rows = slice(b * PIECE, (b + 1) * PIECE)
            (left, left_log), (right, right_log) = done
            done = []
            joined = jnp.where(head_mask(0), left, right)
            out[rows, :] = jnp.where(slots(b * PIECE) < s[LENGTH], joined, 0.0).astype(bf16)
            lse[0, rows, :] = jnp.where(lane == 0, left_log, right_log)


def attend(scalars, qkv):
    pairs = qkv.shape[1] // 3 // PAIR
    spec = lambda m: pl.BlockSpec((MAXLEN, PAIR), lambda p, s, m=m: (0, m * pairs + p))
    return call(
        attend_body,
        (pairs,),
        [spec(0), spec(1), spec(2)],
        [pl.BlockSpec((MAXLEN, PAIR), lambda p, s: (0, p)), pl.BlockSpec((1, MAXLEN, PAIR), lambda p, s: (p, 0, 0))],
        [sds((MAXLEN, pairs * PAIR), bf16), sds((pairs, MAXLEN, PAIR), f32)],
    )(scalars, qkv, qkv, qkv)


def pack_rows(block):
    half = block.shape[0] // 2
    lane = lax.broadcasted_iota(jnp.int32, (1, PAIR), 1)
    top, bottom = block[:half], block[half:]
    left = jnp.where(lane < HEAD_FEATURES, top, pltpu.roll(bottom, HEAD_FEATURES, 1))
    right = jnp.where(lane < HEAD_FEATURES, pltpu.roll(top, HEAD_FEATURES, 1), bottom)
    return left, right


def plane_blocks(s, keep, arrived, targets, rows, with_out):
    size = 2 * rows if with_out else rows
    core = s[CORE]
    for r, target in enumerate(targets):
        place = s[OWN_B] ^ r
        for z in range(4):
            at = pl.ds(pl.multiple_of((2 * z + place % 2) * rows, 16), rows)
            target[z * size : z * size + rows, :] = jnp.where(place // 2 == core, keep[at, :], arrived[at, :])
            if with_out:
                at = pl.ds(pl.multiple_of((8 + z % 2 * 4 + place) * rows, 16), rows)
                target[z * size + rows : (z + 1) * size, :] = jnp.where(z // 2 == core, keep[at, :], arrived[at, :])


def attend_back_body(pair, n_seq, s, *refs):
    first, last = pair == 0, pair == len(SIDES) - 1
    refs = list(refs)
    take = lambda count: [refs.pop(0) for _ in range(count)]
    qkv_hbm, attn_hbm, lse_hbm = take(3)
    if first:
        hidden_hbm, dyb_hbm, mine_hbm, theirs_hbm, gain, layer_hbm, layer_far_hbm = take(7)
    else:
        (dhb_hbm,) = take(1)
    wo_hbm, wq_hbm, wk_hbm, wv_hbm, normed_hbm, table_hbm = take(6)
    earlier = take(len(SIDES) - 1) if last else []
    sent = [] if first else take(2) if n_seq == 8 else []
    if last:
        stay_hbm, leave_hbm, x_hbm, second_in = take(4)
    (keep_out,) = take(1)
    packed = n_seq == 8
    if not (last and packed):
        (send_out,) = take(1)
    if first:
        dhb_out, second, layer_stay, layer_leave = take(4)
    if last:
        norm_keep, norm_send, gains, layer_out = take(4)
        if packed:
            send_out = norm_send.at[pl.ds(MAXLEN, norm_send.shape[0] - MAXLEN), :]
    else:
        (d_out,) = take(1)
    plane = take(4) if sent else []
    q, k, v, o, lse, wo, weights, normed, table, sems = take(10)
    da, da_t, q_t, dk_t, dv_t, dq, grads = take(7)
    if first:
        hidden, dyb, mine, theirs, attn, out_grad, layer, layer_far = take(8)
        dhb = dhb_out
    else:
        (dhb,) = take(1)
    if last:
        before, joined, x, gain_rows = take(4)
    before_sent = take(2) if sent else []
    core = s[CORE]
    width = normed.shape[1]
    zero = jnp.zeros((), bf16)
    pairs = len(SIDES)
    heads = pairs * PAIR
    copies = []

    def fetch(source, target):
        copy = pltpu.make_async_copy(source, target, sems.at[len(copies)])
        copy.start()
        copies.append(copy)
        return copy

    lanes_of = lambda m: slice((m * pairs + pair) * PAIR, (m * pairs + pair + 1) * PAIR)
    chunks = [slice(t * PIECE, (t + 1) * PIECE) for t in range(GROUP)]
    chunk_copies = []
    if first:
        for rows in chunks:
            chunk_copies.append(
                [
                    fetch(source.at[rows, :], target.at[rows, :])
                    for source, target in (
                        (mine_hbm, mine),
                        (theirs_hbm, theirs),
                        (hidden_hbm, hidden),
                        (dyb_hbm, dyb),
                    )
                ]
            )
    wo_copies = [
        fetch(
            wo_hbm.at[pl.ds(pl.multiple_of(core * heads + head * HEAD_FEATURES, HEAD_FEATURES), HEAD_FEATURES), :],
            wo.at[index * HEAD_FEATURES : (index + 1) * HEAD_FEATURES, :],
        )
        for index, head in enumerate(HEAD_ORDER[2 * pair : 2 * pair + 2])
    ]
    if first:
        attn_copy = fetch(attn_hbm, attn)
        lane_o = slice(0, PAIR)
    else:
        dhb_copy = fetch(dhb_hbm, dhb)
    q_copies = [fetch(qkv_hbm.at[:, lanes_of(0)], q), fetch(qkv_hbm.at[:, lanes_of(1)], k)]
    v_copies = [
        fetch(qkv_hbm.at[:, lanes_of(2)], v),
        fetch(attn_hbm.at[:, pair * PAIR : (pair + 1) * PAIR], o),
        fetch(lse_hbm.at[pair], lse),
    ]
    late_copies = [fetch(normed_hbm, normed), fetch(table_hbm, table)]
    late_copies += [fetch(source, target) for source, target in zip(sent, before_sent)]
    for m, w in enumerate((wq_hbm, wk_hbm, wv_hbm)):
        if last:
            late_copies.append(fetch(w.at[:, pl.ds(pl.multiple_of(core * heads, PAIR), heads)], weights.at[m]))
    if first:
        layer_copies = [fetch(layer_hbm, layer), fetch(layer_far_hbm, layer_far)]
    if last:
        late_copies.append(fetch(x_hbm, x))
        late_copies.append(fetch(stay_hbm, layer_out.at[s[CHIP]]))
        late_copies.append(fetch(leave_hbm, layer_out.at[s[OTHER_CHIP]]))
        for at, source in enumerate(earlier):
            late_copies.append(fetch(source, before.at[:, at * heads : (at + 1) * heads]))

    if first:
        scale = gain[1:2, :].astype(f32)
        sums = jnp.zeros((1, width), f32)
        for rows, waiting in zip(chunks, chunk_copies):
            for copy in waiting:
                copy.wait()
            h = hidden[rows, :].astype(f32)
            r = lax.rsqrt(jnp.mean(h * h, axis=-1, keepdims=True) + epsilon)
            g = mine[rows, :].astype(f32) + theirs[rows, :].astype(f32)
            sums = sums + jnp.sum(g * h * r, axis=0, keepdims=True)
            scaled = g * scale
            inner = jnp.mean(scaled * h, axis=-1, keepdims=True)
            d = dyb[rows, :].astype(f32) + r * scaled - h * (r * r * r) * inner
            dhb[rows, :] = d.astype(bf16)
        second[...] = sums * 0.5
    else:
        dhb_copy.wait()
    for copy in wo_copies + q_copies:
        copy.wait()
    for t, rows in enumerate(chunks):
        d = mm_nt(dhb[rows, :], wo[...])
        da[rows, :] = jnp.where(slots(t * PIECE) < s[LENGTH], d, 0.0).astype(bf16)
    da_t[...] = jnp.transpose(da[...])
    q_t[...] = jnp.transpose(q[...])
    for copy in v_copies:
        copy.wait()

    row = lax.broadcasted_iota(jnp.int32, (PIECE, PIECE), 0)
    col = lax.broadcasted_iota(jnp.int32, (PIECE, PIECE), 1)

    def score(a, h):
        at = a * PIECE
        mask = head_mask(h)
        qh = jnp.where(mask, q[at : at + PIECE, :], zero)
        gh = jnp.where(mask, da[at : at + PIECE, :], zero)
        near = mm_nt(qh, k[at : at + PIECE, :]), mm_nt(gh, v[at : at + PIECE, :])
        far = (mm_nt(qh, k[:at, :]), mm_nt(gh, v[:at, :])) if a else None
        return near, far

    def back(a, h, near, far):
        at = a * PIECE
        rows = slice(at, at + PIECE)
        feats = slice(h * HEAD_FEATURES, (h + 1) * HEAD_FEATURES)
        mask = head_mask(h)
        shift = lse[rows, h : h + 1] * LOG2E
        product = da[rows, :].astype(f32) * o[rows, :].astype(f32)
        inner = jnp.sum(jnp.where(mask, product, 0.0), axis=-1, keepdims=True)
        near_prob = jnp.exp2(jnp.where(row >= col, near[0] * LOG2E - shift, masked_score))
        near_ds = (near_prob * (near[1] - inner)).astype(bf16)
        query_grad = mm(near_ds, jnp.where(mask, k[rows, :], zero))
        parts = [(rows, near_prob.astype(bf16), near_ds)]
        if a:
            far_prob = jnp.exp2(far[0] * LOG2E - shift)
            far_ds = (far_prob * (far[1] - inner)).astype(bf16)
            query_grad = query_grad + mm(far_ds, jnp.where(mask, k[:at, :], zero))
            parts.append((slice(0, at), far_prob.astype(bf16), far_ds))
        for cols, prob, ds in parts:
            value_grad = mm(da_t[feats, rows], prob)
            key_grad = mm(q_t[feats, rows], ds)
            if a == GROUP - 1:
                dv_t[feats, cols] = value_grad
                dk_t[feats, cols] = key_grad
            else:
                dv_t[feats, cols] += value_grad
                dk_t[feats, cols] += key_grad
        return query_grad

    units = [(a, h) for a in reversed(range(GROUP)) for h in range(2)]
    ahead = score(*units[0])
    held = None
    for at, (a, h) in enumerate(units):
        now = ahead
        if at + 1 < len(units):
            ahead = score(*units[at + 1])
        g = back(a, h, *now)
        if h == 0:
            held = g
        else:
            dq[a * PIECE : (a + 1) * PIECE, :] = held + g

    for copy in late_copies:
        copy.wait()
    d = jnp.concatenate(
        [
            rotate(dq[...] * (1.0 / math.sqrt(HEAD_FEATURES)), table, -1).astype(bf16),
            rotate(jnp.transpose(dk_t[...]), table, -1).astype(bf16),
            jnp.transpose(dv_t[...].astype(bf16)),
        ],
        axis=1,
    )
    if last:
        before[:, (pairs - 1) * heads :] = d
    else:
        d_out[...] = d
    grads[...] = mm_tn(normed[...], d)
    if sent:
        plane_blocks(s, *before_sent, plane, width // n_seq // 2, pair == 1)

    rows = width // n_seq
    half_row = rows // 2
    if rows % 16:
        keep_out[:width, :] = grads[...].astype(bf16)
    else:
        left_x = SIDES[pair][0] * 2 // pairs
        for target, place in ((keep_out, core), (send_out, 1 - core)):
            for z in range(n_seq // 2):
                at = pl.ds(pl.multiple_of((2 * z + place) * rows, 8), rows)
                for m in range(3):
                    lanes = slice(m * PAIR, (m + 1) * PAIR)
                    left, right = pack_rows(grads[at, lanes])
                    for x_of, value in ((left_x, left), (1 - left_x, right)):
                        to = (2 * z + x_of) * half_row
                        target[to : to + half_row, lanes] = value.astype(bf16)

    if first:
        for copy in layer_copies:
            copy.wait()
        for target, half in ((layer_leave, s[OTHER_CHIP]), (layer_stay, s[CHIP])):
            value = layer[half] + layer_far[half].astype(f32)
            live = slots(half * 2 * PIECE + core * PIECE) < s[LENGTH]
            target[...] = jnp.where(live, value, 0.0).astype(bf16)
        attn_copy.wait()
        g = mm_tn(attn[...], dhb[...])
        for index, head in enumerate(HEAD_ORDER):
            out_grad[head * HEAD_FEATURES : (head + 1) * HEAD_FEATURES, :] = g[
                index * HEAD_FEATURES : (index + 1) * HEAD_FEATURES, :
            ]
        if rows % 16:
            keep_out[width:, :] = jnp.concatenate([out_grad[:, :heads], out_grad[:, heads:]], axis=0).astype(bf16)
        else:
            column = width // 4
            for target, place in ((keep_out, core), (send_out, 1 - core)):
                for z in range(n_seq // 4):
                    block = out_grad[pl.ds(pl.multiple_of((2 * z + place) * rows, 8), rows), :]
                    for b in range(4):
                        lanes = slice(b * column, (b + 1) * column)
                        to = (n_seq + 4 * z + b) * half_row
                        target[to : to + half_row, :] = jnp.concatenate(
                            [block[:half_row, lanes], block[half_row:, lanes]], axis=1
                        ).astype(bf16)
    if last:
        for p, side in enumerate(SIDES):
            for m in range(3):
                at = p * heads + m * PAIR
                joined[:, at : at + PAIR] = pair_of(weights[m], side)
        sums = jnp.zeros((1, width), f32)
        for half in range(2):
            for target, place in ((norm_send, 1 - core), (norm_keep, core)):
                where = piece_rows(half, place)
                part = mm_nt(before[where, :], joined[...])
                if target is norm_keep:
                    target[half] = part.astype(bf16)
                else:
                    for side in range(2):
                        at = (2 * half + side) * PIECE
                        target[at : at + PIECE, :] = part[:, side * heads : (side + 1) * heads].astype(bf16)
                h = x[where, :].astype(f32)
                sums = sums + jnp.sum(part * (h * lax.rsqrt(jnp.mean(h * h, axis=-1, keepdims=True) + epsilon)), axis=0, keepdims=True)
        gain_rows[...] = jnp.zeros_like(gain_rows)
        for index, value in enumerate((sums, second_in[...])):
            for part in range(2):
                gain_rows[2 * index + part : 2 * index + part + 1, :] = value[:, part * heads : (part + 1) * heads]
        high = gain_rows[...].astype(bf16)
        low = (gain_rows[...] - high.astype(f32)).astype(bf16)
        gains[...] = jnp.concatenate([high, low], axis=0)
        if rows % 16 == 0:
            send_out[n_seq * half_row :, :] = gains[...]


def attend_back(pair, scalars, qkv, attn, lse, given, wo, weights, normed, table, earlier, n_seq, sent=()):
    first, last = pair == 0, pair == len(SIDES) - 1
    heads = attn.shape[1]
    width = wo.shape[1]
    rows = width // n_seq
    token_shape = (2, PIECE, width)
    if rows % 16 == 0:
        count = n_seq * rows // 2 * (2 if first else 1)
        shapes = [(count, heads)] * 2
    else:
        shapes = [(2 * width if first else width, heads), (8, 128)]
    extra = shapes[1][0] + 16 if n_seq == 8 else 0
    outs = [sds(a, bf16) for a in shapes[: 1 if last and n_seq == 8 else 2]]
    if first:
        outs += [sds((MAXLEN, width), bf16), sds((1, width), f32)]
        outs += [sds((PIECE, width), bf16)] * 2
    if last:
        outs += [sds(token_shape, bf16), sds((MAXLEN + extra, heads), bf16), sds((16, heads), bf16)]
        outs += [sds(token_shape, bf16)]
    else:
        outs += [sds((MAXLEN, heads), bf16)]
    outs += [sds((2 * rows * (2 if pair == 1 else 1), heads), bf16)] * (4 if sent else 0)
    later = list(earlier[: len(SIDES) - 1]) + list(sent) + list(earlier[len(SIDES) - 1 :])
    args = [qkv, attn, lse, *given, wo, *weights, normed, table, *later]
    in_specs = [pl.BlockSpec(memory_space=pl.ANY)] * len(args)
    if first:
        in_specs[7] = whole((2, width))
    if last:
        in_specs[-1] = whole((1, width))
    scratch = [
        pltpu.VMEM((MAXLEN, PAIR), bf16),
        pltpu.VMEM((MAXLEN, PAIR), bf16),
        pltpu.VMEM((MAXLEN, PAIR), bf16),
        pltpu.VMEM((MAXLEN, PAIR), bf16),
        pltpu.VMEM((MAXLEN, PAIR), f32),
        pltpu.VMEM((PAIR, width), bf16),
        pltpu.VMEM((3, width, heads) if last else (3, 16, 128), bf16),
        pltpu.VMEM((MAXLEN, width), bf16),
        pltpu.VMEM((3, MAXLEN, PAIR), f32),
        pltpu.SemaphoreType.DMA((32,)),
        pltpu.VMEM((MAXLEN, PAIR), bf16),
        pltpu.VMEM((PAIR, MAXLEN), bf16),
        pltpu.VMEM((PAIR, MAXLEN), bf16),
        pltpu.VMEM((PAIR, MAXLEN), f32),
        pltpu.VMEM((PAIR, MAXLEN), f32),
        pltpu.VMEM((MAXLEN, PAIR), f32),
        pltpu.VMEM((width, heads), f32),
    ]
    if first:
        scratch += [
            pltpu.VMEM((MAXLEN, width), bf16),
            pltpu.VMEM((MAXLEN, width), bf16),
            pltpu.VMEM((MAXLEN, width), bf16),
            pltpu.VMEM((MAXLEN, width), bf16),
            pltpu.VMEM((MAXLEN, heads), bf16),
            pltpu.VMEM((heads, width), f32),
            pltpu.VMEM(token_shape, f32),
            pltpu.VMEM(token_shape, bf16),
        ]
    else:
        scratch += [pltpu.VMEM((MAXLEN, width), bf16)]
    if last:
        scratch += [
            pltpu.VMEM((MAXLEN, len(SIDES) * heads), bf16),
            pltpu.VMEM((width, len(SIDES) * heads), bf16),
            pltpu.VMEM((MAXLEN, width), bf16),
            pltpu.VMEM((8, heads), f32),
        ]
    if sent:
        scratch += [pltpu.VMEM(a.shape, bf16) for a in sent]
    return call(
        functools.partial(attend_back_body, pair, n_seq),
        (1,),
        in_specs,
        [whole(a.shape) for a in outs],
        outs,
        scratch=scratch,
    )(scalars, *args)


def feed_body(
    packed, s, x_hbm, dy_hbm, dy_pair_hbm, dy_far_hbm, dy_far_pair_hbm, attn_hbm, attn_pair_hbm, wo_hbm, gain, *refs
):
    refs = list(refs)
    take = lambda count: [refs.pop(0) for _ in range(count)]
    wg_hbm, wu_hbm, wd_hbm = take(3)
    hidden_out, dyb_out, dn_out, layer_out, send_out = take(5)
    grads_out = take(6 if packed else 3)
    x, attn, wo, wg, wu, wd, dyb = take(7)
    hidden, hidden_low, low, low_t, dyb_t, acts, dgs, dus, total, dn, layer, send = take(12)
    blocks = take(6 if packed else 3)
    (sems,) = take(1)
    core = s[CORE]
    tokens, width = x.shape
    heads = width // 2
    steps = 4
    cols = wg.shape[1] // steps
    used = [0]

    def copy(source, target):
        made = pltpu.make_async_copy(source, target, sems.at[used[0]])
        used[0] += 1
        made.start()
        return made

    chunks = [slice(t * PIECE, (t + 1) * PIECE) for t in range(GROUP)]
    unit = [2 * ((3 - step) ^ s[OWN_B]) + core for step in range(steps)]

    wo_copies = [
        copy(
            wo_hbm.at[pl.ds(pl.multiple_of(place * heads + head * HEAD_FEATURES, HEAD_FEATURES), HEAD_FEATURES), :],
            wo.at[at * heads + index * HEAD_FEATURES : at * heads + (index + 1) * HEAD_FEATURES, :],
        )
        for at, place in enumerate((core, 1 - core))
        for index, head in enumerate(HEAD_ORDER)
    ]
    token_copies = [
        [
            copy(x_hbm.at[rows, :], x.at[rows, :]),
            copy(attn_hbm.at[rows, :], attn.at[rows, :heads]),
            copy(attn_pair_hbm.at[rows, :], attn.at[rows, heads:]),
        ]
        for rows in chunks
    ]
    def weights_of(step):
        at = pl.ds(pl.multiple_of(unit[step] * cols, cols), cols)
        here = slice(step * cols, (step + 1) * cols)
        return [
            copy(wg_hbm.at[:, at], wg.at[:, here]),
            copy(wu_hbm.at[:, at], wu.at[:, here]),
            copy(wd_hbm.at[at, :], wd.at[here, :]),
        ]

    dy_copies = [
        copy(source, dyb.at[piece_rows(half, place), :])
        for source, half, place in (
            (dy_hbm.at[s[CHIP]], s[CHIP], core),
            (dy_pair_hbm.at[s[CHIP]], s[CHIP], 1 - core),
            (dy_far_hbm.at[0], s[OTHER_CHIP], core),
            (dy_far_pair_hbm.at[0], s[OTHER_CHIP], 1 - core),
        )
    ]
    out_copies = []

    for made in wo_copies:
        made.wait()
    scale = gain[1:2, :].astype(f32)
    weight_copies = [weights_of(0)]
    for t, rows in enumerate(chunks):
        for made in token_copies[t]:
            made.wait()
        h = x[rows, :].astype(f32) + mm(attn[rows, :], wo[...])
        hidden[rows, :] = h
        hidden_low[rows, :] = h.astype(bf16)
        out_copies.append(copy(hidden_low.at[rows, :], hidden_out.at[rows, :]))
        r = lax.rsqrt(jnp.mean(h * h, axis=-1, keepdims=True) + epsilon)
        low[rows, :] = (h * r * scale).astype(bf16)
    low_t[...] = jnp.transpose(low[...])
    for made in dy_copies:
        made.wait()
    for t, rows in enumerate(chunks):
        dyb[rows, :] = jnp.where(slots(t * PIECE) < s[LENGTH], dyb[rows, :], jnp.zeros((), bf16))
    dyb_t[...] = jnp.transpose(dyb[...])
    out_copies.append(copy(dyb, dyb_out))

    def products(step, t):
        if t == 0:
            for made in weight_copies.pop():
                made.wait()
            if step + 1 < steps:
                weight_copies.append(weights_of(step + 1))
        rows, here = chunks[t], slice(step * cols, (step + 1) * cols)
        return mm(low[rows, :], wg[:, here]), mm(low[rows, :], wu[:, here]), mm_nt(dyb[rows, :], wd[here, :])

    def pointwise(step, t, gate, up, dact):
        rows, here = chunks[t], slice(step * cols, (step + 1) * cols)
        sig = 1.0 / (1.0 + jnp.exp2(gate * -LOG2E))
        silu = gate * sig
        acts[rows, here] = (silu * up).astype(bf16)
        dgs[rows, here] = (dact * up * (sig + silu * (1.0 - sig))).astype(bf16)
        dus[rows, here] = (dact * silu).astype(bf16)

    def emit(grad, own, write):
        total[...] = grad
        rows = width // 4
        for b in range(4):
            write(b // 2, b % 2, total[pl.ds(pl.multiple_of((b ^ own) * rows, 16), rows), :].astype(bf16))

    def weight_grads(step, which):
        here = slice(step * cols, (step + 1) * cols)
        if which == 0:
            grad = mm(low_t[...], dgs[:, here])
        elif which == 1:
            grad = mm(low_t[...], dus[:, here])
        else:
            grad = mm(dyb_t[...], acts[:, here])
        if not packed:
            at = pl.ds(pl.multiple_of(unit[step] // 2 * cols, cols), cols)
            blocks[which][:, here] = grad.astype(bf16)
            out_copies.append(copy(blocks[which].at[:, here], grads_out[which].at[:, at]))
            return
        y, x_side = (3 - step) // 2, (3 - step) % 2
        if which == 0:
            target, target_out = (blocks[0], grads_out[0]) if x_side else (blocks[1], grads_out[1])

            def write(z1, z0, value):
                target[y, z0, z1] = value

            emit(grad, s[OWN_Z], write)
            out_copies.append(copy(target.at[y], target_out.at[y]))
        elif which == 1:
            target, target_out = (blocks[2], grads_out[2]) if y else (blocks[3], grads_out[3])

            def write(z1, z0, value):
                target[z0, z1, x_side] = value

            emit(grad, s[OWN_Z], write)
            out_copies.append(copy(target.at[:, :, x_side], target_out.at[:, :, x_side]))
        else:
            z = (unit[step] // 2) ^ s[OWN_Z]

            def write(y, x, value):
                @pl.when(z % 2 == 1)
                def _():
                    blocks[4][x, z // 2, y] = value

                @pl.when(z % 2 == 0)
                def _():
                    blocks[5][x, z // 2, y] = value

            emit(grad, s[OWN_B], write)
            if step == steps - 1:
                for at in (4, 5):
                    out_copies.append(copy(blocks[at], grads_out[at]))

    units = [(step, t) for step in range(steps) for t in range(GROUP)]
    ahead = products(*units[0])
    for index, (step, t) in enumerate(units):
        now = ahead
        if index + 1 < len(units):
            ahead = products(*units[index + 1])
        pointwise(step, t, *now)
        if step and t < 3:
            weight_grads(step - 1, t)
    for which in range(3):
        weight_grads(steps - 1, which)
    for rows in chunks:
        dn[rows, :] = (mm_nt(dgs[rows, :], wg[...]) + mm_nt(dus[rows, :], wu[...])).astype(bf16)
        out_copies.append(copy(dn.at[rows, :], dn_out.at[rows, :]))
    for half in range(2):
        send[half] = mm(acts[piece_rows(half, 1 - core), :], wd[...]).astype(bf16)
        out_copies.append(copy(send.at[half], send_out.at[half]))
    for half in range(2):
        rows = piece_rows(half, core)
        layer[half] = hidden[rows, :] + mm(acts[rows, :], wd[...])
        out_copies.append(copy(layer.at[half], layer_out.at[half]))
    for made in out_copies:
        made.wait()


def feed(scalars, x, dy, dy_pair, dy_far, dy_far_pair, attn, attn_pair, wo, gain, wg, wu, wd, packed):
    tokens, width = x.shape
    units = wg.shape[1] // 2
    cols = units // 4
    token_shape = (2, PIECE, width)
    if packed:
        shapes = [(2, 2, 2, width // 4, cols)] * 6
    else:
        shapes = [(width, units)] * 3
    outs = [
        sds((tokens, width), bf16),
        sds((tokens, width), bf16),
        sds((tokens, width), bf16),
        sds(token_shape, f32),
        sds(token_shape, bf16),
    ] + [sds(a, bf16) for a in shapes]
    args = [x, dy, dy_pair, dy_far, dy_far_pair, attn, attn_pair, wo, gain, wg, wu, wd]
    in_specs = [pl.BlockSpec(memory_space=pl.ANY)] * len(args)
    in_specs[8] = whole((2, width))
    low = pltpu.VMEM((tokens, width), bf16)
    high = pltpu.VMEM((tokens, width), f32)
    turned = pltpu.VMEM((width, tokens), bf16)
    hidden_units = pltpu.VMEM((tokens, units), bf16)
    return call(
        functools.partial(feed_body, packed),
        (1,),
        in_specs,
        [pl.BlockSpec(memory_space=pl.ANY)] * len(outs),
        outs,
        scratch=[
            low,
            low,
            pltpu.VMEM((width, width), bf16),
            pltpu.VMEM((width, units), bf16),
            pltpu.VMEM((width, units), bf16),
            pltpu.VMEM((units, width), bf16),
            low,
            high,
            low,
            low,
            turned,
            turned,
            hidden_units,
            hidden_units,
            hidden_units,
            pltpu.VMEM((width, cols), f32),
            low,
            pltpu.VMEM(token_shape, f32),
            pltpu.VMEM(token_shape, bf16),
        ]
        + [pltpu.VMEM(a, bf16) for a in shapes]
        + [pltpu.SemaphoreType.DMA((80,))],
    )(scalars, *args)


def piece_of(half, side):
    return pl.ds(pl.multiple_of((2 * half + side) * PIECE, PIECE), PIECE)


def finish_body(s, x, keep, recv, dh, gain, stay, leave):
    scale = gain[0:1, :].astype(f32)
    for out, half in ((leave, s[OTHER_CHIP]), (stay, s[CHIP])):
        h = x[half, 0].astype(f32)
        there = jnp.concatenate([recv[piece_of(half, side), :] for side in range(2)], axis=1)
        dn = keep[half].astype(f32) + there.astype(f32)
        r = lax.rsqrt(jnp.mean(h * h, axis=-1, keepdims=True) + epsilon)
        scaled = dn * scale
        inner = jnp.mean(scaled * h, axis=-1, keepdims=True)
        out[...] = (dh[half, 0].astype(f32) + r * scaled - h * (r * r * r) * inner).astype(bf16)


def finish(scalars, x, keep, recv, dh, gain):
    width = x.shape[1]
    shape = (2, PIECE, width)
    own = pl.BlockSpec((2, 1, PIECE, width), lambda f, s: (0, s[CORE], 0, 0))
    return call(
        finish_body,
        (1,),
        [own, whole(shape), whole((MAXLEN, recv.shape[1])), own, whole((2, width))],
        [whole((PIECE, width))] * 2,
        [sds((PIECE, width), bf16)] * 2,
    )(scalars, x.reshape(2, 2, PIECE, width), keep, recv, dh.reshape(2, 2, PIECE, width), gain)


def decode(coded):
    return coded[:8].astype(f32) + coded[8:].astype(f32)


def encode(value):
    high = value.astype(bf16)
    return jnp.concatenate([high, (value - high.astype(f32)).astype(bf16)], axis=0)


def sum_parts(fetch, groups, scratch):
    loads = []
    for group in groups:
        loads.append([])
        for source in group:
            target = scratch.pop(0)
            loads[-1].append((fetch(source, target), target))

    def total(group):
        value = None
        for made, target in group:
            made.wait()
            part = target[...].astype(f32)
            value = part if value is None else value + part
        return value

    return [functools.partial(total, group) for group in loads]


def fetcher(sems):
    used = [0]

    def fetch(source, target):
        made = pltpu.make_async_copy(source, target, sems.at[used[0]])
        used[0] += 1
        made.start()
        return made

    return fetch


def feed_step_body(paths, s, *refs):
    refs = list(refs)
    groups = [[refs.pop(0).at[path] for path in group] for group in paths]
    outs = [refs.pop(0) for _ in groups]
    sems = refs.pop()
    for out, total in zip(outs, sum_parts(fetcher(sems), groups, refs)):
        out[...] = total().astype(bf16)


def feed_step(scalars, reductions):
    groups = [r.paths(1) for r in reductions]
    args = [array for group in groups for array, _ in group]
    paths = [[path for _, path in group] for group in groups]
    slices = [array.shape[len(path) :] for group in groups for array, path in group]
    outs = [sds(group[0][0].shape[len(group[0][1]) :], bf16) for group in groups]
    return call(
        functools.partial(feed_step_body, paths),
        (1,),
        [pl.BlockSpec(memory_space=pl.ANY)] * len(args),
        [whole(a.shape) for a in outs],
        outs,
        scratch=[pltpu.VMEM(a, bf16) for a in slices] + [pltpu.SemaphoreType.DMA((len(args),))],
    )(scalars, *args)


def third_step_body(paths, s, keep_hbm, arrived_hbm, gains, *refs):
    refs = list(refs)
    groups = [[refs.pop(0).at[path] for path in group] for group in paths]
    parts_hbm = [refs.pop(0) for _ in range(4)]
    plane = [refs.pop(0) for _ in range(4)]
    line_send, line_keep = refs.pop(0), refs.pop(0)
    sends, kept = [refs.pop(0) for _ in range(3)], refs.pop(0)
    keep, arrived = refs.pop(0), refs.pop(0)
    parts = [refs.pop(0) for _ in range(4)]
    sems = refs.pop()
    fetch = fetcher(sems)
    rows = keep.shape[0] // 8
    first = [
        fetch(keep_hbm, keep),
        fetch(arrived_hbm.at[pl.ds(MAXLEN, arrived.shape[0]), :], arrived),
    ]
    second = [fetch(source, target) for source, target in zip(parts_hbm, parts)]
    totals = sum_parts(fetch, groups, refs)
    for made in first:
        made.wait()
    plane_blocks(s, keep, arrived, plane, rows, False)
    coded = encode(decode(gains[...]) + decode(arrived[8 * rows :, :]))
    for target in plane:
        target[4 * rows :, :] = coded
    for made in second:
        made.wait()
    size = line_keep.shape[0] // 2
    own = s[OWN_Z] % 2
    for target, z0 in ((line_send, 1 - own), (line_keep, own)):
        for z1 in range(2):
            at = pl.ds(pl.multiple_of((2 * z1 + z0) * size, 16), size)
            total = None
            for part in parts:
                value = part[at, :].astype(f32)
                total = value if total is None else total + value
            target[z1 * size : (z1 + 1) * size, :] = total.astype(bf16)
    for index in range(3):
        sends[index][...] = totals[index]().astype(bf16)
        kept[index] = totals[3 + index]()


def third_step(scalars, keep, arrived, gains, parts, reductions):
    groups = [r.paths(1) for r in reductions] + [r.paths(0) for r in reductions]
    sums = [array for group in groups for array, _ in group]
    paths = [[path for _, path in group] for group in groups]
    slices = [array.shape[len(path) :] for group in groups for array, path in group]
    rows, columns = keep.shape
    outs = [sds((rows // 2 + 16, columns), bf16)] * 4
    outs += [sds((parts[0].shape[0] // 2, columns), bf16)] * 2
    outs += [sds(slices[0], bf16)] * 3 + [sds((3,) + slices[0], f32)]
    hbm = pl.BlockSpec(memory_space=pl.ANY)
    return call(
        functools.partial(third_step_body, paths),
        (1,),
        [hbm, hbm, whole(gains.shape)] + [hbm] * (len(sums) + 4),
        [whole(a.shape) for a in outs],
        outs,
        scratch=[pltpu.VMEM(keep.shape, bf16), pltpu.VMEM((rows + 16, columns), bf16)]
        + [pltpu.VMEM(a.shape, bf16) for a in parts]
        + [pltpu.VMEM(a, bf16) for a in slices]
        + [pltpu.SemaphoreType.DMA((len(sums) + 6,))],
    )(scalars, keep, arrived, gains, *sums, *parts)


def second_line_body(s, *refs):
    middle, last, (keep0, arrived0), outs = refs[:4], refs[4:8], refs[8:10], refs[10:]
    rows = middle[0].shape[0] // 4
    coded = [ref[4 * rows :, :] for ref in last]
    gains = encode((decode(coded[0]) + decode(coded[1])) + (decode(coded[2]) + decode(coded[3])))
    for r, target in enumerate(outs[:4]):
        at = pl.ds(pl.multiple_of((s[OWN_Z] ^ r) * rows, 16), rows)
        for index, parts in enumerate((middle, last)):
            total = None
            for part in parts:
                value = part[at, :].astype(f32)
                total = value if total is None else total + value
            target[index * rows : (index + 1) * rows, :] = total.astype(bf16)
        target[2 * rows :, :] = gains
    size = keep0.shape[0] // 2
    own = s[OWN_Z] // 2
    for target, z1 in ((outs[4], own), (outs[5], 1 - own)):
        at = pl.ds(pl.multiple_of(z1 * size, 16), size)
        target[...] = (keep0[at, :].astype(f32) + arrived0[at, :].astype(f32)).astype(bf16)


def second_line(scalars, middle, last, keep0, arrived0):
    rows, columns = middle[0].shape[0] // 4, middle[0].shape[1]
    outs = [sds((2 * rows + 16, columns), bf16)] * 4 + [sds((keep0.shape[0] // 2, columns), bf16)] * 2
    args = [*middle, *last, keep0, arrived0]
    return call(
        second_line_body,
        (1,),
        [whole(a.shape) for a in args],
        [whole(a.shape) for a in outs],
        outs,
    )(scalars, *args)


def feed_total_body(s, keep, gate, up, down, side_keep, side_send, down_out):
    rows = side_keep.shape[1]
    for index in range(2):
        value = keep[index] + (gate, up)[index][...].astype(f32)
        for part in range(2):
            block = value[part * rows : (part + 1) * rows]

            @pl.when(s[CORE] == part)
            def _():
                side_keep[index] = block

            @pl.when(s[CORE] != part)
            def _():
                side_send[index] = block.astype(bf16)

    down_out[...] = keep[2] + down[...].astype(f32)


def feed_total(scalars, keep, arrived):
    rows, cols = keep.shape[1:]
    outs = [sds((2, rows // 2, cols), f32), sds((2, rows // 2, cols), bf16), sds((rows, cols), f32)]
    args = [keep, *arrived]
    return call(
        feed_total_body,
        (1,),
        [whole(a.shape) for a in args],
        [whole(a.shape) for a in outs],
        outs,
    )(scalars, *args)


def shards_body(s, keep0, arrived0, line0, line1, line2, line3, side_keep, side_arrived, stay, back, *outs):
    half, width = outs[0].shape[0] // 2, outs[0].shape[1]
    first = keep0[...].astype(f32) + arrived0[...].astype(f32)
    rest = (line0[...].astype(f32) + line1[...].astype(f32)) + (line2[...].astype(f32) + line3[...].astype(f32))
    out = first[half:]
    outs[3][:half, :] = out[:, :width]
    outs[3][half:, :] = out[:, width:]
    for pair, part in enumerate((first[:half], rest[:half], rest[half : 2 * half])):
        lanes = slice(pair * HEAD_FEATURES, (pair + 1) * HEAD_FEATURES)
        for m in range(3):
            at = m * PAIR
            outs[m][:half, lanes] = part[:, at : at + HEAD_FEATURES]
            outs[m][half:, lanes] = part[:, at + HEAD_FEATURES : at + PAIR]
    gains = rest[2 * half : 2 * half + 8] + rest[2 * half + 8 :]
    for index in range(2):
        row = jnp.concatenate([gains[2 * index : 2 * index + 1], gains[2 * index + 1 : 2 * index + 2]], axis=1)
        for at in range(outs[6].shape[0]):
            outs[6 + index][at : at + 1, :] = row[:, at * PAIR : (at + 1) * PAIR]
    cols = side_keep.shape[2]
    for index in range(2):
        for core in range(2):

            @pl.when(s[CORE] == core)
            def _():
                outs[4 + index][:, core * cols : (core + 1) * cols] = side_keep[index]
                outs[4 + index][:, (1 - core) * cols : (2 - core) * cols] = side_arrived[index].astype(f32)

    outs[8][s[CHIP]] = stay[...]
    outs[8][s[OTHER_CHIP]] = back[...]


def make_shards(scalars, args, rows, columns, width):
    side = sds((rows, 2 * args[6].shape[-1]), f32)
    outs = [sds((rows, columns), f32)] * 4 + [side] * 2 + [sds((width // PAIR, PAIR), f32)] * 2
    outs.append(sds((2,) + args[-1].shape, bf16))
    return call(
        shards_body,
        (1,),
        [whole(a.shape) for a in args],
        [whole(a.shape) for a in outs],
        outs,
    )(scalars, *args)


def exchange_by(block, axis, difference, name):
    count = lax.axis_size(axis)
    with jax.named_scope(name):
        return lax.ppermute(block, axis, [(a, a ^ difference) for a in range(count)])


def exchange(block, axis, bit, name="swap"):
    return exchange_by(block, axis, 1 << bit, name)


def pick(block, index, dim):
    return lax.dynamic_index_in_dim(block, index, dim, keepdims=False)


def together(*values):
    return lax.optimization_barrier(values)


X, Y, Z0, Z1 = ("batch", 0), ("batch", 1), ("seq", 1), ("seq", 2)


class Reduction:
    def __init__(self, order, keep, send):
        self.order, self.level, self.send, self.parts = order, 0, send, [keep]

    def go(self):
        bit = self.order[self.level]
        self.arrived = exchange(self.send, *bit, "feed_" + "_".join(map(str, bit)))
        return self

    def paths(self, side):
        found = []
        for index, array in enumerate([*self.parts, self.arrived]):
            found.append((array, (0,) * (self.level - max(index - 1, 0)) + (side,)))
        return found

    def next(self, send):
        self.parts.append(self.arrived)
        self.send = send
        self.level += 1
        return self


def start_all(reductions, *others):
    sends = together(*[r.send for r in reductions], *others)
    for r, send in zip(reductions, sends):
        r.send = send
        r.go()
    return sends[len(reductions) :]


def wait_all(reductions, *others):
    values = together(*[r.arrived for r in reductions], *others)
    for r, arrived in zip(reductions, values):
        r.arrived = arrived
    return values[len(reductions) :]


def body(
    states,
    lengths,
    first_gain,
    query_weight,
    key_weight,
    value_weight,
    output_weight,
    second_gain,
    gate_weight,
    up_weight,
    down_weight,
    cotangent,
):
    tokens, width = states.shape
    n_seq, n_batch = lax.axis_size("seq"), lax.axis_size("batch")
    packed = n_seq == 8 and n_batch == 4
    place = lax.axis_index("seq")
    batch = lax.axis_index("batch")
    core = place & 1
    chip = place >> 1 & 1
    sequence = (batch * (n_seq // GROUP) + place // GROUP) * 2 + chip
    length = pick(lengths, sequence, 0)
    own_b, own_z = batch & 3, place >> 1 & 3
    scalars = jnp.stack([core, chip, length, 1 - chip, own_b, own_z]).astype(jnp.int32)
    table = jnp.asarray(rope_tables())
    both_gains = jnp.stack([first_gain, second_gain])
    weights = (query_weight, key_weight, value_weight)

    held = states.reshape(2, PIECE, width)
    held_back = cotangent.reshape(2, PIECE, width)
    far = exchange(pick(held, 1 - chip, 0), *Z0, "states_far")[None]
    held_pair = exchange(held, "seq", 0, "states_pair")
    filled = project(scalars, held, held_pair, CHIP, both_gains, weights, table, None)
    far, leaving, *filled = together(far, pick(held_back, 1 - chip, 0), *filled)
    far_pair = exchange(far, "seq", 0, "states_far_pair")
    back_far = exchange(leaving, *Z0, "cotangent_far")[None]
    back_pair = exchange(held_back, "seq", 0, "cotangent_pair")
    qkv, normed, x = project(scalars, far, far_pair, OTHER_CHIP, both_gains, weights, table, filled)
    attn, lse = attend(scalars, qkv)
    attn_pair = exchange(attn, "seq", 0, "attn_pair")
    back_far, attn = together(back_far, attn)
    back_far_pair = exchange(back_far, "seq", 0, "cotangent_far_pair")
    hidden, dyb, dn, layer_keep, layer_send, *feed_grads = feed(
        scalars,
        x,
        held_back,
        back_pair,
        back_far,
        back_far_pair,
        attn,
        attn_pair,
        output_weight,
        both_gains,
        gate_weight,
        up_weight,
        down_weight,
        packed,
    )
    if packed:
        gate_send, gate_keep, up_send, up_keep, down_send, down_keep = feed_grads
        gate = Reduction([X, Y, Z0, Z1], gate_keep, gate_send).go()
        up = Reduction([Y, Z0, Z1, X], up_keep, up_send).go()
        down = Reduction([Z0, X, Z1, Y], down_keep, down_send).go()
    dn_pair = exchange(dn, "seq", 0, "dn_pair")
    layer_arrived = exchange(layer_send, "seq", 0, "layer_pair")

    def back(pair, given, later, sent=()):
        return attend_back(
            pair, scalars, qkv, attn, lse, given, output_weight, weights, normed, table, later, n_seq, sent
        )

    keep0, send0, dhb, second, layer_stay, layer_leave, d0 = back(
        0, [hidden, dyb, dn, dn_pair, both_gains, layer_keep, layer_arrived], []
    )

    def in_order(kept, arrived):
        return jnp.concatenate(
            [jnp.where(chip == 0, kept, arrived), jnp.where(chip == 0, arrived, kept)], axis=0
        )

    if packed:
        rows = width // n_seq // 2

        def to_plane(parts, name):
            return [parts[0]] + [exchange_by(parts[r], "batch", r, name + str(r)) for r in (1, 2, 3)]

        feeds = [gate, up, down]
        keep0, send0, dhb, second, layer_stay, layer_leave, d0 = wait_all(
            feeds, keep0, send0, dhb, second, layer_stay, layer_leave, d0
        )
        arrived0 = exchange(send0, "seq", 0, "grad0_pair")
        layer_back = exchange(layer_leave, *Z0, "layer_back")
        for r, send in zip(feeds, feed_step(scalars, feeds)):
            r.next(send)
        (dhb,) = start_all(feeds, dhb)
        keep1, send1, d1, *plane0 = back(1, [dhb], [], (keep0, arrived0))

        layer_back, keep1, send1, d1, *plane0 = wait_all(feeds, layer_back, keep1, send1, d1, *plane0)
        arrived1 = exchange(send1, "seq", 0, "grad1_pair")
        flow0 = to_plane(plane0, "plane0_")
        for r, send in zip(feeds, feed_step(scalars, feeds)):
            r.next(send)
        (arrived1, d1) = start_all(feeds, arrived1, d1)
        keep2, norm_keep, norm_send, gains, layer_out, *plane1 = back(
            2, [dhb], [d0, d1, layer_stay, layer_back, x, second], (keep1, arrived1)
        )

        flow0[1], flow0[2], flow0[3], keep2, norm_keep, norm_send, gains, layer_out, *plane1 = wait_all(
            feeds, *flow0[1:], keep2, norm_keep, norm_send, gains, layer_out, *plane1
        )
        layer_out = layer_out.reshape(tokens, width)
        norm_arrived = exchange(norm_send, "seq", 0, "dn1_pair")
        flow1 = to_plane(plane1, "plane1_")
        *plane2, line0_send, line0_keep, gate_send, up_send, down_send, feed_keep = third_step(
            scalars, keep2, norm_arrived, gains, flow0, feeds
        )
        flow2 = to_plane(plane2, "plane2_")
        arrived0 = exchange(line0_send, *Z0, "line0")
        for r, send in zip(feeds, (gate_send, up_send, down_send)):
            r.next(send).go()
        stay, leave = finish(scalars, x, norm_keep, norm_arrived, dhb, both_gains)
        grad_back = exchange(leave, *Z0, "grad_back")
        stay, line0_keep, arrived0, *flow12 = together(stay, line0_keep, arrived0, *flow1, *flow2)
        flow1, flow2 = flow12[:4], flow12[4:]
        *lines, last_keep, last_send = second_line(scalars, flow1, flow2, line0_keep, arrived0)
        lines = [lines[0]] + [exchange_by(lines[r], "seq", 2 * r, "line12_" + str(r)) for r in (1, 2, 3)]
        last_arrived = exchange(last_send, *Z1, "line0_last")
        (last_keep,) = wait_all(feeds, last_keep)
        side_keep, side_send, down_grad = feed_total(scalars, feed_keep, [r.arrived for r in feeds])
        down_grad = jnp.transpose(down_grad)
        side_arrived = exchange(side_send, "seq", 0, "feed_pair")
        *shards, gate_grad, up_grad, first, second, input_grad = make_shards(
            scalars,
            [last_keep, last_arrived, *lines, side_keep, side_arrived, stay, grad_back],
            2 * rows,
            width // n_batch,
            width,
        )
        first, second, input_grad = first.reshape(width), second.reshape(width), input_grad.reshape(tokens, width)
    else:
        keep1, _, d1 = back(1, [dhb], [])
        layer_back = exchange(layer_leave, *Z0)
        keep2, _, norm_keep, norm_send, gains, layer_out = back(2, [dhb], [d0, d1, layer_stay, layer_back, x, second])
        norm_arrived = exchange(norm_send, "seq", 0)
        stay, leave = finish(scalars, x, norm_keep, norm_arrived, dhb, both_gains)
        layer_out = layer_out.reshape(tokens, width)
        input_grad = in_order(stay, exchange(leave, *Z0))
        gains = gains[:8].astype(f32) + gains[8:].astype(f32)
        for axis in ("seq", "batch"):
            for bit in range(int(math.log2(lax.axis_size(axis)))):
                gains = gains + exchange(gains, axis, bit)
        first, second = gains[:2].reshape(width), gains[2:4].reshape(width)
        gate_keep, up_keep, down_keep = feed_grads
        units = gate_keep.shape[1]
        zeros = lambda shape: jnp.zeros(shape, bf16)
        blocks = 4

        def spread(array):
            parts = array.reshape(width, blocks, 1, units // blocks)
            full = zeros((width, blocks, 2, units // blocks))
            return lax.dynamic_update_slice_in_dim(full, parts, core, 2).reshape(width, 2 * units)

        heads = attn.shape[1]
        out_keep = jnp.concatenate([keep0[width : width + heads], keep0[width + heads :]], axis=1)
        columns = lambda a: lax.dynamic_update_slice_in_dim(zeros((width, width)), a, core * heads, 1)

        def by_head(m):
            found = {}
            for index, head in enumerate(HEAD_ORDER):
                at = m * PAIR + index % 2 * HEAD_FEATURES
                found[head] = (keep0, keep1, keep2)[index // 2][:width, at : at + HEAD_FEATURES]
            return jnp.concatenate([found[head] for head in sorted(found)], axis=1)

        full = [columns(by_head(m)) for m in range(3)]
        full.append(lax.dynamic_update_slice_in_dim(zeros((width, width)), out_keep, core * heads, 0))
        full += [spread(gate_keep), spread(up_keep), jnp.transpose(spread(down_keep))]
        full = [lax.psum_scatter(a.astype(f32), "seq", scatter_dimension=0, tiled=True) for a in full]
        full = [lax.psum_scatter(a, "batch", scatter_dimension=1, tiled=True) for a in full]
        shards, (gate_grad, up_grad, down_grad) = full[:4], full[4:]

    return (
        layer_out,
        input_grad,
        first,
        shards[0],
        shards[1],
        shards[2],
        shards[3],
        second,
        gate_grad,
        up_grad,
        down_grad,
    )


def solution(mesh):
    split = P(("batch", "seq"), None)
    in_specs = (split,) + (P(),) * 10 + (split,)
    shard = P("seq", "batch")
    out_specs = (split, split, P(), shard, shard, shard, shard, P(), shard, shard, shard)
    return jax.shard_map(body, mesh=mesh, in_specs=in_specs, out_specs=out_specs, check_vma=False)
```

time: 216 us -> 196 us (0.907)
  waiting for transfers between devices: 55.2 us -> 24.9 us
  Pallas kernels: 95 us -> 122 us
  other arithmetic: 13.7 us -> 0.59 us
  local copies, waits for them, and re-layouts: 12.4 us -> 7.37 us
    ppermute x44 -> x41, waiting for transfers between devices: 55.2 us -> 24.9 us  [exchange_by(): lax.ppermute(block, axis, [(a, a ^ difference) for a in range(count)])]
    pallas_call x4 -> x11, Pallas kernels: 75 us -> 102 us  [the longest x1 38.6 us: feed(): call(functools.partial(feed_body, packed), (1,), in_specs, [pl.BlockSpec(...]
    convert_element_type x23 -> x0, other arithmetic: 5.08 us -> none  [the longest x10 4.36 us: take(): parts.append((a + b).astype(bf16))]
    unnamed x48 -> x0, local copies, waits for them, and re-layouts: 4.5 us -> none
    reshape x4 -> x0, local copies, waits for them, and re-layouts: 3.15 us -> none  [the longest x2 1.31 us: body(): two = lambda a: a.reshape((a.shape[0], 2, 2) + a.shape[2:])]
    concatenate x5 -> x0, other arithmetic: 2.94 us -> none  [the longest x2 1.86 us: in_order(): jnp.concatenate([jnp.where(chip == 0, kept, arrived), jnp.where(chip == 0...]
    squeeze x5 -> x2, local copies, waits for them, and re-layouts: 1.18 us -> 3.53 us  [pick(): return lax.dynamic_index_in_dim(block, index, dim, keepdims=False)]
    ppermute x44 -> x41, starting transfers between devices: 37.7 us -> 38.5 us  [exchange_by(): lax.ppermute(block, axis, [(a, a ^ difference) for a in range(count)])]
  transfers between devices with their start and end apart: 44 -> 41, of which waited for: 21 -> 13; matrix products, arithmetic and copies ran while one was open for 9% -> 4% of each run, Pallas kernels for 34% -> 41%
where the time goes in v3:
time: 196 us; the launch traced here: 194 us
  Pallas kernels  122 us (62%)
  starting transfers between devices  38.5 us (20%)
  waiting for transfers between devices  24.9 us (13%)
  local copies, waits for them, and re-layouts  7.37 us (4%)
    pallas_call x1, Pallas kernels, feed(): call(functools.partial(feed_body, packed), (1,), in_specs, [pl.BlockSpec(...  38.6 us
    ppermute x41, starting transfers between devices, exchange_by(): lax.ppermute(block, axis, [(a, a ^ difference) for a in range(count)])  38.5 us
    pallas_call x3, Pallas kernels, attend_back(): call(functools.partial(attend_back_body, pair, n_seq), (1,), in_specs, [w...  38.4 us
    ppermute x41, waiting for transfers between devices, exchange_by(): lax.ppermute(block, axis, [(a, a ^ difference) for a in range(count)])  24.9 us
    pallas_call x2, Pallas kernels, project(): call(project_body, (2,), in_specs, [pl.BlockSpec((PIECE, 3 * cols), place...  10.9 us
    pallas_call x1, Pallas kernels, attend(): call(attend_body, (pairs,), [spec(0), spec(1), spec(2)], [pl.BlockSpec((M...  8.99 us
    pallas_call x2, Pallas kernels, feed_step(): call(functools.partial(feed_step_body, paths), (1,), [pl.BlockSpec(memory...  6.39 us
    pallas_call x1, Pallas kernels, third_step(): call(functools.partial(third_step_body, paths), (1,), [hbm, hbm, whole(ga...  5.02 us
  transfers between devices with their start and end apart: 41, of which 13 were waited for; matrix products, arithmetic and copies ran while one was open for 4% of the time, Pallas kernels for 41%

profile of v3, /device:TPU:0, one launch (start us, length us, event | category | flops | bytes accessed | tf_op | source)
XLA Modules:
  0.0 194.0 jit_solution(659607436108977962)
XLA Ops:
  0.6 0.5 collective-permute-start.1
  1.2 1.8 dynamic-slice_bitcast_fusion.1
  2.9 2.6 %collective-permute-start = (bf16[256,768]{1,0:T(8,128)(2,1)}, bf16[256,768]{1,0:T(8,128)(2,1)}, u32[]{:S(2)}, u32[]{:S(2)}) collective-permute-start(bf16[256,768]{1,0:T(8,128)(2,1)} %dynamic-slice_bitcast_fusion.1), channel_id=1, source_target_pairs={{0,2},{1,3},{2,0},{3,1},{4,6},{5,7},{6,4},{7,5},{8,10},{9,11},{10,... | collective-permute-start | bytes 1179656 | tf_op jit(solution)/shard_map/states_far/ppermute | solution.py:1096
  5.5 0.7 stack.34
  6.2 0.7 stack.35
  6.9 1.2 dynamic_slice.11
  8.1 1.2 stack.33.s
  9.4 0.6 pad_maximum_fusion.gain.refs_7_
  10.0 1.8 dynamic-slice_bitcast_fusion
  11.7 5.5 %shard_map.212 = (bf16[1024,1152]{1,0:T(8,128)(2,1)}, bf16[1024,768]{1,0:T(8,128)(2,1)}, bf16[1024,768]{1,0:T(8,128)(2,1)}) custom-call(s32[6]{0:T(128)} %stack.33.s, bf16[2,256,768]{2,1,0:T(8,128)(2,1)} %bitcast.27, bf16[2,256,768]{2,1,0:T(8,128)(2,1)} %collective-permute-done.1.part, bf16[2,768]{1,0:T(2,128)(2,1)} %pad_maximum_fusion.gain.refs_7_, ...), custom_call_target="tpu_custom_call" | custom-call | flops 1000 | bytes 1000 | tf_op jit(solution)/shard_map/pallas_call | solution.py:151
  17.9 1.5 collective-permute-done.2.part
  19.3 5.4 %shard_map.213 = (bf16[1024,1152]{1,0:T(8,128)(2,1)}, bf16[1024,768]{1,0:T(8,128)(2,1)}, bf16[1024,768]{1,0:T(8,128)(2,1)}) custom-call(s32[6]{0:T(128)} %stack.33.s, bf16[1,256,768]{2,1,0:T(8,128)(2,1)} %bitcast.7.own, bf16[1,256,768]{2,1,0:T(8,128)(2,1)} %collective-permute-done.2.part, ...), custom_call_target="tpu_custom_call", output_to_operand_aliasing={{0}: (8, {}), {1}: (9, {}), {2}: (10, {})} | custom-call | flops 1000 | bytes 1000 | tf_op jit(solution)/shard_map/pallas_call | solution.py:151
  24.8 9.0 %shard_map.214 = (bf16[1024,384]{1,0:T(8,128)(2,1)}, f32[3,1024,128]{2,1,0:T(8,128)}) custom-call(s32[6]{0:T(128)} %stack.33.s, bf16[1024,1152]{1,0:T(8,128)(2,1)} %get-tuple-element.165.q.k.v.refs_0_, bf16[1024,1152]{1,0:T(8,128)(2,1)} %get-tuple-element.165.q.k.v.refs_0_, bf16[1024,1152]{1,0:T(8,128)(2,1)} %get-tuple-element.165.q.k.v.refs_0_), custom_call_target="tpu_custom_call" | custom-call | flops 1000 | bytes 1000 | tf_op jit(solution)/shard_map/pallas_call | solution.py:213
  33.9 0.3 collective-permute-start.5
  34.3 2.7 %collective-permute-done.5.dy_far_pair_hbm = bf16[1,256,768]{2,1,0:T(8,128)(2,1)} collective-permute-done((bf16[1,256,768]{2,1,0:T(8,128)(2,1)}, bf16[1,256,768]{2,1,0:T(8,128)(2,1)}, u32[]{:S(2)}, u32[]{:S(2)}) %collective-permute-start.5) | collective-permute-done | bytes 393248 | tf_op jit(solution)/shard_map/cotangent_far_pair/ppermute | solution.py:1096
  37.0 38.6 %shard_map.215 = (bf16[1024,768]{1,0:T(8,128)(2,1)}, bf16[1024,768]{1,0:T(8,128)(2,1)}, bf16[1024,768]{1,0:T(8,128)(2,1)}, f32[2,256,768]{2,1,0:T(8,128)}, bf16[...) custom-call(s32[6]{0:T(128)} %stack.33.s, ...), custom_call_target="tpu_custom_call" | custom-call | flops 1000 | bytes 1000 | tf_op jit(solution)/shard_map/pallas_call | solution.py:794
  75.8 0.3 collective-permute-start.11
  76.2 1.5 collective-permute-start.7
  77.6 1.5 collective-permute-start.8
  79.1 0.5 collective-permute-start.9
  79.6 0.9 collective-permute-done.11.refs_9_
  80.5 14.7 %shard_map.216 = (bf16[768,384]{1,0:T(8,128)(2,1)}, bf16[768,384]{1,0:T(8,128)(2,1)}, bf16[1024,768]{1,0:T(8,128)(2,1)}, f32[1,768]{1,0:T(1,128)}, bf16[256,768]...) custom-call(s32[6]{0:T(128)} %stack.33.s, bf16[1024,1152]{1,0:T(8,128)(2,1)} %get-tuple-element.165.q.k.v.refs_0_, ...), custom_call_target="tpu_custom_call" | custom-call | flops 1000 | bytes 1000 | tf_op jit(solution)/shard_map/pallas_call | solution.py:581
  95.2 0.9 collective-permute-done.7.refs_1_.refs_13_
  96.1 1.2 collective-permute-done.8.refs_3_.refs_4_.refs_5_.refs_17_
  97.3 1.3 collective-permute-done.9.refs_5_.refs_7_.refs_9_.refs_21_
  98.6 0.5 collective-permute-start.15
  99.1 3.3 %shard_map.217 = (bf16[2,2,192,256]{3,2,1,0:T(8,128)(2,1)}, bf16[2,2,192,256]{3,2,1,0:T(8,128)(2,1)}, bf16[2,2,192,256]{3,2,1,0:T(8,128)(2,1)}) custom-call(s32[6]{0:T(128)} %stack.33.s, bf16[2,2,2,192,256]{4,3,2,1,0:T(8,128)(2,1)} %get-tuple-element.169.refs_0_.refs_12_, bf16[2,2,2,192,256]{4,3,2,1,0:T(8,128)(2,1)} %collective-permute-done.7.refs_1_.refs_13_, ...), custom_call_target="tpu_custom_call" | custom-call | flops 1000 | bytes 1000 | tf_op jit(solution)/shard_map/pallas_call | solution.py:910
  102.4 0.5 collective-permute-start.12
  102.9 1.6 collective-permute-start.13
  104.5 0.5 collective-permute-start.14
  105.0 10.1 %shard_map.218 = (bf16[384,384]{1,0:T(8,128)(2,1)}, bf16[384,384]{1,0:T(8,128)(2,1)}, bf16[1024,384]{1,0:T(8,128)(2,1)}, bf16[384,384]{1,0:T(8,128)(2,1)}, bf16[...) custom-call(s32[6]{0:T(128)} %stack.33.s, ...), custom_call_target="tpu_custom_call" | custom-call | flops 1000 | bytes 1000 | tf_op jit(solution)/shard_map/pallas_call | solution.py:581
  115.2 3.7 %collective-permute-done.13.refs_5_.refs_6_.refs_18_ = bf16[2,2,192,256]{3,2,1,0:T(8,128)(2,1)} collective-permute-done((bf16[2,2,192,256]{3,2,1,0:T(8,128)(2,1)}, bf16[2,2,192,256]{3,2,1,0:T(8,128)(2,1)}, u32[]{:S(2)}, u32[]{:S(2)}) %collective-permute-start.13) | collective-permute-done | bytes 393248 | tf_op jit(solution)/shard_map/feed_seq_1/ppermute | solution.py:1096
  118.8 0.5 collective-permute-start.21
  119.4 0.5 collective-permute-start.22
  119.9 2.5 %collective-permute-start.23 = (bf16[384,384]{1,0:T(8,128)(2,1)}, bf16[384,384]{1,0:T(8,128)(2,1)}, u32[]{:S(2)}, u32[]{:S(2)}) collective-permute-start(bf16[384,384]{1,0:T(8,128)(2,1)} %get-tuple-element.223), channel_id=1, source_target_pairs={{0,24},{8,16},{16,8},{24,0},{1,25},{9,17},{17,9},{25,1},{2,26},{10... | collective-permute-start | bytes 884744 | tf_op jit(solution)/shard_map/plane0_3/ppermute | solution.py:1096
  122.3 3.1 %shard_map.219 = (bf16[2,192,256]{2,1,0:T(8,128)(2,1)}, bf16[2,192,256]{2,1,0:T(8,128)(2,1)}, bf16[2,192,256]{2,1,0:T(8,128)(2,1)}) custom-call(s32[6]{0:T(128)} %stack.33.s, bf16[2,2,2,192,256]{4,3,2,1,0:T(8,128)(2,1)} %get-tuple-element.169.refs_0_.refs_12_, bf16[2,2,2,192,256]{4,3,2,1,0:T(8,128)(2,1)} %collective-permute-done.7.refs_1_.refs_13_, ...), custom_call_target="tpu_custom_call" | custom-call | flops 1000 | bytes 1000 | tf_op jit(solution)/shard_map/pallas_call | solution.py:910
  125.4 0.6 collective-permute-start.18
  126.0 2.5 %collective-permute-start.19 = (bf16[2,192,256]{2,1,0:T(8,128)(2,1)}, bf16[2,192,256]{2,1,0:T(8,128)(2,1)}, u32[]{:S(2)}, u32[]{:S(2)}) collective-permute-start(bf16[2,192,256]{2,1,0:T(8,128)(2,1)} %get-tuple-element.219), channel_id=1, source_target_pairs={{0,4},{1,5},{2,6},{3,7},{4,0},{5,1},{6,2},{7,3},{8,12},{9,13},{10,... | collective-permute-start | bytes 589832 | tf_op jit(solution)/shard_map/feed_seq_2/ppermute | solution.py:1096
  128.5 0.5 collective-permute-done.21.refs_25_
  129.0 2.6 %collective-permute-start.20 = (bf16[2,192,256]{2,1,0:T(8,128)(2,1)}, bf16[2,192,256]{2,1,0:T(8,128)(2,1)}, u32[]{:S(2)}, u32[]{:S(2)}) collective-permute-start(bf16[2,192,256]{2,1,0:T(8,128)(2,1)} %get-tuple-element.220), channel_id=1, source_target_pairs={{0,4},{1,5},{2,6},{3,7},{4,0},{5,1},{6,2},{7,3},{8,12},{9,13},{10,... | collective-permute-start | bytes 589832 | tf_op jit(solution)/shard_map/feed_seq_2/ppermute | solution.py:1096
  131.5 13.6 %shard_map.220 = (bf16[384,384]{1,0:T(8,128)(2,1)}, bf16[2,256,768]{2,1,0:T(8,128)(2,1)}, bf16[1424,384]{1,0:T(8,128)(2,1)}, bf16[16,384]{1,0:T(8,128)(2,1)}, bf...) custom-call(s32[6]{0:T(128)} %stack.33.s, ...), custom_call_target="tpu_custom_call" | custom-call | flops 1000 | bytes 1000 | tf_op jit(solution)/shard_map/pallas_call | solution.py:581
  145.2 0.9 collective-permute-done.20.refs_11_.refs_23_
  146.1 0.5 collective-permute-start.29
  146.5 0.5 collective-permute-start.30
  147.1 2.5 %collective-permute-start.31 = (bf16[192,384]{1,0:T(8,128)(2,1)}, bf16[192,384]{1,0:T(8,128)(2,1)}, u32[]{:S(2)}, u32[]{:S(2)}) collective-permute-start(bf16[192,384]{1,0:T(8,128)(2,1)} %get-tuple-element.261), channel_id=1, source_target_pairs={{0,24},{8,16},{16,8},{24,0},{1,25},{9,17},{17,9},{25,1},{2,26},{10... | collective-permute-start | bytes 442376 | tf_op jit(solution)/shard_map/plane1_3/ppermute | solution.py:1096
  149.6 4.1 %shard_map.222 = (bf16[256,768]{1,0:T(8,128)(2,1)}, bf16[256,768]{1,0:T(8,128)(2,1)}) custom-call(s32[6]{0:T(128)} %stack.33.s, bf16[2,2,256,768]{3,2,1,0:T(8,128)(2,1)} %bitcast.20, bf16[2,256,768]{2,1,0:T(8,128)(2,1)} %get-tuple-element.254.keep, bf16[1424,384]{1,0:T(8,128)(2,1)} %collective-permute-done.24.arrived_hbm.recv, ...), custom_call_target="tpu_custom_call" | custom-call | flops 1000 | bytes 1000 | tf_op jit(solution)/shard_map/pallas_call | solution.py:846
  153.6 0.7 collective-permute-start.40
  154.3 5.0 %shard_map.221 = (bf16[208,384]{1,0:T(8,128)(2,1)}, bf16[208,384]{1,0:T(8,128)(2,1)}, bf16[208,384]{1,0:T(8,128)(2,1)}, bf16[208,384]{1,0:T(8,128)(2,1)}, bf16[1...) custom-call(s32[6]{0:T(128)} %stack.33.s, ...), custom_call_target="tpu_custom_call" | custom-call | flops 1000 | bytes 1000 | tf_op jit(solution)/shard_map/pallas_call | solution.py:971
  159.4 0.6 collective-permute-start.32
  160.0 0.5 collective-permute-start.33
  160.5 1.3 collective-permute-start.28
  161.8 2.5 %collective-permute-start.34 = (bf16[208,384]{1,0:T(8,128)(2,1)}, bf16[208,384]{1,0:T(8,128)(2,1)}, u32[]{:S(2)}, u32[]{:S(2)}) collective-permute-start(bf16[208,384]{1,0:T(8,128)(2,1)} %get-tuple-element.265), channel_id=1, source_target_pairs={{0,24},{8,16},{16,8},{24,0},{1,25},{9,17},{17,9},{25,1},{2,26},{10... | collective-permute-start | bytes 479240 | tf_op jit(solution)/shard_map/plane2_3/ppermute | solution.py:1096
  164.3 3.6 %collective-permute-done.28.refs_9_ = bf16[192,384]{1,0:T(8,128)(2,1)} collective-permute-done((bf16[192,384]{1,0:T(8,128)(2,1)}, bf16[192,384]{1,0:T(8,128)(2,1)}, u32[]{:S(2)}, u32[]{:S(2)}) %collective-permute-start.28) | collective-permute-done | bytes 147488 | tf_op jit(solution)/shard_map/line0/ppermute | solution.py:1096
  167.8 2.3 %collective-permute-start.25 = (bf16[192,256]{1,0:T(8,128)(2,1)}, bf16[192,256]{1,0:T(8,128)(2,1)}, u32[]{:S(2)}, u32[]{:S(2)}) collective-permute-start(bf16[192,256]{1,0:T(8,128)(2,1)} %get-tuple-element.251), channel_id=1, source_target_pairs={{0,4},{1,5},{2,6},{3,7},{4,0},{5,1},{6,2},{7,3},{8,12},{9,13},{10,... | collective-permute-start | bytes 294920 | tf_op jit(solution)/shard_map/feed_seq_2/ppermute | solution.py:1096
  170.2 0.6 collective-permute-start.26
  170.8 1.5 collective-permute-start.27
  172.3 3.0 %shard_map.223 = (bf16[112,384]{1,0:T(8,128)(2,1)}, bf16[112,384]{1,0:T(8,128)(2,1)}, bf16[112,384]{1,0:T(8,128)(2,1)}, bf16[112,384]{1,0:T(8,128)(2,1)}, bf16[9...) custom-call(s32[6]{0:T(128)} %stack.33.s, bf16[192,384]{1,0:T(8,128)(2,1)} %get-tuple-element.266.refs_0_, ...), custom_call_target="tpu_custom_call" | custom-call | flops 1000 | bytes 1000 | tf_op jit(solution)/shard_map/pallas_call | solution.py:1009
  175.3 0.4 collective-permute-done.27.down
  175.7 2.7 %shard_map.224 = (f32[2,96,256]{2,1,0:T(8,128)}, bf16[2,96,256]{2,1,0:T(8,128)(2,1)}, f32[192,256]{1,0:T(8,128)}) custom-call(s32[6]{0:T(128)} %stack.33.s, f32[3,192,256]{2,1,0:T(8,128)} %get-tuple-element.283.keep, bf16[192,256]{1,0:T(8,128)(2,1)} %collective-permute-done.25.gate, bf16[192,256]{1,0:T(8,128)(2,1)} %collective-permute-done.26.up, ...), custom_call_target="tpu_custom_call" | custom-call | flops 1000 | bytes 1000 | tf_op jit(solution)/shard_map/pallas_call | solution.py:1040
  178.4 1.7 collective-permute-start.36
  180.1 2.5 %collective-permute-start.37 = (bf16[112,384]{1,0:T(8,128)(2,1)}, bf16[112,384]{1,0:T(8,128)(2,1)}, u32[]{:S(2)}, u32[]{:S(2)}) collective-permute-start(bf16[112,384]{1,0:T(8,128)(2,1)} %get-tuple-element.281), channel_id=1, source_target_pairs={{0,4},{1,5},{2,6},{3,7},{4,0},{5,1},{6,2},{7,3},{8,12},{9,13},{10,... | collective-permute-start | bytes 258056 | tf_op jit(solution)/shard_map/line12_2/ppermute | solution.py:1096
  182.8 0.9 collective-permute-done.36.line1
  183.7 6.7 %collective-permute-done.37.line2 = bf16[112,384]{1,0:T(8,128)(2,1)} collective-permute-done((bf16[112,384]{1,0:T(8,128)(2,1)}, bf16[112,384]{1,0:T(8,128)(2,1)}, u32[]{:S(2)}, u32[]{:S(2)}) %collective-permute-start.37) | collective-permute-done | bytes 86048 | tf_op jit(solution)/shard_map/line12_2/ppermute | solution.py:1096
  190.3 3.5 %shard_map.225 = (f32[96,192]{1,0:T(8,128)}, f32[96,192]{1,0:T(8,128)}, f32[96,192]{1,0:T(8,128)}, f32[96,192]{1,0:T(8,128)}, f32[96,512]{1,0:T(8,128)}, /*index...) custom-call(s32[6]{0:T(128)} %stack.33.s, ...), custom_call_target="tpu_custom_call" | custom-call | flops 1000 | bytes 1000 | tf_op jit(solution)/shard_map/pallas_call | solution.py:1084
  (39 shorter events, 1.4 us)
Async XLA Ops:
  0.6 11.1 %collective-permute-start.1 = (bf16[2,256,768]{2,1,0:T(8,128)(2,1)}, bf16[2,256,768]{2,1,0:T(8,128)(2,1)}, u32[]{:S(2)}, u32[]{:S(2)}) collective-permute-start(bf16[2,256,768]{2,1,0:T(8,128)(2,1)} %bitcast.25), channel_id=1, source_target_pairs={{0,1},{1,0},{2,3},{3,2},{4,5},{5,4},{6,7},{7,6},{8,9},{9,8},{10,11... | collective-permute-start | bytes 2359304 | tf_op jit(solution)/shard_map/states_pair/ppermute | solution.py:1096
  2.9 14.3 %collective-permute-start = (bf16[256,768]{1,0:T(8,128)(2,1)}, bf16[256,768]{1,0:T(8,128)(2,1)}, u32[]{:S(2)}, u32[]{:S(2)}) collective-permute-start(bf16[256,768]{1,0:T(8,128)(2,1)} %dynamic-slice_bitcast_fusion.1), channel_id=1, source_target_pairs={{0,2},{1,3},{2,0},{3,1},{4,6},{5,7},{6,4},{7,5},{8,10},{9,11},{10,... | collective-permute-start | bytes 1179656 | tf_op jit(solution)/shard_map/states_far/ppermute | solution.py:1096
  17.2 2.1 %collective-permute-start.2 = (bf16[1,256,768]{2,1,0:T(8,128)(2,1)}, bf16[1,256,768]{2,1,0:T(8,128)(2,1)}, u32[]{:S(2)}, u32[]{:S(2)}) collective-permute-start(bf16[1,256,768]{2,1,0:T(8,128)(2,1)} %bitcast.7.own), channel_id=1, source_target_pairs={{0,1},{1,0},{2,3},{3,2},{4,5},{5,4},{6,7},{7,6},{8,9},{9,8},{10,11... | collective-permute-start | bytes 1179656 | tf_op jit(solution)/shard_map/states_far_pair/ppermute | solution.py:1096
  17.4 16.8 %collective-permute-start.3 = (bf16[2,256,768]{2,1,0:T(8,128)(2,1)}, bf16[2,256,768]{2,1,0:T(8,128)(2,1)}, u32[]{:S(2)}, u32[]{:S(2)}) collective-permute-start(bf16[2,256,768]{2,1,0:T(8,128)(2,1)} %bitcast.23), channel_id=1, source_target_pairs={{0,1},{1,0},{2,3},{3,2},{4,5},{5,4},{6,7},{7,6},{8,9},{9,8},{10,11... | collective-permute-start | bytes 2359304 | tf_op jit(solution)/shard_map/cotangent_pair/ppermute | solution.py:1096
  17.8 16.2 %collective-permute-start.4 = (bf16[256,768]{1,0:T(8,128)(2,1)}, bf16[256,768]{1,0:T(8,128)(2,1)}, u32[]{:S(2)}, u32[]{:S(2)}) collective-permute-start(bf16[256,768]{1,0:T(8,128)(2,1)} %dynamic-slice_bitcast_fusion), channel_id=1, source_target_pairs={{0,2},{1,3},{2,0},{3,1},{4,6},{5,7},{6,4},{7,5},{8,10},{9,11},{10,... | collective-permute-start | bytes 1179656 | tf_op jit(solution)/shard_map/cotangent_far/ppermute | solution.py:1096
  33.8 3.2 %collective-permute-start.6 = (bf16[1024,384]{1,0:T(8,128)(2,1)}, bf16[1024,384]{1,0:T(8,128)(2,1)}, u32[]{:S(2)}, u32[]{:S(2)}) collective-permute-start(bf16[1024,384]{1,0:T(8,128)(2,1)} %get-tuple-element.168.attn_hbm.refs_1_), channel_id=1, source_target_pairs={{0,1},{1,0},{2,3},{3,2},{4,5},{5,4},{6,7},{7,6},{8,9},{9,8},{10,11... | collective-permute-start | bytes 2359304 | tf_op jit(solution)/shard_map/attn_pair/ppermute | solution.py:1096
  33.9 3.0 %collective-permute-start.5 = (bf16[1,256,768]{2,1,0:T(8,128)(2,1)}, bf16[1,256,768]{2,1,0:T(8,128)(2,1)}, u32[]{:S(2)}, u32[]{:S(2)}) collective-permute-start(bf16[1,256,768]{2,1,0:T(8,128)(2,1)} %bitcast.10.dy_far_hbm), channel_id=1, source_target_pairs={{0,1},{1,0},{2,3},{3,2},{4,5},{5,4},{6,7},{7,6},{8,9},{9,8},{10,11... | collective-permute-start | bytes 1179656 | tf_op jit(solution)/shard_map/cotangent_far_pair/ppermute | solution.py:1096
  75.6 4.9 %collective-permute-start.10 = (bf16[1024,768]{1,0:T(8,128)(2,1)}, bf16[1024,768]{1,0:T(8,128)(2,1)}, u32[]{:S(2)}, u32[]{:S(2)}) collective-permute-start(bf16[1024,768]{1,0:T(8,128)(2,1)} %get-tuple-element.176.refs_5_), channel_id=1, source_target_pairs={{0,1},{1,0},{2,3},{3,2},{4,5},{5,4},{6,7},{7,6},{8,9},{9,8},{10,11... | collective-permute-start | bytes 4718600 | tf_op jit(solution)/shard_map/dn_pair/ppermute | solution.py:1096
  75.8 4.7 %collective-permute-start.11 = (bf16[2,256,768]{2,1,0:T(8,128)(2,1)}, bf16[2,256,768]{2,1,0:T(8,128)(2,1)}, u32[]{:S(2)}, u32[]{:S(2)}) collective-permute-start(bf16[2,256,768]{2,1,0:T(8,128)(2,1)} %get-tuple-element.178), channel_id=1, source_target_pairs={{0,1},{1,0},{2,3},{3,2},{4,5},{5,4},{6,7},{7,6},{8,9},{9,8},{10,11... | collective-permute-start | bytes 2359304 | tf_op jit(solution)/shard_map/layer_pair/ppermute | solution.py:1096
  76.2 19.9 %collective-permute-start.7 = (bf16[2,2,2,192,256]{4,3,2,1,0:T(8,128)(2,1)}, bf16[2,2,2,192,256]{4,3,2,1,0:T(8,128)(2,1)}, u32[]{:S(2)}, u32[]{:S(2)}) collective-permute-start(bf16[2,2,2,192,256]{4,3,2,1,0:T(8,128)(2,1)} %get-tuple-element.170), channel_id=1, source_target_pairs={{0,8},{8,0},{16,24},{24,16},{1,9},{9,1},{17,25},{25,17},{2,10},{10... | collective-permute-start | bytes 2359304 | tf_op jit(solution)/shard_map/feed_batch_0/ppermute | solution.py:1096
  77.6 19.7 %collective-permute-start.8 = (bf16[2,2,2,192,256]{4,3,2,1,0:T(8,128)(2,1)}, bf16[2,2,2,192,256]{4,3,2,1,0:T(8,128)(2,1)}, u32[]{:S(2)}, u32[]{:S(2)}) collective-permute-start(bf16[2,2,2,192,256]{4,3,2,1,0:T(8,128)(2,1)} %get-tuple-element.171), channel_id=1, source_target_pairs={{0,16},{8,24},{16,0},{24,8},{1,17},{9,25},{17,1},{25,9},{2,18},{10... | collective-permute-start | bytes 2359304 | tf_op jit(solution)/shard_map/feed_batch_1/ppermute | solution.py:1096
  79.1 19.4 %collective-permute-start.9 = (bf16[2,2,2,192,256]{4,3,2,1,0:T(8,128)(2,1)}, bf16[2,2,2,192,256]{4,3,2,1,0:T(8,128)(2,1)}, u32[]{:S(2)}, u32[]{:S(2)}) collective-permute-start(bf16[2,2,2,192,256]{4,3,2,1,0:T(8,128)(2,1)} %get-tuple-element.172), channel_id=1, source_target_pairs={{0,2},{1,3},{2,0},{3,1},{4,6},{5,7},{6,4},{7,5},{8,10},{9,11},{10,... | collective-permute-start | bytes 2359304 | tf_op jit(solution)/shard_map/feed_seq_1/ppermute | solution.py:1096
  98.6 6.5 %collective-permute-start.16 = (bf16[768,384]{1,0:T(8,128)(2,1)}, bf16[768,384]{1,0:T(8,128)(2,1)}, u32[]{:S(2)}, u32[]{:S(2)}) collective-permute-start(bf16[768,384]{1,0:T(8,128)(2,1)} %get-tuple-element.202), channel_id=1, source_target_pairs={{0,1},{1,0},{2,3},{3,2},{4,5},{5,4},{6,7},{7,6},{8,9},{9,8},{10,11... | collective-permute-start | bytes 1769480 | tf_op jit(solution)/shard_map/grad0_pair/ppermute | solution.py:1096
  98.6 16.6 %collective-permute-start.15 = (bf16[256,768]{1,0:T(8,128)(2,1)}, bf16[256,768]{1,0:T(8,128)(2,1)}, u32[]{:S(2)}, u32[]{:S(2)}) collective-permute-start(bf16[256,768]{1,0:T(8,128)(2,1)} %get-tuple-element.199), channel_id=1, source_target_pairs={{0,2},{1,3},{2,0},{3,1},{4,6},{5,7},{6,4},{7,5},{8,10},{9,11},{10,... | collective-permute-start | bytes 1179656 | tf_op jit(solution)/shard_map/layer_back/ppermute | solution.py:1096
  102.4 12.8 %collective-permute-start.12 = (bf16[2,2,192,256]{3,2,1,0:T(8,128)(2,1)}, bf16[2,2,192,256]{3,2,1,0:T(8,128)(2,1)}, u32[]{:S(2)}, u32[]{:S(2)}) collective-permute-start(bf16[2,2,192,256]{3,2,1,0:T(8,128)(2,1)} %get-tuple-element.196), channel_id=1, source_target_pairs={{0,16},{8,24},{16,0},{24,8},{1,17},{9,25},{17,1},{25,9},{2,18},{10... | collective-permute-start | bytes 1179656 | tf_op jit(solution)/shard_map/feed_batch_1/ppermute | solution.py:1096
  102.9 15.9 %collective-permute-start.13 = (bf16[2,2,192,256]{3,2,1,0:T(8,128)(2,1)}, bf16[2,2,192,256]{3,2,1,0:T(8,128)(2,1)}, u32[]{:S(2)}, u32[]{:S(2)}) collective-permute-start(bf16[2,2,192,256]{3,2,1,0:T(8,128)(2,1)} %get-tuple-element.197), channel_id=1, source_target_pairs={{0,2},{1,3},{2,0},{3,1},{4,6},{5,7},{6,4},{7,5},{8,10},{9,11},{10,... | collective-permute-start | bytes 1179656 | tf_op jit(solution)/shard_map/feed_seq_1/ppermute | solution.py:1096
  104.5 14.4 %collective-permute-start.14 = (bf16[2,2,192,256]{3,2,1,0:T(8,128)(2,1)}, bf16[2,2,192,256]{3,2,1,0:T(8,128)(2,1)}, u32[]{:S(2)}, u32[]{:S(2)}) collective-permute-start(bf16[2,2,192,256]{3,2,1,0:T(8,128)(2,1)} %get-tuple-element.198), channel_id=1, source_target_pairs={{0,8},{8,0},{16,24},{24,16},{1,9},{9,1},{17,25},{25,17},{2,10},{10... | collective-permute-start | bytes 1179656 | tf_op jit(solution)/shard_map/feed_batch_0/ppermute | solution.py:1096
  118.8 6.6 %collective-permute-start.17 = (bf16[384,384]{1,0:T(8,128)(2,1)}, bf16[384,384]{1,0:T(8,128)(2,1)}, u32[]{:S(2)}, u32[]{:S(2)}) collective-permute-start(bf16[384,384]{1,0:T(8,128)(2,1)} %get-tuple-element.216), channel_id=1, source_target_pairs={{0,1},{1,0},{2,3},{3,2},{4,5},{5,4},{6,7},{7,6},{8,9},{9,8},{10,11... | collective-permute-start | bytes 884744 | tf_op jit(solution)/shard_map/grad1_pair/ppermute | solution.py:1096
  118.8 10.1 %collective-permute-start.21 = (bf16[384,384]{1,0:T(8,128)(2,1)}, bf16[384,384]{1,0:T(8,128)(2,1)}, u32[]{:S(2)}, u32[]{:S(2)}) collective-permute-start(bf16[384,384]{1,0:T(8,128)(2,1)} %get-tuple-element.221), channel_id=1, source_target_pairs={{0,8},{8,0},{16,24},{24,16},{1,9},{9,1},{17,25},{25,17},{2,10},{10... | collective-permute-start | bytes 884744 | tf_op jit(solution)/shard_map/plane0_1/ppermute | solution.py:1096
  119.4 25.8 %collective-permute-start.22 = (bf16[384,384]{1,0:T(8,128)(2,1)}, bf16[384,384]{1,0:T(8,128)(2,1)}, u32[]{:S(2)}, u32[]{:S(2)}) collective-permute-start(bf16[384,384]{1,0:T(8,128)(2,1)} %get-tuple-element.222), channel_id=1, source_target_pairs={{0,16},{8,24},{16,0},{24,8},{1,17},{9,25},{17,1},{25,9},{2,18},{10... | collective-permute-start | bytes 884744 | tf_op jit(solution)/shard_map/plane0_2/ppermute | solution.py:1096
  119.9 25.3 %collective-permute-start.23 = (bf16[384,384]{1,0:T(8,128)(2,1)}, bf16[384,384]{1,0:T(8,128)(2,1)}, u32[]{:S(2)}, u32[]{:S(2)}) collective-permute-start(bf16[384,384]{1,0:T(8,128)(2,1)} %get-tuple-element.223), channel_id=1, source_target_pairs={{0,24},{8,16},{16,8},{24,0},{1,25},{9,17},{17,9},{25,1},{2,26},{10... | collective-permute-start | bytes 884744 | tf_op jit(solution)/shard_map/plane0_3/ppermute | solution.py:1096
  125.4 19.8 %collective-permute-start.18 = (bf16[2,192,256]{2,1,0:T(8,128)(2,1)}, bf16[2,192,256]{2,1,0:T(8,128)(2,1)}, u32[]{:S(2)}, u32[]{:S(2)}) collective-permute-start(bf16[2,192,256]{2,1,0:T(8,128)(2,1)} %get-tuple-element.218), channel_id=1, source_target_pairs={{0,2},{1,3},{2,0},{3,1},{4,6},{5,7},{6,4},{7,5},{8,10},{9,11},{10,... | collective-permute-start | bytes 589832 | tf_op jit(solution)/shard_map/feed_seq_1/ppermute | solution.py:1096
  126.0 19.2 %collective-permute-start.19 = (bf16[2,192,256]{2,1,0:T(8,128)(2,1)}, bf16[2,192,256]{2,1,0:T(8,128)(2,1)}, u32[]{:S(2)}, u32[]{:S(2)}) collective-permute-start(bf16[2,192,256]{2,1,0:T(8,128)(2,1)} %get-tuple-element.219), channel_id=1, source_target_pairs={{0,4},{1,5},{2,6},{3,7},{4,0},{5,1},{6,2},{7,3},{8,12},{9,13},{10,... | collective-permute-start | bytes 589832 | tf_op jit(solution)/shard_map/feed_seq_2/ppermute | solution.py:1096
  129.0 17.1 %collective-permute-start.20 = (bf16[2,192,256]{2,1,0:T(8,128)(2,1)}, bf16[2,192,256]{2,1,0:T(8,128)(2,1)}, u32[]{:S(2)}, u32[]{:S(2)}) collective-permute-start(bf16[2,192,256]{2,1,0:T(8,128)(2,1)} %get-tuple-element.220), channel_id=1, source_target_pairs={{0,4},{1,5},{2,6},{3,7},{4,0},{5,1},{6,2},{7,3},{8,12},{9,13},{10,... | collective-permute-start | bytes 589832 | tf_op jit(solution)/shard_map/feed_seq_2/ppermute | solution.py:1096
  146.1 3.5 %collective-permute-start.24 = (bf16[1424,384]{1,0:T(8,128)(2,1)}, bf16[1424,384]{1,0:T(8,128)(2,1)}, u32[]{:S(2)}, u32[]{:S(2)}) collective-permute-start(bf16[1424,384]{1,0:T(8,128)(2,1)} %get-tuple-element.242), channel_id=1, source_target_pairs={{0,1},{1,0},{2,3},{3,2},{4,5},{5,4},{6,7},{7,6},{8,9},{9,8},{10,11... | collective-permute-start | bytes 3280904 | tf_op jit(solution)/shard_map/dn1_pair/ppermute | solution.py:1096
  146.1 13.9 %collective-permute-start.29 = (bf16[192,384]{1,0:T(8,128)(2,1)}, bf16[192,384]{1,0:T(8,128)(2,1)}, u32[]{:S(2)}, u32[]{:S(2)}) collective-permute-start(bf16[192,384]{1,0:T(8,128)(2,1)} %get-tuple-element.259), channel_id=1, source_target_pairs={{0,8},{8,0},{16,24},{24,16},{1,9},{9,1},{17,25},{25,17},{2,10},{10... | collective-permute-start | bytes 442376 | tf_op jit(solution)/shard_map/plane1_1/ppermute | solution.py:1096
  146.5 14.0 %collective-permute-start.30 = (bf16[192,384]{1,0:T(8,128)(2,1)}, bf16[192,384]{1,0:T(8,128)(2,1)}, u32[]{:S(2)}, u32[]{:S(2)}) collective-permute-start(bf16[192,384]{1,0:T(8,128)(2,1)} %get-tuple-element.260), channel_id=1, source_target_pairs={{0,16},{8,24},{16,0},{24,8},{1,17},{9,25},{17,1},{25,9},{2,18},{10... | collective-permute-start | bytes 442376 | tf_op jit(solution)/shard_map/plane1_2/ppermute | solution.py:1096
  147.1 14.7 %collective-permute-start.31 = (bf16[192,384]{1,0:T(8,128)(2,1)}, bf16[192,384]{1,0:T(8,128)(2,1)}, u32[]{:S(2)}, u32[]{:S(2)}) collective-permute-start(bf16[192,384]{1,0:T(8,128)(2,1)} %get-tuple-element.261), channel_id=1, source_target_pairs={{0,24},{8,16},{16,8},{24,0},{1,25},{9,17},{17,9},{25,1},{2,26},{10... | collective-permute-start | bytes 442376 | tf_op jit(solution)/shard_map/plane1_3/ppermute | solution.py:1096
  153.6 36.7 %collective-permute-start.40 = (bf16[256,768]{1,0:T(8,128)(2,1)}, bf16[256,768]{1,0:T(8,128)(2,1)}, u32[]{:S(2)}, u32[]{:S(2)}) collective-permute-start(bf16[256,768]{1,0:T(8,128)(2,1)} %get-tuple-element.290), channel_id=1, source_target_pairs={{0,2},{1,3},{2,0},{3,1},{4,6},{5,7},{6,4},{7,5},{8,10},{9,11},{10,... | collective-permute-start | bytes 1179656 | tf_op jit(solution)/shard_map/grad_back/ppermute | solution.py:1096
  159.4 10.8 %collective-permute-start.32 = (bf16[208,384]{1,0:T(8,128)(2,1)}, bf16[208,384]{1,0:T(8,128)(2,1)}, u32[]{:S(2)}, u32[]{:S(2)}) collective-permute-start(bf16[208,384]{1,0:T(8,128)(2,1)} %get-tuple-element.263), channel_id=1, source_target_pairs={{0,8},{8,0},{16,24},{24,16},{1,9},{9,1},{17,25},{25,17},{2,10},{10... | collective-permute-start | bytes 479240 | tf_op jit(solution)/shard_map/plane2_1/ppermute | solution.py:1096
  160.0 10.8 %collective-permute-start.33 = (bf16[208,384]{1,0:T(8,128)(2,1)}, bf16[208,384]{1,0:T(8,128)(2,1)}, u32[]{:S(2)}, u32[]{:S(2)}) collective-permute-start(bf16[208,384]{1,0:T(8,128)(2,1)} %get-tuple-element.264), channel_id=1, source_target_pairs={{0,16},{8,24},{16,0},{24,8},{1,17},{9,25},{17,1},{25,9},{2,18},{10... | collective-permute-start | bytes 479240 | tf_op jit(solution)/shard_map/plane2_2/ppermute | solution.py:1096
  160.5 7.3 %collective-permute-start.28 = (bf16[192,384]{1,0:T(8,128)(2,1)}, bf16[192,384]{1,0:T(8,128)(2,1)}, u32[]{:S(2)}, u32[]{:S(2)}) collective-permute-start(bf16[192,384]{1,0:T(8,128)(2,1)} %get-tuple-element.257), channel_id=1, source_target_pairs={{0,2},{1,3},{2,0},{3,1},{4,6},{5,7},{6,4},{7,5},{8,10},{9,11},{10,... | collective-permute-start | bytes 442376 | tf_op jit(solution)/shard_map/line0/ppermute | solution.py:1096
  161.8 10.6 %collective-permute-start.34 = (bf16[208,384]{1,0:T(8,128)(2,1)}, bf16[208,384]{1,0:T(8,128)(2,1)}, u32[]{:S(2)}, u32[]{:S(2)}) collective-permute-start(bf16[208,384]{1,0:T(8,128)(2,1)} %get-tuple-element.265), channel_id=1, source_target_pairs={{0,24},{8,16},{16,8},{24,0},{1,25},{9,17},{17,9},{25,1},{2,26},{10... | collective-permute-start | bytes 479240 | tf_op jit(solution)/shard_map/plane2_3/ppermute | solution.py:1096
  167.8 7.5 %collective-permute-start.25 = (bf16[192,256]{1,0:T(8,128)(2,1)}, bf16[192,256]{1,0:T(8,128)(2,1)}, u32[]{:S(2)}, u32[]{:S(2)}) collective-permute-start(bf16[192,256]{1,0:T(8,128)(2,1)} %get-tuple-element.251), channel_id=1, source_target_pairs={{0,4},{1,5},{2,6},{3,7},{4,0},{5,1},{6,2},{7,3},{8,12},{9,13},{10,... | collective-permute-start | bytes 294920 | tf_op jit(solution)/shard_map/feed_seq_2/ppermute | solution.py:1096
  170.2 5.1 %collective-permute-start.26 = (bf16[192,256]{1,0:T(8,128)(2,1)}, bf16[192,256]{1,0:T(8,128)(2,1)}, u32[]{:S(2)}, u32[]{:S(2)}) collective-permute-start(bf16[192,256]{1,0:T(8,128)(2,1)} %get-tuple-element.252), channel_id=1, source_target_pairs={{0,8},{8,0},{16,24},{24,16},{1,9},{9,1},{17,25},{25,17},{2,10},{10... | collective-permute-start | bytes 294920 | tf_op jit(solution)/shard_map/feed_batch_0/ppermute | solution.py:1096
  170.8 4.9 %collective-permute-start.27 = (bf16[192,256]{1,0:T(8,128)(2,1)}, bf16[192,256]{1,0:T(8,128)(2,1)}, u32[]{:S(2)}, u32[]{:S(2)}) collective-permute-start(bf16[192,256]{1,0:T(8,128)(2,1)} %get-tuple-element.253), channel_id=1, source_target_pairs={{0,16},{8,24},{16,0},{24,8},{1,17},{9,25},{17,1},{25,9},{2,18},{10... | collective-permute-start | bytes 294920 | tf_op jit(solution)/shard_map/feed_batch_1/ppermute | solution.py:1096
  175.3 7.3 %collective-permute-start.35 = (bf16[96,384]{1,0:T(8,128)(2,1)}, bf16[96,384]{1,0:T(8,128)(2,1)}, u32[]{:S(2)}, u32[]{:S(2)}) collective-permute-start(bf16[96,384]{1,0:T(8,128)(2,1)} %get-tuple-element.278), channel_id=1, source_target_pairs={{0,4},{1,5},{2,6},{3,7},{4,0},{5,1},{6,2},{7,3},{8,12},{9,13},{10,... | collective-permute-start | bytes 221192 | tf_op jit(solution)/shard_map/line0_last/ppermute | solution.py:1096
  178.4 11.9 %collective-permute-start.39 = (bf16[2,96,256]{2,1,0:T(8,128)(2,1)}, bf16[2,96,256]{2,1,0:T(8,128)(2,1)}, u32[]{:S(2)}, u32[]{:S(2)}) collective-permute-start(bf16[2,96,256]{2,1,0:T(8,128)(2,1)} %get-tuple-element.288), channel_id=1, source_target_pairs={{0,1},{1,0},{2,3},{3,2},{4,5},{5,4},{6,7},{7,6},{8,9},{9,8},{10,11... | collective-permute-start | bytes 294920 | tf_op jit(solution)/shard_map/feed_pair/ppermute | solution.py:1096
  178.4 5.3 %collective-permute-start.36 = (bf16[112,384]{1,0:T(8,128)(2,1)}, bf16[112,384]{1,0:T(8,128)(2,1)}, u32[]{:S(2)}, u32[]{:S(2)}) collective-permute-start(bf16[112,384]{1,0:T(8,128)(2,1)} %get-tuple-element.280), channel_id=1, source_target_pairs={{0,2},{1,3},{2,0},{3,1},{4,6},{5,7},{6,4},{7,5},{8,10},{9,11},{10,... | collective-permute-start | bytes 258056 | tf_op jit(solution)/shard_map/line12_1/ppermute | solution.py:1096
  180.1 10.3 %collective-permute-start.37 = (bf16[112,384]{1,0:T(8,128)(2,1)}, bf16[112,384]{1,0:T(8,128)(2,1)}, u32[]{:S(2)}, u32[]{:S(2)}) collective-permute-start(bf16[112,384]{1,0:T(8,128)(2,1)} %get-tuple-element.281), channel_id=1, source_target_pairs={{0,4},{1,5},{2,6},{3,7},{4,0},{5,1},{6,2},{7,3},{8,12},{9,13},{10,... | collective-permute-start | bytes 258056 | tf_op jit(solution)/shard_map/line12_2/ppermute | solution.py:1096
  182.6 7.7 %collective-permute-start.38 = (bf16[112,384]{1,0:T(8,128)(2,1)}, bf16[112,384]{1,0:T(8,128)(2,1)}, u32[]{:S(2)}, u32[]{:S(2)}) collective-permute-start(bf16[112,384]{1,0:T(8,128)(2,1)} %get-tuple-element.282), channel_id=1, source_target_pairs={{0,6},{1,7},{2,4},{3,5},{4,2},{5,3},{6,0},{7,1},{8,14},{9,15},{10,... | collective-permute-start | bytes 258056 | tf_op jit(solution)/shard_map/line12_3/ppermute | solution.py:1096
